TPU v7x, 32 devices: a whole 2x2x4 slice. The times are simulated.
32 devices in a mesh: grid: 16 (over z, y, core), batch: 2 (over x).
Axes of the slice: x: 2, y: 2, z: 4, core: 2. Of those that a mesh axis runs over, the one named last changes fastest.
Arguments:
- inputs: bfloat16 [2, 256, 16384], P('batch', None, 'grid'), may hold values from -6 to 6
- cotangent: bfloat16 [2, 256, 16384], P('batch', None, 'grid'), may hold values from -8 to 8
- weights: bfloat16 [128, 8, 9216], P('grid', 'batch'), may hold values from -0.375 to 0.375
- gate_logits: float32 [2, 64, 2], replicated, may hold values from -5 to 5
- routes: int32 [2, 64, 2], replicated, may hold values from 0 to 127, as said below
Outputs:
- d_inputs: bfloat16 [2, 256, 16384], P('batch', None, 'grid')
- d_weights: float32 [128, 8, 9216], P('grid', 'batch')
- gate_grad: float32 [2, 64, 2], P(None, 'grid')
Inputs may be any that keep to these rules, and one draw needn't show every extreme that they name: Expert e is owned by grid index e // 8. The 16 routes of the patches g * 4 to (g + 1) * 4 - 1 of all samples name experts of one owner at most 1 times, for every grid index g; in every draw some owner is named exactly 1 times by the routes of every grid index. The 2 routes of a patch name different experts.
All inputs are finite; a program needn't handle non-finite values.
Results may differ from a plain program's by a relative error of at most 0.0051.
Values may be sent and summed in bfloat16 or wider, within the bound.
No kernel may reach another device: no remote copies, remote signals or barrier semaphores. Data moves between devices by JAX's collectives and lax.ppermute only.
A program may use at most 256 MiB of HBM per device.

v0:
```python
import functools

import jax
import jax.numpy as jnp
from jax import lax
from jax.experimental import pallas as pl
from jax.experimental.pallas import tpu as pltpu
from jax.sharding import PartitionSpec as P

CG = 32
SIDE = 16
PIX = SIDE * SIDE
TAPS = 9
ROW = CG * TAPS
WIDE = 384
QUAD = 4 * ROW
ROWS = 8
DOT_ROWS = 16
VMEM_LIMIT = 48 * 1024 * 1024


def rolled(values, shift):
    extent = values.shape[1]
    shift %= extent
    return values if shift == 0 else pltpu.roll(values, shift, 1)


def pixel_masks(rows):
    pixel = lax.broadcasted_iota(jnp.int32, (rows, PIX), 1)
    column = pixel % SIDE
    return {
        "row": {-1: pixel >= SIDE, 1: pixel < PIX - SIDE},
        "column": {-1: column > 0, 1: column < SIDE - 1},
    }


def moved(values, row_shift, column_shift, masks):
    out = rolled(values, -(row_shift * SIDE + column_shift))
    if row_shift:
        out = jnp.where(masks["row"][row_shift], out, 0.0)
    if column_shift:
        out = jnp.where(masks["column"][column_shift], out, 0.0)
    return out


def joined(ref, start, count):
    return jnp.concatenate([ref[m, start:start + count, :] for m in range(ref.shape[0])], axis=1)


def strided(ref, start, count, stride):
    return jnp.concatenate(
        [ref[m, pl.ds(start, count, stride=stride), :] for m in range(ref.shape[0])], axis=1
    )


def put(ref, start, values):
    for at in range(0, values.shape[1], 128):
        piece = values[:, at:at + 128]
        ref[at // 128, start:start + values.shape[0], :piece.shape[1]] = piece


def pick_kernel(
    routes_ref, logits_ref, weights_ref, x_ref, dy_ref, wire_ref, send_ref, local_ref, logit_ref,
    wire_sem, send_sem,
):
    samples, top_count, patches = routes_ref.shape
    owned = weights_ref.shape[0]
    tiles = wire_ref.shape[0]
    others, _, channels, _ = send_ref.shape
    per_tile = patches // tiles
    first = lax.axis_index("grid") * owned
    mine = lax.axis_index("batch")

    def wire_copy(tile, local):
        return pltpu.make_async_copy(weights_ref.at[local], wire_ref.at[tile], wire_sem.at[tile])

    def send_copies(step):
        block = lax.rem(mine + step, others + 1)
        rows = pl.ds(pl.multiple_of(block * channels, channels), channels)
        return [
            pltpu.make_async_copy(
                source.at[0, rows], send_ref.at[step - 1, which], send_sem.at[step - 1, which]
            )
            for which, source in enumerate((x_ref, dy_ref))
        ]

    def pick(tile, carry):
        local = jnp.int32(0)
        logit = jnp.float32(0)
        for sample in range(samples):
            for place in range(per_tile):
                for rank in range(top_count):
                    patch = tile * per_tile + place
                    inside = routes_ref[sample, rank, patch] - first
                    hit = (inside >= 0) & (inside < owned)
                    local = jnp.where(hit, inside, local)
                    logit = jnp.where(hit, logits_ref[sample, rank, patch], logit)
        wire_copy(tile, local).start()
        local_ref[tile] = local
        logit_ref[tile] = logit
        return carry

    lax.fori_loop(0, tiles, pick, 0)
    for step in range(1, others + 1):
        for copy in send_copies(step):
            copy.start()

    def finish(tile, carry):
        wire_copy(tile, 0).wait()
        return carry

    lax.fori_loop(0, tiles, finish, 0)
    for step in range(1, others + 1):
        for copy in send_copies(step):
            copy.wait()


def grads_kernel(
    owned, routes_ref, x_ref, dy_ref, got_ref, wire_ref, dy_all_ref, x_all_ref, taps_ref, grad_ref
):
    samples, top_count, patches = routes_ref.shape
    tiles, groups, _ = wire_ref.shape
    others, _, channels, _ = got_ref.shape
    per_tile = patches // tiles
    together = ROWS // groups
    tile = lax.axis_index("grid")
    mine = lax.axis_index("batch")
    own_rows = pl.ds(pl.multiple_of(mine * channels, channels), channels)
    for place in range(per_tile):
        span = slice(place * PIX, (place + 1) * PIX)
        x_all_ref[mine * per_tile + place] = x_ref[0, own_rows, span]
        dy_all_ref[mine * per_tile + place] = dy_ref[0, own_rows, span]
        for step in range(1, others + 1):
            sample = lax.rem(mine - step + others + 1, others + 1)
            x_all_ref[sample * per_tile + place] = got_ref[step - 1, 0, :, span]
            dy_all_ref[sample * per_tile + place] = got_ref[step - 1, 1, :, span]
    grad_ref[WIDE // 128 - 1] = jnp.zeros((ROWS * CG, 128), jnp.float32)
    masks = pixel_masks(CG)

    def work(block, carry):
        for unit in range(ROWS):
            patch = block * together + unit // groups
            rows = slice((unit % groups) * CG, (unit % groups + 1) * CG)
            x_unit = x_all_ref[patch, rows, :].astype(jnp.float32)
            for tap in range(TAPS):
                part = moved(x_unit, tap // 3 - 1, tap % 3 - 1, masks)
                for half in range(PIX // 128):
                    taps_ref[half, pl.ds(unit * ROW + tap, CG, stride=TAPS), :] = part[
                        :, half * 128:(half + 1) * 128
                    ]
            grad = lax.dot_general(
                dy_all_ref[patch, rows, :],
                joined(taps_ref, unit * ROW, ROW).astype(jnp.bfloat16),
                (((1,), (1,)), ((), ())),
                preferred_element_type=jnp.float32,
            )
            put(grad_ref, unit * CG, grad)
        slots = []
        for place in range(together):
            patch = block * together + place
            column = tile * per_tile + lax.rem(patch, per_tile)
            slots.append(
                [
                    lax.div(routes_ref[lax.div(patch, per_tile), rank, column], owned)
                    for rank in range(top_count)
                ]
            )
        for quad in range(CG // 4):
            parts = [None] * TAPS
            for j in range(4):
                line = rolled(strided(grad_ref, quad * 4 + j, ROWS, CG), 32 * j)
                for m in range(3):
                    piece = line[:, m * 128:(m + 1) * 128]
                    at = 2 * j + m
                    parts[at] = piece if parts[at] is None else parts[at] + piece
            flat = jnp.concatenate(parts, axis=1)
            for place in range(together):
                value = flat[place * groups:(place + 1) * groups].astype(jnp.bfloat16)
                for slot in slots[place]:
                    wire_ref[slot, :, quad * QUAD:(quad + 1) * QUAD] = value
        return carry

    lax.fori_loop(0, samples * per_tile // together, work, 0)


def adjoint_kernel(
    owned, routes_ref, logits_ref, kernels_ref, grads_ref, dy_all_ref, out_ref,
    flat_ref, mixed_ref, spread_ref, dots_ref,
):
    samples, top_count, patches = routes_ref.shape
    tiles, groups, _ = kernels_ref.shape
    channels = groups * CG
    per_tile = patches // tiles
    together = ROWS // groups
    blocks = samples * per_tile // together
    tile = lax.axis_index("grid")
    mine = lax.axis_index("batch")
    masks = pixel_masks(CG)

    def work(block, carry):
        for place in range(together):
            patch = block * together + place
            sample = lax.div(patch, per_tile)
            column = tile * per_tile + lax.rem(patch, per_tile)
            gates, slots = [], []
            for rank in range(top_count):
                logit = logits_ref[sample, rank, column]
                gates.append(jax.nn.sigmoid(jnp.full((groups, 128), logit, jnp.float32)))
                slots.append(lax.div(routes_ref[sample, rank, column], owned))
            dots = [jnp.zeros((groups, 128), jnp.float32) for _ in range(top_count)]
            for at in range(0, CG * ROW, 128):
                lanes = slice(at, at + 128)
                mixed = jnp.zeros((groups, 128), jnp.float32)
                for rank in range(top_count):
                    kernel = kernels_ref[slots[rank], :, lanes].astype(jnp.float32)
                    grad = grads_ref[slots[rank], :, lanes].astype(jnp.float32)
                    dots[rank] += kernel * grad
                    mixed += gates[rank] * kernel
                flat_ref[place * groups:(place + 1) * groups, lanes] = mixed
            for rank in range(top_count):
                start = (block * top_count + rank) * ROWS + place * groups
                dots_ref[pl.ds(start, groups), :] = dots[rank]
        for quad in range(CG // 4):
            for j in range(4):
                start = quad * QUAD + 2 * j * 128
                line = rolled(flat_ref[:, start:start + WIDE], -32 * j)
                for m in range(WIDE // 128):
                    mixed_ref[m, pl.ds(quad * 4 + j, ROWS, stride=CG), :] = line[
                        :, m * 128:(m + 1) * 128
                    ]
        for unit in range(ROWS):
            patch = block * together + unit // groups
            rows = slice((unit % groups) * CG, (unit % groups + 1) * CG)
            kernel = joined(mixed_ref, unit * CG, CG)[:, :ROW].astype(jnp.bfloat16)
            spread = lax.dot_general(
                kernel,
                dy_all_ref[patch, rows, :],
                (((0,), (0,)), ((), ())),
                preferred_element_type=jnp.float32,
            )
            put(spread_ref, unit * ROW, spread)
            total = jnp.zeros((CG, PIX), jnp.float32)
            for tap in range(TAPS):
                part = strided(spread_ref, unit * ROW + tap, CG, TAPS)
                total += moved(part, 1 - tap // 3, 1 - tap % 3, masks)
            step = lax.rem(lax.div(patch, per_tile) - mine + samples, samples)
            offset = pl.multiple_of(lax.rem(patch, per_tile) * PIX, PIX)
            out_ref[step, rows, pl.ds(offset, PIX)] = total.astype(jnp.bfloat16)
        return carry

    lax.fori_loop(0, blocks, work, 0)
    count = blocks * top_count * ROWS
    sums = lax.dot_general(
        jnp.ones((DOT_ROWS, 128), jnp.float32),
        dots_ref[...],
        (((1,), (1,)), ((), ())),
        precision=lax.Precision.HIGHEST,
        preferred_element_type=jnp.float32,
    )
    row = lax.broadcasted_iota(jnp.int32, (count, 128), 0)
    lane = lax.broadcasted_iota(jnp.int32, (count, 128), 1)
    row_patch = row // (top_count * ROWS) * together + row % ROWS // groups
    row_rank = row // ROWS % top_count
    chosen = (lane == row_patch * top_count + row_rank).astype(jnp.float32)
    route_dots = lax.dot_general(
        sums,
        chosen,
        (((1,), (0,)), ((), ())),
        precision=lax.Precision.HIGHEST,
        preferred_element_type=jnp.float32,
    ).astype(jnp.bfloat16)
    for step in range(samples):
        out_ref[step, channels:channels + DOT_ROWS, :128] = route_dots


def sum_kernel(local_ref, logit_ref, got_ref, out_ref):
    tiles, groups, width = got_ref.shape
    out_ref[...] = jnp.zeros(out_ref.shape, jnp.float32)

    def add(tile, carry):
        local = local_ref[tile]
        gate = jax.nn.sigmoid(jnp.full((groups, 128), logit_ref[tile], jnp.float32)) / SIDE
        for at in range(0, width, 128):
            lanes = slice(at, at + 128)
            out_ref[local, :, lanes] += gate * got_ref[tile, :, lanes].astype(jnp.float32)
        return carry

    lax.fori_loop(0, tiles, add, 0)


def per_device(inputs, cotangent, weights, gate_logits, routes):
    tiles = lax.axis_size("grid")
    batch = lax.axis_size("batch")
    owned, groups, width = weights.shape
    samples, patches, top_count = routes.shape
    per_tile = patches // tiles
    span = inputs.shape[2]
    channels = groups * CG
    assert samples * per_tile * top_count == tiles and samples == batch
    smem = pl.BlockSpec(memory_space=pltpu.SMEM)
    vmem = pl.BlockSpec(memory_space=pltpu.VMEM)
    hbm = pl.BlockSpec(memory_space=pl.ANY)
    params = pltpu.CompilerParams(vmem_limit_bytes=VMEM_LIMIT)
    routes_t = routes.transpose(0, 2, 1)
    logits_t = gate_logits.transpose(0, 2, 1)
    wire_shape = jax.ShapeDtypeStruct((tiles, groups, width), jnp.bfloat16)

    picked, to_send, local, logit = pl.pallas_call(
        pick_kernel,
        out_shape=(
            wire_shape,
            jax.ShapeDtypeStruct((batch - 1, 2, channels, span), jnp.bfloat16),
            jax.ShapeDtypeStruct((tiles,), jnp.int32),
            jax.ShapeDtypeStruct((tiles,), jnp.float32),
        ),
        in_specs=[smem, smem, hbm, hbm, hbm],
        out_specs=(hbm, hbm, smem, smem),
        scratch_shapes=[
            pltpu.SemaphoreType.DMA((tiles,)),
            pltpu.SemaphoreType.DMA((batch - 1, 2)),
        ],
        compiler_params=params,
        name="pick",
    )(routes_t, logits_t, weights, inputs, cotangent)

    def exchange(blocks):
        return [
            lax.ppermute(
                blocks[step - 1], "batch", [(i, (i + step) % batch) for i in range(batch)]
            )
            for step in range(1, batch)
        ]

    kernels = lax.all_to_all(picked, "grid", split_axis=0, concat_axis=0, tiled=True)
    got = jnp.stack(exchange([to_send[step] for step in range(batch - 1)]))

    work = samples * patches // tiles * groups * width * PIX * 2
    grads, dy_all = pl.pallas_call(
        functools.partial(grads_kernel, owned),
        out_shape=(
            wire_shape,
            jax.ShapeDtypeStruct((samples * per_tile, channels, PIX), jnp.bfloat16),
        ),
        in_specs=[smem, vmem, vmem, vmem],
        out_specs=(vmem, vmem),
        scratch_shapes=[
            pltpu.VMEM((samples * per_tile, channels, PIX), jnp.bfloat16),
            pltpu.VMEM((PIX // 128, ROWS * ROW, 128), jnp.float32),
            pltpu.VMEM((WIDE // 128, ROWS * CG, 128), jnp.float32),
        ],
        compiler_params=params,
        cost_estimate=pl.CostEstimate(
            flops=work * 10, bytes_accessed=4 * 1024 * 1024, transcendentals=0
        ),
        name="kernel_grads",
    )(routes_t, inputs, cotangent, got)

    grads_back = lax.all_to_all(grads, "grid", split_axis=0, concat_axis=0, tiled=True)

    parts = pl.pallas_call(
        functools.partial(adjoint_kernel, owned),
        out_shape=jax.ShapeDtypeStruct((batch, channels + DOT_ROWS, span), jnp.bfloat16),
        in_specs=[smem, smem, vmem, vmem, vmem],
        out_specs=vmem,
        scratch_shapes=[
            pltpu.VMEM((ROWS, width), jnp.float32),
            pltpu.VMEM((WIDE // 128, ROWS * CG, 128), jnp.float32),
            pltpu.VMEM((PIX // 128, ROWS * ROW, 128), jnp.float32),
            pltpu.VMEM((samples * per_tile * top_count * groups, 128), jnp.float32),
        ],
        compiler_params=params,
        cost_estimate=pl.CostEstimate(
            flops=work * 10, bytes_accessed=4 * 1024 * 1024, transcendentals=0
        ),
        name="adjoint",
    )(routes_t, logits_t, kernels, grads, dy_all)

    arrived = exchange([parts[step] for step in range(1, batch)])
    mine = lax.axis_index("batch")
    d_inputs = jnp.zeros(inputs.shape, jnp.bfloat16)
    dots = jnp.zeros((128,), jnp.float32)
    for step, part in enumerate([parts[0]] + arrived):
        block = lax.rem(mine - step + batch, batch)
        d_inputs = lax.dynamic_update_slice(
            d_inputs, part[None, :channels], (0, block * channels, 0)
        )
        dots += part[channels, :128].astype(jnp.float32)
    dots = dots[:tiles].reshape(samples, per_tile, top_count)
    gates = jax.nn.sigmoid(
        lax.dynamic_slice_in_dim(gate_logits, lax.axis_index("grid") * per_tile, per_tile, 1)
    )
    gate_grad = gates * (1.0 - gates) * dots / SIDE

    d_weights = pl.pallas_call(
        sum_kernel,
        out_shape=jax.ShapeDtypeStruct(weights.shape, jnp.float32),
        in_specs=[smem, smem, vmem],
        out_specs=vmem,
        compiler_params=params,
        name="weight_sum",
    )(local, logit, grads_back)
    return (d_inputs, d_weights, gate_grad)


def solution(mesh):
    placed = (
        P("batch", None, "grid"),
        P("batch", None, "grid"),
        P("grid", "batch", None),
        P(),
        P(),
    )
    return jax.shard_map(
        per_device,
        mesh=mesh,
        in_specs=placed,
        out_specs=(P("batch", None, "grid"), P("grid", "batch", None), P(None, "grid", None)),
        check_vma=False,
    )
```

profile of v0, /device:TPU:13, one launch (start us, length us, event | category | flops | bytes accessed | tf_op | source)
XLA Modules:
  0.0 77.6 jit_solution(5531889715196476539)
XLA Ops:
  0.6 0.0 copy-start
  0.6 1.1 %copy-done = bf16[8,4,9216]{2,1,0:T(4,128)(2,1)S(1)} copy-done((bf16[8,4,9216]{2,1,0:T(4,128)(2,1)S(1)}, bf16[8,4,9216]{2,1,0:T(4,128)(2,1)}, u32[]{:S(2)}) %copy-start) | copy-done | bytes 589848
  1.7 0.0 copy-start.1
  1.7 1.0 %copy-done.1 = bf16[1,256,1024]{2,1,0:T(8,128)(2,1)S(1)} copy-done((bf16[1,256,1024]{2,1,0:T(8,128)(2,1)S(1)}, bf16[1,256,1024]{2,1,0:T(8,128)(2,1)}, u32[]{:S(2)}) %copy-start.1) | copy-done | bytes 524312
  2.7 0.0 copy-start.3
  2.7 1.0 %copy-done.3 = bf16[1,256,1024]{2,1,0:T(8,128)(2,1)S(1)} copy-done((bf16[1,256,1024]{2,1,0:T(8,128)(2,1)S(1)}, bf16[1,256,1024]{2,1,0:T(8,128)(2,1)}, u32[]{:S(2)}) %copy-start.3) | copy-done | bytes 524312
  3.8 0.0 copy-start.5
  3.8 0.7 copy-done.5
  4.5 0.0 copy-start.7
  4.5 0.7 copy-done.7
  5.1 2.8 %pick.1 = (bf16[16,4,9216]{2,1,0:T(4,128)(2,1)}, bf16[1,2,128,1024]{3,2,1,0:T(8,128)(2,1)S(1)}, s32[16]{0:T(128)S(1)}, f32[16]{0:T(128)S(1)}) custom-call(s32[2,2,64]{2,1,0:T(2,128)S(1)} %bitcast.14, f32[2,2,64]{2,1,0:T(2,128)S(1)} %bitcast.12, bf16[8,4,9216]{2,1,0:T(4,128)(2,1)S(1)} %copy-done, bf16[1,256,1024]{2,1,0:T(8,128)(2,1)S(1)} %copy-done.1, ...), custom_call_target="tpu_custom_call" | custom-call | tf_op jit(solution)/shard_map/pick/pallas_call | solution.py:308
  8.0 0.0 copy-start.2
  8.0 0.0 copy-start.4
  8.0 0.0 copy-start.8
  8.0 6.7 %all-to-all-start = ((bf16[16,4,9216]{2,1,0:T(4,128)(2,1)}), bf16[16,4,9216]{2,1,0:T(4,128)(2,1)S(1)}, u32[]{:S(2)}, u32[]{:S(2)}) async-start(bf16[16,4,9216]{2,1,0:T(4,128)(2,1)} %get-tuple-element.9), calls=%async_computation | async-start | bytes 2359296 | tf_op jit(solution)/shard_map/all_to_all | solution.py:334
  14.7 1.2 %collective-permute-start = (bf16[2,128,1024]{2,1,0:T(8,128)(2,1)S(1)}, bf16[2,128,1024]{2,1,0:T(8,128)(2,1)S(1)}, u32[]{:S(2)}, u32[]{:S(2)}) collective-permute-start(bf16[2,128,1024]{2,1,0:T(8,128)(2,1)S(1)} %bitcast.17), channel_id=1, source_target_pairs={{0,1},{1,0},{2,3},{3,2},{4,5},{5,4},{6,7},{7,6},{8,9},{9,8},{10,11... | collective-permute-start | bytes 1572872 | tf_op jit(solution)/shard_map/ppermute | solution.py:328
  15.9 11.9 %collective-permute-done = bf16[2,128,1024]{2,1,0:T(8,128)(2,1)S(1)} collective-permute-done((bf16[2,128,1024]{2,1,0:T(8,128)(2,1)S(1)}, bf16[2,128,1024]{2,1,0:T(8,128)(2,1)S(1)}, u32[]{:S(2)}, u32[]{:S(2)}) %collective-permute-start) | collective-permute-done | bytes 524320 | tf_op jit(solution)/shard_map/ppermute | solution.py:328
  27.9 0.0 copy-done.2
  27.9 0.0 copy-done.4
  27.9 0.0 copy-done.8
  27.9 4.8 %kernel_grads.1 = (bf16[16,4,9216]{2,1,0:T(4,128)(2,1)}, bf16[8,128,256]{2,1,0:T(8,128)(2,1)S(1)}) custom-call(s32[2,2,64]{2,1,0:T(2,128)S(1)} %bitcast.15, bf16[1,256,1024]{2,1,0:T(8,128)(2,1)S(1)} %copy-done.2, bf16[1,256,1024]{2,1,0:T(8,128)(2,1)S(1)} %copy-done.4, bf16[1,2,128,1024]{3,2,1,0:T(8,128)(2,1)S(1)} %bitcast.18), custom_call_target="tpu_custom_call" | custom-call | flops 1509949440 | bytes 4194304 | tf_op jit(solution)/shard_map/kernel_grads/pallas_call | solution.py:338
  32.7 9.8 %all-to-all-done.kernels_ref = bf16[16,4,9216]{2,1,0:T(4,128)(2,1)S(1)} async-done(((bf16[16,4,9216]{2,1,0:T(4,128)(2,1)}), bf16[16,4,9216]{2,1,0:T(4,128)(2,1)S(1)}, u32[]{:S(2)}, u32[]{:S(2)}) %all-to-all-start) | async-done | bytes 1179680 | tf_op jit(solution)/shard_map/all_to_all | solution.py:334
  42.5 0.0 copy-start.6
  42.5 5.0 %all-to-all-start.1 = ((bf16[16,4,9216]{2,1,0:T(4,128)(2,1)}), bf16[16,4,9216]{2,1,0:T(4,128)(2,1)S(1)}, u32[]{:S(2)}, u32[]{:S(2)}) async-start(bf16[16,4,9216]{2,1,0:T(4,128)(2,1)} %get-tuple-element.11.grads_ref), calls=%async_computation.1 | async-start | bytes 2359296 | tf_op jit(solution)/shard_map/all_to_all | solution.py:358
  47.5 0.0 copy-done.6
  47.5 7.6 %adjoint.1 = bf16[2,144,1024]{2,1,0:T(8,128)(2,1)S(1)} custom-call(s32[2,2,64]{2,1,0:T(2,128)S(1)} %bitcast.16, f32[2,2,64]{2,1,0:T(2,128)S(1)} %bitcast.13, bf16[16,4,9216]{2,1,0:T(4,128)(2,1)S(1)} %all-to-all-done.kernels_ref, bf16[16,4,9216]{2,1,0:T(4,128)(2,1)} %get-tuple-element.11.grads_ref, bf16[8,128,256]{2,1,0:T(8,128)(2,1)S(1)} %get-tuple-element.12.dy_all_ref), custom_call_target="tpu_custom_call" | custom-call | flops 1509949440 | bytes 4194304 | tf_op jit(solution)/shard_map/adjoint/pallas_call | solution.py:360
  55.1 1.3 %collective-permute-start.1 = (bf16[144,1024]{1,0:T(8,128)(2,1)S(1)}, bf16[144,1024]{1,0:T(8,128)(2,1)S(1)}, u32[]{:S(2)}, u32[]{:S(2)}) collective-permute-start(bf16[144,1024]{1,0:T(8,128)(2,1)S(1)} %get-tuple-element.22), channel_id=1, source_target_pairs={{0,1},{1,0},{2,3},{3,2},{4,5},{5,4},{6,7},{7,6},{8,9},{9,8},{10,11... | collective-permute-start | bytes 884744 | tf_op jit(solution)/shard_map/ppermute | solution.py:328
  56.4 0.1 constant_dynamic-slice_fusion
  56.5 0.1 copy.12
  56.6 0.1 broadcast_in_dim.7
  56.7 6.8 %collective-permute-done.1 = bf16[144,1024]{1,0:T(8,128)(2,1)S(1)} collective-permute-done((bf16[144,1024]{1,0:T(8,128)(2,1)S(1)}, bf16[144,1024]{1,0:T(8,128)(2,1)S(1)}, u32[]{:S(2)}, u32[]{:S(2)}) %collective-permute-start.1) | collective-permute-done | bytes 294944 | tf_op jit(solution)/shard_map/ppermute | solution.py:328
  63.4 0.1 slice.34
  63.6 0.7 copy.11
  64.3 0.0 copy-start.9
  64.3 11.0 %all-to-all-done.1.got_ref = bf16[16,4,9216]{2,1,0:T(4,128)(2,1)S(1)} async-done(((bf16[16,4,9216]{2,1,0:T(4,128)(2,1)}), bf16[16,4,9216]{2,1,0:T(4,128)(2,1)S(1)}, u32[]{:S(2)}, u32[]{:S(2)}) %all-to-all-start.1) | async-done | bytes 1179680 | tf_op jit(solution)/shard_map/all_to_all | solution.py:358
  75.2 2.3 %weight_sum.1 = f32[8,4,9216]{2,1,0:T(4,128)} custom-call(s32[16]{0:T(128)S(1)} %get-tuple-element.13.local_ref, f32[16]{0:T(128)S(1)} %get-tuple-element.14.logit_ref, bf16[16,4,9216]{2,1,0:T(4,128)(2,1)S(1)} %all-to-all-done.1.got_ref), custom_call_target="tpu_custom_call" | custom-call | tf_op jit(solution)/shard_map/weight_sum/pallas_call | solution.py:394
  77.6 0.0 copy-done.9
  (6 shorter events, 0.1 us)
Async XLA Ops:
  0.6 1.1 %copy-start = (bf16[8,4,9216]{2,1,0:T(4,128)(2,1)S(1)}, bf16[8,4,9216]{2,1,0:T(4,128)(2,1)}, u32[]{:S(2)}) copy-start(bf16[8,4,9216]{2,1,0:T(4,128)(2,1)} %weights_ref.1) | copy-start | bytes 1769476
  1.7 1.0 %copy-start.1 = (bf16[1,256,1024]{2,1,0:T(8,128)(2,1)S(1)}, bf16[1,256,1024]{2,1,0:T(8,128)(2,1)}, u32[]{:S(2)}) copy-start(bf16[1,256,1024]{2,1,0:T(8,128)(2,1)} %x_ref.3) | copy-start | bytes 1572868
  2.7 1.0 %copy-start.3 = (bf16[1,256,1024]{2,1,0:T(8,128)(2,1)S(1)}, bf16[1,256,1024]{2,1,0:T(8,128)(2,1)}, u32[]{:S(2)}) copy-start(bf16[1,256,1024]{2,1,0:T(8,128)(2,1)} %dy_ref.3) | copy-start | bytes 1572868
  3.8 0.7 copy-start.5
  4.5 0.7 copy-start.7
  8.0 19.9 %copy-start.2 = (bf16[1,256,1024]{2,1,0:T(8,128)(2,1)S(1)}, bf16[1,256,1024]{2,1,0:T(8,128)(2,1)}, u32[]{:S(2)}) copy-start(bf16[1,256,1024]{2,1,0:T(8,128)(2,1)} %x_ref.3) | copy-start | bytes 1572868
  8.0 19.9 %copy-start.4 = (bf16[1,256,1024]{2,1,0:T(8,128)(2,1)S(1)}, bf16[1,256,1024]{2,1,0:T(8,128)(2,1)}, u32[]{:S(2)}) copy-start(bf16[1,256,1024]{2,1,0:T(8,128)(2,1)} %dy_ref.3) | copy-start | bytes 1572868
  8.0 19.9 %copy-start.8 = (s32[2,64,2]{1,2,0:T(2,128)S(1)}, s32[2,64,2]{1,2,0:T(2,128)}, u32[]{:S(2)}) copy-start(s32[2,64,2]{1,2,0:T(2,128)} %param.9) | copy-start | bytes 3076
  8.0 34.5 %all-to-all-start = ((bf16[16,4,9216]{2,1,0:T(4,128)(2,1)}), bf16[16,4,9216]{2,1,0:T(4,128)(2,1)S(1)}, u32[]{:S(2)}, u32[]{:S(2)}) async-start(bf16[16,4,9216]{2,1,0:T(4,128)(2,1)} %get-tuple-element.9), calls=%async_computation | async-start | bytes 2359296 | tf_op jit(solution)/shard_map/all_to_all | solution.py:334
  14.7 13.1 %collective-permute-start = (bf16[2,128,1024]{2,1,0:T(8,128)(2,1)S(1)}, bf16[2,128,1024]{2,1,0:T(8,128)(2,1)S(1)}, u32[]{:S(2)}, u32[]{:S(2)}) collective-permute-start(bf16[2,128,1024]{2,1,0:T(8,128)(2,1)S(1)} %bitcast.17), channel_id=1, source_target_pairs={{0,1},{1,0},{2,3},{3,2},{4,5},{5,4},{6,7},{7,6},{8,9},{9,8},{10,11... | collective-permute-start | bytes 1572872 | tf_op jit(solution)/shard_map/ppermute | solution.py:328
  42.5 5.0 %copy-start.6 = (f32[2,64,2]{1,2,0:T(2,128)S(1)}, f32[2,64,2]{1,2,0:T(2,128)}, u32[]{:S(2)}) copy-start(f32[2,64,2]{1,2,0:T(2,128)} %param.8) | copy-start | bytes 3076
  42.5 32.8 %all-to-all-start.1 = ((bf16[16,4,9216]{2,1,0:T(4,128)(2,1)}), bf16[16,4,9216]{2,1,0:T(4,128)(2,1)S(1)}, u32[]{:S(2)}, u32[]{:S(2)}) async-start(bf16[16,4,9216]{2,1,0:T(4,128)(2,1)} %get-tuple-element.11.grads_ref), calls=%async_computation.1 | async-start | bytes 2359296 | tf_op jit(solution)/shard_map/all_to_all | solution.py:358
  55.1 8.3 %collective-permute-start.1 = (bf16[144,1024]{1,0:T(8,128)(2,1)S(1)}, bf16[144,1024]{1,0:T(8,128)(2,1)S(1)}, u32[]{:S(2)}, u32[]{:S(2)}) collective-permute-start(bf16[144,1024]{1,0:T(8,128)(2,1)S(1)} %get-tuple-element.22), channel_id=1, source_target_pairs={{0,1},{1,0},{2,3},{3,2},{4,5},{5,4},{6,7},{7,6},{8,9},{9,8},{10,11... | collective-permute-start | bytes 884744 | tf_op jit(solution)/shard_map/ppermute | solution.py:328
  64.3 13.3 %copy-start.9 = (bf16[1,256,1024]{2,1,0:T(8,128)(2,1)}, bf16[1,256,1024]{2,1,0:T(8,128)(2,1)S(1)}, u32[]{:S(2)}) copy-start(bf16[1,256,1024]{2,1,0:T(8,128)(2,1)S(1)} %fusion) | copy-start | bytes 1572868
where the time goes:
time: 78.1 us; the launch traced here: 77.6 us
  waiting for transfers between devices  39.4 us (50%)
  Pallas kernels  17.6 us (23%)
  starting transfers between devices  14.2 us (18%)
  local copies, waits for them, and re-layouts  5.64 us (7%)
    ppermute x2, waiting for transfers between devices, exchange(): lax.ppermute(blocks[step - 1], 'batch', [(i, (i + step) % batch) for i in...  18.7 us
    all_to_all x1, waiting for transfers between devices, per_device(): lax.all_to_all(grads, 'grid', split_axis=0, concat_axis=0, tiled=True)  11 us
    all_to_all x1, waiting for transfers between devices, per_device(): lax.all_to_all(picked, 'grid', split_axis=0, concat_axis=0, tiled=True)  9.76 us
    pallas_call x1, Pallas kernels, per_device(): pl.pallas_call(functools.partial(adjoint_kernel, owned), out_shape=jax.Sh...  7.58 us
    all_to_all x1, starting transfers between devices, per_device(): lax.all_to_all(picked, 'grid', split_axis=0, concat_axis=0, tiled=True)  6.7 us
    unnamed x22, local copies, waits for them, and re-layouts  5.31 us
    all_to_all x1, starting transfers between devices, per_device(): lax.all_to_all(grads, 'grid', split_axis=0, concat_axis=0, tiled=True)  5 us
    pallas_call x1, Pallas kernels, per_device(): pl.pallas_call(functools.partial(grads_kernel, owned), out_shape=(wire_sh...  4.83 us
  transfers between devices with their start and end apart: 4, of which 4 were waited for; matrix products, arithmetic and copies ran while one was open for 1% of the time, Pallas kernels for 16%

commit v1 on v0

--- a/solution.py
+++ b/solution.py
@@ -17,6 +17,7 @@
 ROWS = 8
 DOT_ROWS = 16
 VMEM_LIMIT = 48 * 1024 * 1024
+WHOLE_VMEM = 60 * 1024 * 1024
 
 
 def rolled(values, shift):
@@ -60,8 +61,9 @@
 
 
 def pick_kernel(
-    routes_ref, logits_ref, weights_ref, x_ref, dy_ref, wire_ref, send_ref, local_ref, logit_ref,
-    wire_sem, send_sem,
+    routes_hbm, logits_hbm, weights_hbm, x_hbm, dy_hbm, wire_ref, send_ref, local_ref, logit_ref,
+    routes_ref, logits_ref, weights_ref, halves_ref, table_sem, weights_sem, halves_sem, wire_sem,
+    send_sem,
 ):
     samples, top_count, patches = routes_ref.shape
     owned = weights_ref.shape[0]
@@ -70,19 +72,30 @@
     per_tile = patches // tiles
     first = lax.axis_index("grid") * owned
     mine = lax.axis_index("batch")
+    tables = [
+        pltpu.make_async_copy(routes_hbm, routes_ref, table_sem.at[0]),
+        pltpu.make_async_copy(logits_hbm, logits_ref, table_sem.at[1]),
+    ]
+    fetched = pltpu.make_async_copy(weights_hbm, weights_ref, weights_sem)
+    taken, sent = [], []
+    for step in range(1, others + 1):
+        block = lax.rem(mine + step, others + 1)
+        rows = pl.ds(pl.multiple_of(block * channels, channels), channels)
+        for which, source in enumerate((x_hbm, dy_hbm)):
+            at = (step - 1, which)
+            taken.append(
+                pltpu.make_async_copy(source.at[0, rows], halves_ref.at[at], halves_sem.at[at])
+            )
+            sent.append(
+                pltpu.make_async_copy(halves_ref.at[at], send_ref.at[at], send_sem.at[at])
+            )
+    for copy in tables + [fetched] + taken:
+        copy.start()
+    for copy in tables:
+        copy.wait()
 
     def wire_copy(tile, local):
         return pltpu.make_async_copy(weights_ref.at[local], wire_ref.at[tile], wire_sem.at[tile])
-
-    def send_copies(step):
-        block = lax.rem(mine + step, others + 1)
-        rows = pl.ds(pl.multiple_of(block * channels, channels), channels)
-        return [
-            pltpu.make_async_copy(
-                source.at[0, rows], send_ref.at[step - 1, which], send_sem.at[step - 1, which]
-            )
-            for which, source in enumerate((x_ref, dy_ref))
-        ]
 
     def pick(tile, carry):
         local = jnp.int32(0)
@@ -95,24 +108,28 @@
                     hit = (inside >= 0) & (inside < owned)
                     local = jnp.where(hit, inside, local)
                     logit = jnp.where(hit, logits_ref[sample, rank, patch], logit)
-        wire_copy(tile, local).start()
         local_ref[tile] = local
         logit_ref[tile] = logit
         return carry
 
-    lax.fori_loop(0, tiles, pick, 0)
-    for step in range(1, others + 1):
-        for copy in send_copies(step):
-            copy.start()
+    def send(tile, carry):
+        wire_copy(tile, local_ref[tile]).start()
+        return carry
 
     def finish(tile, carry):
         wire_copy(tile, 0).wait()
         return carry
 
+    lax.fori_loop(0, tiles, pick, 0)
+    fetched.wait()
+    lax.fori_loop(0, tiles, send, 0)
+    for copy in taken:
+        copy.wait()
+    for copy in sent:
+        copy.start()
     lax.fori_loop(0, tiles, finish, 0)
-    for step in range(1, others + 1):
-        for copy in send_copies(step):
-            copy.wait()
+    for copy in sent:
+        copy.wait()
 
 
 def grads_kernel(
@@ -299,7 +316,7 @@
     assert samples * per_tile * top_count == tiles and samples == batch
     smem = pl.BlockSpec(memory_space=pltpu.SMEM)
     vmem = pl.BlockSpec(memory_space=pltpu.VMEM)
-    hbm = pl.BlockSpec(memory_space=pl.ANY)
+    hbm = pl.BlockSpec(memory_space=pltpu.HBM)
     params = pltpu.CompilerParams(vmem_limit_bytes=VMEM_LIMIT)
     routes_t = routes.transpose(0, 2, 1)
     logits_t = gate_logits.transpose(0, 2, 1)
@@ -313,13 +330,20 @@
             jax.ShapeDtypeStruct((tiles,), jnp.int32),
             jax.ShapeDtypeStruct((tiles,), jnp.float32),
         ),
-        in_specs=[smem, smem, hbm, hbm, hbm],
+        in_specs=[hbm] * 5,
         out_specs=(hbm, hbm, smem, smem),
         scratch_shapes=[
+            pltpu.SMEM(routes_t.shape, jnp.int32),
+            pltpu.SMEM(routes_t.shape, jnp.float32),
+            pltpu.VMEM(weights.shape, jnp.bfloat16),
+            pltpu.VMEM((batch - 1, 2, channels, span), jnp.bfloat16),
+            pltpu.SemaphoreType.DMA((2,)),
+            pltpu.SemaphoreType.DMA,
+            pltpu.SemaphoreType.DMA((batch - 1, 2)),
             pltpu.SemaphoreType.DMA((tiles,)),
             pltpu.SemaphoreType.DMA((batch - 1, 2)),
         ],
-        compiler_params=params,
+        compiler_params=pltpu.CompilerParams(vmem_limit_bytes=WHOLE_VMEM),
         name="pick",
     )(routes_t, logits_t, weights, inputs, cotangent)
 

time: 78.1 us -> 74 us (0.948)
  local copies, waits for them, and re-layouts: 5.64 us -> 1.15 us
    unnamed x22 -> x18, local copies, waits for them, and re-layouts: 5.31 us -> 0.82 us
  transfers between devices with their start and end apart: 4 -> 4, of which waited for: 4 -> 4; matrix products, arithmetic and copies ran while one was open for 1% -> 2% of each run, Pallas kernels for 16% -> 17%
where the time goes in v1:
time: 74 us; the launch traced here: 73.7 us
  waiting for transfers between devices  39.3 us (53%)
  Pallas kernels  18.3 us (25%)
  starting transfers between devices  14.3 us (19%)
  local copies, waits for them, and re-layouts  1.15 us (2%)
  between operations  0.74 us (1%)
    ppermute x2, waiting for transfers between devices, exchange(): lax.ppermute(blocks[step - 1], 'batch', [(i, (i + step) % batch) for i in...  18.7 us
    all_to_all x1, waiting for transfers between devices, per_device(): lax.all_to_all(grads, 'grid', split_axis=0, concat_axis=0, tiled=True)  10.9 us
    all_to_all x1, waiting for transfers between devices, per_device(): lax.all_to_all(picked, 'grid', split_axis=0, concat_axis=0, tiled=True)  9.64 us
    pallas_call x1, Pallas kernels, per_device(): pl.pallas_call(functools.partial(adjoint_kernel, owned), out_shape=jax.Sh...  7.58 us
    all_to_all x1, starting transfers between devices, per_device(): lax.all_to_all(picked, 'grid', split_axis=0, concat_axis=0, tiled=True)  6.7 us
    all_to_all x1, starting transfers between devices, per_device(): lax.all_to_all(grads, 'grid', split_axis=0, concat_axis=0, tiled=True)  5 us
    pallas_call x1, Pallas kernels, per_device(): pl.pallas_call(functools.partial(grads_kernel, owned), out_shape=(wire_sh...  4.89 us
    pallas_call x1, Pallas kernels, per_device(): pl.pallas_call(pick_kernel, out_shape=(wire_shape, jax.ShapeDtypeStruct((...  3.44 us
  transfers between devices with their start and end apart: 4, of which 4 were waited for; matrix products, arithmetic and copies ran while one was open for 2% of the time, Pallas kernels for 17%

profile of v1, /device:TPU:13, one launch (start us, length us, event | category | flops | bytes accessed | tf_op | source)
XLA Modules:
  0.0 73.7 jit_solution(16087361533285197460)
XLA Ops:
  0.6 3.4 %pick.1 = (bf16[16,4,9216]{2,1,0:T(4,128)(2,1)}, bf16[1,2,128,1024]{3,2,1,0:T(8,128)(2,1)}, s32[16]{0:T(128)}, f32[16]{0:T(128)}) custom-call(s32[2,2,64]{2,1,0:T(2,128)} %bitcast.14, f32[2,2,64]{2,1,0:T(2,128)} %bitcast.12, bf16[8,4,9216]{2,1,0:T(4,128)(2,1)} %weights_hbm.1, bf16[1,256,1024]{2,1,0:T(8,128)(2,1)} %x_ref.1, bf16[1,256,1024]{2,1,0:T(8,128)(2,1)} %dy_ref.1), custom_call_target="tpu_custom_call" | custom-call | tf_op jit(solution)/shard_map/pick/pallas_call | solution.py:325
  4.1 0.0 copy-start.7
  4.1 0.0 copy-start
  4.1 0.0 copy-start.1
  4.1 0.0 copy-start.3
  4.1 6.7 %all-to-all-start = ((bf16[16,4,9216]{2,1,0:T(4,128)(2,1)}), bf16[16,4,9216]{2,1,0:T(4,128)(2,1)S(1)}, u32[]{:S(2)}, u32[]{:S(2)}) async-start(bf16[16,4,9216]{2,1,0:T(4,128)(2,1)} %get-tuple-element.9), calls=%async_computation | async-start | bytes 2359296 | tf_op jit(solution)/shard_map/all_to_all | solution.py:358
  10.8 0.0 copy-done.7
  10.8 1.3 %collective-permute-start = (bf16[2,128,1024]{2,1,0:T(8,128)(2,1)S(1)}, bf16[2,128,1024]{2,1,0:T(8,128)(2,1)S(1)}, u32[]{:S(2)}, u32[]{:S(2)}) collective-permute-start(bf16[2,128,1024]{2,1,0:T(8,128)(2,1)S(1)} %bitcast.18), channel_id=1, source_target_pairs={{0,1},{1,0},{2,3},{3,2},{4,5},{5,4},{6,7},{7,6},{8,9},{9,8},{10,11... | collective-permute-start | bytes 1572872 | tf_op jit(solution)/shard_map/ppermute | solution.py:352
  12.1 11.9 %collective-permute-done = bf16[2,128,1024]{2,1,0:T(8,128)(2,1)S(1)} collective-permute-done((bf16[2,128,1024]{2,1,0:T(8,128)(2,1)S(1)}, bf16[2,128,1024]{2,1,0:T(8,128)(2,1)S(1)}, u32[]{:S(2)}, u32[]{:S(2)}) %collective-permute-start) | collective-permute-done | bytes 524320 | tf_op jit(solution)/shard_map/ppermute | solution.py:352
  24.0 0.0 copy-done
  24.0 0.0 copy-done.1
  24.0 0.0 copy-done.3
  24.1 4.9 %kernel_grads.1 = (bf16[16,4,9216]{2,1,0:T(4,128)(2,1)}, bf16[8,128,256]{2,1,0:T(8,128)(2,1)S(1)}) custom-call(s32[2,2,64]{2,1,0:T(2,128)S(1)} %bitcast.15, bf16[1,256,1024]{2,1,0:T(8,128)(2,1)S(1)} %copy-done, bf16[1,256,1024]{2,1,0:T(8,128)(2,1)S(1)} %copy-done.1, bf16[1,2,128,1024]{3,2,1,0:T(8,128)(2,1)S(1)} %bitcast.17), custom_call_target="tpu_custom_call" | custom-call | flops 1509949440 | bytes 4194304 | tf_op jit(solution)/shard_map/kernel_grads/pallas_call | solution.py:362
  28.9 9.6 %all-to-all-done.kernels_ref = bf16[16,4,9216]{2,1,0:T(4,128)(2,1)S(1)} async-done(((bf16[16,4,9216]{2,1,0:T(4,128)(2,1)}), bf16[16,4,9216]{2,1,0:T(4,128)(2,1)S(1)}, u32[]{:S(2)}, u32[]{:S(2)}) %all-to-all-start) | async-done | bytes 1179680 | tf_op jit(solution)/shard_map/all_to_all | solution.py:358
  38.6 0.0 copy-start.2
  38.6 5.0 %all-to-all-start.1 = ((bf16[16,4,9216]{2,1,0:T(4,128)(2,1)}), bf16[16,4,9216]{2,1,0:T(4,128)(2,1)S(1)}, u32[]{:S(2)}, u32[]{:S(2)}) async-start(bf16[16,4,9216]{2,1,0:T(4,128)(2,1)} %get-tuple-element.11.grads_ref), calls=%async_computation.1 | async-start | bytes 2359296 | tf_op jit(solution)/shard_map/all_to_all | solution.py:382
  43.6 0.0 copy-done.2
  43.6 7.6 %adjoint.1 = bf16[2,144,1024]{2,1,0:T(8,128)(2,1)S(1)} custom-call(s32[2,2,64]{2,1,0:T(2,128)S(1)} %bitcast.16, f32[2,2,64]{2,1,0:T(2,128)S(1)} %bitcast.13, bf16[16,4,9216]{2,1,0:T(4,128)(2,1)S(1)} %all-to-all-done.kernels_ref, bf16[16,4,9216]{2,1,0:T(4,128)(2,1)} %get-tuple-element.11.grads_ref, bf16[8,128,256]{2,1,0:T(8,128)(2,1)S(1)} %get-tuple-element.12.dy_all_ref), custom_call_target="tpu_custom_call" | custom-call | flops 1509949440 | bytes 4194304 | tf_op jit(solution)/shard_map/adjoint/pallas_call | solution.py:384
  51.2 0.0 copy-start.4
  51.2 0.0 copy-start.5
  51.2 1.3 %collective-permute-start.1 = (bf16[144,1024]{1,0:T(8,128)(2,1)S(1)}, bf16[144,1024]{1,0:T(8,128)(2,1)S(1)}, u32[]{:S(2)}, u32[]{:S(2)}) collective-permute-start(bf16[144,1024]{1,0:T(8,128)(2,1)S(1)} %get-tuple-element.22), channel_id=1, source_target_pairs={{0,1},{1,0},{2,3},{3,2},{4,5},{5,4},{6,7},{7,6},{8,9},{9,8},{10,11... | collective-permute-start | bytes 884744 | tf_op jit(solution)/shard_map/ppermute | solution.py:352
  52.5 0.1 constant_dynamic-slice_fusion
  52.6 0.1 copy.12
  52.7 0.1 broadcast_in_dim.7
  52.8 6.8 %collective-permute-done.1 = bf16[144,1024]{1,0:T(8,128)(2,1)S(1)} collective-permute-done((bf16[144,1024]{1,0:T(8,128)(2,1)S(1)}, bf16[144,1024]{1,0:T(8,128)(2,1)S(1)}, u32[]{:S(2)}, u32[]{:S(2)}) %collective-permute-start.1) | collective-permute-done | bytes 294944 | tf_op jit(solution)/shard_map/ppermute | solution.py:352
  59.6 0.1 slice.34
  59.7 0.7 copy.11
  60.4 0.0 copy-start.6
  60.4 10.9 %all-to-all-done.1.got_ref = bf16[16,4,9216]{2,1,0:T(4,128)(2,1)S(1)} async-done(((bf16[16,4,9216]{2,1,0:T(4,128)(2,1)}), bf16[16,4,9216]{2,1,0:T(4,128)(2,1)S(1)}, u32[]{:S(2)}, u32[]{:S(2)}) %all-to-all-start.1) | async-done | bytes 1179680 | tf_op jit(solution)/shard_map/all_to_all | solution.py:382
  71.3 0.0 copy-done.4
  71.3 0.0 copy-done.5
  71.3 2.4 %weight_sum.1 = f32[8,4,9216]{2,1,0:T(4,128)} custom-call(s32[16]{0:T(128)S(1)} %copy-done.4, f32[16]{0:T(128)S(1)} %copy-done.5, bf16[16,4,9216]{2,1,0:T(4,128)(2,1)S(1)} %all-to-all-done.1.got_ref), custom_call_target="tpu_custom_call" | custom-call | tf_op jit(solution)/shard_map/weight_sum/pallas_call | solution.py:418
  73.7 0.0 copy-done.6
  (6 shorter events, 0.1 us)
Async XLA Ops:
  4.1 6.7 %copy-start.7 = (bf16[1,2,128,1024]{3,2,1,0:T(8,128)(2,1)S(1)}, bf16[1,2,128,1024]{3,2,1,0:T(8,128)(2,1)}, u32[]{:S(2)}) copy-start(bf16[1,2,128,1024]{3,2,1,0:T(8,128)(2,1)} %get-tuple-element.10) | copy-start | bytes 1572868
  4.1 20.0 %copy-start = (bf16[1,256,1024]{2,1,0:T(8,128)(2,1)S(1)}, bf16[1,256,1024]{2,1,0:T(8,128)(2,1)}, u32[]{:S(2)}) copy-start(bf16[1,256,1024]{2,1,0:T(8,128)(2,1)} %x_ref.1) | copy-start | bytes 1572868
  4.1 19.9 %copy-start.1 = (bf16[1,256,1024]{2,1,0:T(8,128)(2,1)S(1)}, bf16[1,256,1024]{2,1,0:T(8,128)(2,1)}, u32[]{:S(2)}) copy-start(bf16[1,256,1024]{2,1,0:T(8,128)(2,1)} %dy_ref.1) | copy-start | bytes 1572868
  4.1 19.9 %copy-start.3 = (s32[2,64,2]{1,2,0:T(2,128)S(1)}, s32[2,64,2]{1,2,0:T(2,128)}, u32[]{:S(2)}) copy-start(s32[2,64,2]{1,2,0:T(2,128)} %param.9) | copy-start | bytes 3076
  4.1 34.5 %all-to-all-start = ((bf16[16,4,9216]{2,1,0:T(4,128)(2,1)}), bf16[16,4,9216]{2,1,0:T(4,128)(2,1)S(1)}, u32[]{:S(2)}, u32[]{:S(2)}) async-start(bf16[16,4,9216]{2,1,0:T(4,128)(2,1)} %get-tuple-element.9), calls=%async_computation | async-start | bytes 2359296 | tf_op jit(solution)/shard_map/all_to_all | solution.py:358
  10.8 13.2 %collective-permute-start = (bf16[2,128,1024]{2,1,0:T(8,128)(2,1)S(1)}, bf16[2,128,1024]{2,1,0:T(8,128)(2,1)S(1)}, u32[]{:S(2)}, u32[]{:S(2)}) collective-permute-start(bf16[2,128,1024]{2,1,0:T(8,128)(2,1)S(1)} %bitcast.18), channel_id=1, source_target_pairs={{0,1},{1,0},{2,3},{3,2},{4,5},{5,4},{6,7},{7,6},{8,9},{9,8},{10,11... | collective-permute-start | bytes 1572872 | tf_op jit(solution)/shard_map/ppermute | solution.py:352
  38.6 5.0 %copy-start.2 = (f32[2,64,2]{1,2,0:T(2,128)S(1)}, f32[2,64,2]{1,2,0:T(2,128)}, u32[]{:S(2)}) copy-start(f32[2,64,2]{1,2,0:T(2,128)} %param.8) | copy-start | bytes 3076
  38.6 32.8 %all-to-all-start.1 = ((bf16[16,4,9216]{2,1,0:T(4,128)(2,1)}), bf16[16,4,9216]{2,1,0:T(4,128)(2,1)S(1)}, u32[]{:S(2)}, u32[]{:S(2)}) async-start(bf16[16,4,9216]{2,1,0:T(4,128)(2,1)} %get-tuple-element.11.grads_ref), calls=%async_computation.1 | async-start | bytes 2359296 | tf_op jit(solution)/shard_map/all_to_all | solution.py:382
  51.2 20.2 %copy-start.4 = (s32[16]{0:T(128)S(1)}, s32[16]{0:T(128)}, u32[]{:S(2)}) copy-start(s32[16]{0:T(128)} %get-tuple-element.13.local_ref) | copy-start | bytes 196
  51.2 20.2 %copy-start.5 = (f32[16]{0:T(128)S(1)}, f32[16]{0:T(128)}, u32[]{:S(2)}) copy-start(f32[16]{0:T(128)} %get-tuple-element.14.logit_ref) | copy-start | bytes 196
  51.2 8.3 %collective-permute-start.1 = (bf16[144,1024]{1,0:T(8,128)(2,1)S(1)}, bf16[144,1024]{1,0:T(8,128)(2,1)S(1)}, u32[]{:S(2)}, u32[]{:S(2)}) collective-permute-start(bf16[144,1024]{1,0:T(8,128)(2,1)S(1)} %get-tuple-element.22), channel_id=1, source_target_pairs={{0,1},{1,0},{2,3},{3,2},{4,5},{5,4},{6,7},{7,6},{8,9},{9,8},{10,11... | collective-permute-start | bytes 884744 | tf_op jit(solution)/shard_map/ppermute | solution.py:352
  60.4 13.3 %copy-start.6 = (bf16[1,256,1024]{2,1,0:T(8,128)(2,1)}, bf16[1,256,1024]{2,1,0:T(8,128)(2,1)S(1)}, u32[]{:S(2)}) copy-start(bf16[1,256,1024]{2,1,0:T(8,128)(2,1)S(1)} %fusion) | copy-start | bytes 1572868

commit v2 on v1

--- a/solution.py
+++ b/solution.py
@@ -16,7 +16,8 @@
 QUAD = 4 * ROW
 ROWS = 8
 DOT_ROWS = 16
-VMEM_LIMIT = 48 * 1024 * 1024
+VMEM_LIMIT = 32 * 1024 * 1024
+COST = 20_000_000_000
 WHOLE_VMEM = 60 * 1024 * 1024
 
 
@@ -60,23 +61,25 @@
         ref[at // 128, start:start + values.shape[0], :piece.shape[1]] = piece
 
 
-def pick_kernel(
-    routes_hbm, logits_hbm, weights_hbm, x_hbm, dy_hbm, wire_ref, send_ref, local_ref, logit_ref,
-    routes_ref, logits_ref, weights_ref, halves_ref, table_sem, weights_sem, halves_sem, wire_sem,
-    send_sem,
+def pair_order(tiles):
+    near, far = list(range(tiles // 4)), list(range(tiles // 4, tiles // 2))
+    return near[1:3] + far + near[3:] + near[:1]
+
+
+def scan_kernel(
+    owned, routes_hbm, logits_hbm, x_hbm, dy_hbm, send_ref, local_ref, logit_ref, beside_ref,
+    routes_ref, logits_ref, halves_ref, table_sem, halves_sem, send_sem,
 ):
     samples, top_count, patches = routes_ref.shape
-    owned = weights_ref.shape[0]
-    tiles = wire_ref.shape[0]
+    tiles = local_ref.shape[0]
     others, _, channels, _ = send_ref.shape
     per_tile = patches // tiles
-    first = lax.axis_index("grid") * owned
+    here = lax.axis_index("grid")
     mine = lax.axis_index("batch")
     tables = [
         pltpu.make_async_copy(routes_hbm, routes_ref, table_sem.at[0]),
         pltpu.make_async_copy(logits_hbm, logits_ref, table_sem.at[1]),
     ]
-    fetched = pltpu.make_async_copy(weights_hbm, weights_ref, weights_sem)
     taken, sent = [], []
     for step in range(1, others + 1):
         block = lax.rem(mine + step, others + 1)
@@ -89,57 +92,75 @@
             sent.append(
                 pltpu.make_async_copy(halves_ref.at[at], send_ref.at[at], send_sem.at[at])
             )
-    for copy in tables + [fetched] + taken:
+    for copy in tables + taken:
         copy.start()
     for copy in tables:
         copy.wait()
-
-    def wire_copy(tile, local):
-        return pltpu.make_async_copy(weights_ref.at[local], wire_ref.at[tile], wire_sem.at[tile])
-
-    def pick(tile, carry):
-        local = jnp.int32(0)
+    for copy in taken:
+        copy.wait()
+    for copy in sent:
+        copy.start()
+    first = here * owned
+    first_beside = (here ^ 1) * owned
+
+    def scan(tile, carry):
+        local, beside = jnp.int32(0), jnp.int32(0)
         logit = jnp.float32(0)
         for sample in range(samples):
             for place in range(per_tile):
                 for rank in range(top_count):
                     patch = tile * per_tile + place
-                    inside = routes_ref[sample, rank, patch] - first
+                    expert = routes_ref[sample, rank, patch]
+                    inside = expert - first
                     hit = (inside >= 0) & (inside < owned)
                     local = jnp.where(hit, inside, local)
                     logit = jnp.where(hit, logits_ref[sample, rank, patch], logit)
+                    inside = expert - first_beside
+                    hit = (inside >= 0) & (inside < owned)
+                    beside = jnp.where(hit, inside, beside)
         local_ref[tile] = local
         logit_ref[tile] = logit
+        beside_ref[tile] = beside
         return carry
 
-    def send(tile, carry):
-        wire_copy(tile, local_ref[tile]).start()
-        return carry
-
-    def finish(tile, carry):
-        wire_copy(tile, 0).wait()
-        return carry
-
-    lax.fori_loop(0, tiles, pick, 0)
-    fetched.wait()
-    lax.fori_loop(0, tiles, send, 0)
-    for copy in taken:
-        copy.wait()
-    for copy in sent:
-        copy.start()
-    lax.fori_loop(0, tiles, finish, 0)
+    lax.fori_loop(0, tiles, scan, 0)
     for copy in sent:
         copy.wait()
 
 
+def pack_kernel(local_ref, beside_ref, own_hbm, beside_hbm, *rest):
+    pair_refs, (own_ref, next_ref, fetch_sem, pair_sem) = rest[:-4], rest[-4:]
+    here = lax.axis_index("grid")
+    fetches = [
+        pltpu.make_async_copy(own_hbm, own_ref, fetch_sem.at[0]),
+        pltpu.make_async_copy(beside_hbm, next_ref, fetch_sem.at[1]),
+    ]
+    for copy in fetches:
+        copy.start()
+    copies = []
+    for which, (ids, source) in enumerate(((local_ref, own_ref), (beside_ref, next_ref))):
+        fetches[which].wait()
+        for pair, target in zip(pair_order(2 * len(pair_refs)), pair_refs):
+            copies.append(
+                pltpu.make_async_copy(
+                    source.at[ids[here ^ (2 * pair)]], target.at[which], pair_sem.at[pair, which]
+                )
+            )
+            copies[-1].start()
+    for copy in copies:
+        copy.wait()
+
+
 def grads_kernel(
-    owned, routes_ref, x_ref, dy_ref, got_ref, wire_ref, dy_all_ref, x_all_ref, taps_ref, grad_ref
+    owned, routes_ref, x_ref, dy_ref, got_ref, wire_ref, grads_ref, dy_all_ref, x_all_ref, taps_ref,
+    grad_ref,
 ):
     samples, top_count, patches = routes_ref.shape
     tiles, groups, _ = wire_ref.shape
     others, _, channels, _ = got_ref.shape
     per_tile = patches // tiles
-    together = ROWS // groups
+    together = min(ROWS // groups, per_tile)
+    rows_count = together * groups
     tile = lax.axis_index("grid")
     mine = lax.axis_index("batch")
     own_rows = pl.ds(pl.multiple_of(mine * channels, channels), channels)
@@ -151,11 +172,11 @@
             sample = lax.rem(mine - step + others + 1, others + 1)
             x_all_ref[sample * per_tile + place] = got_ref[step - 1, 0, :, span]
             dy_all_ref[sample * per_tile + place] = got_ref[step - 1, 1, :, span]
-    grad_ref[WIDE // 128 - 1] = jnp.zeros((ROWS * CG, 128), jnp.float32)
+    grad_ref[WIDE // 128 - 1] = jnp.zeros((rows_count * CG, 128), jnp.float32)
     masks = pixel_masks(CG)
 
     def work(block, carry):
-        for unit in range(ROWS):
+        for unit in range(rows_count):
             patch = block * together + unit // groups
             rows = slice((unit % groups) * CG, (unit % groups + 1) * CG)
             x_unit = x_all_ref[patch, rows, :].astype(jnp.float32)
@@ -176,16 +197,14 @@
         for place in range(together):
             patch = block * together + place
             column = tile * per_tile + lax.rem(patch, per_tile)
-            slots.append(
-                [
-                    lax.div(routes_ref[lax.div(patch, per_tile), rank, column], owned)
-                    for rank in range(top_count)
-                ]
-            )
+            slots.append([])
+            for rank in range(top_count):
+                expert = routes_ref[lax.div(patch, per_tile), rank, column]
+                slots[-1].append(lax.div(expert, owned))
         for quad in range(CG // 4):
             parts = [None] * TAPS
             for j in range(4):
-                line = rolled(strided(grad_ref, quad * 4 + j, ROWS, CG), 32 * j)
+                line = rolled(strided(grad_ref, quad * 4 + j, rows_count, CG), 32 * j)
                 for m in range(3):
                     piece = line[:, m * 128:(m + 1) * 128]
                     at = 2 * j + m
@@ -193,26 +212,43 @@
             flat = jnp.concatenate(parts, axis=1)
             for place in range(together):
                 value = flat[place * groups:(place + 1) * groups].astype(jnp.bfloat16)
+                lanes = slice(quad * QUAD, (quad + 1) * QUAD)
+                grads_ref[block * together + place, :, lanes] = value
                 for slot in slots[place]:
-                    wire_ref[slot, :, quad * QUAD:(quad + 1) * QUAD] = value
+                    wire_ref[slot, :, lanes] = value
         return carry
 
     lax.fori_loop(0, samples * per_tile // together, work, 0)
 
 
 def adjoint_kernel(
-    owned, routes_ref, logits_ref, kernels_ref, grads_ref, dy_all_ref, out_ref,
-    flat_ref, mixed_ref, spread_ref, dots_ref,
+    owned, routes_ref, logits_ref, grads_ref, dy_all_ref, *rest
 ):
+    pair_refs, rest = rest[:-7], rest[-7:]
+    out_ref, kernels_ref, flat_ref, mixed_ref, spread_ref, dots_ref, place_sem = rest
     samples, top_count, patches = routes_ref.shape
     tiles, groups, _ = kernels_ref.shape
     channels = groups * CG
     per_tile = patches // tiles
-    together = ROWS // groups
+    together = min(ROWS // groups, per_tile)
+    rows_count = together * groups
     blocks = samples * per_tile // together
     tile = lax.axis_index("grid")
     mine = lax.axis_index("batch")
+    places = [
+        (source.at[which], kernels_ref.at[tile ^ (2 * pair + which)])
+        for pair, source in zip(pair_order(tiles), pair_refs)
+        for which in range(2)
+    ]
+    copies = [
+        pltpu.make_async_copy(source, target, place_sem.at[number])
+        for number, (source, target) in enumerate(places)
+    ]
+    for copy in copies:
+        copy.start()
     masks = pixel_masks(CG)
+    for copy in copies:
+        copy.wait()
 
     def work(block, carry):
         for place in range(together):
@@ -228,24 +264,24 @@
             for at in range(0, CG * ROW, 128):
                 lanes = slice(at, at + 128)
                 mixed = jnp.zeros((groups, 128), jnp.float32)
+                grad = grads_ref[patch, :, lanes].astype(jnp.float32)
                 for rank in range(top_count):
                     kernel = kernels_ref[slots[rank], :, lanes].astype(jnp.float32)
-                    grad = grads_ref[slots[rank], :, lanes].astype(jnp.float32)
                     dots[rank] += kernel * grad
                     mixed += gates[rank] * kernel
                 flat_ref[place * groups:(place + 1) * groups, lanes] = mixed
             for rank in range(top_count):
-                start = (block * top_count + rank) * ROWS + place * groups
+                start = (block * top_count + rank) * rows_count + place * groups
                 dots_ref[pl.ds(start, groups), :] = dots[rank]
         for quad in range(CG // 4):
             for j in range(4):
                 start = quad * QUAD + 2 * j * 128
                 line = rolled(flat_ref[:, start:start + WIDE], -32 * j)
                 for m in range(WIDE // 128):
-                    mixed_ref[m, pl.ds(quad * 4 + j, ROWS, stride=CG), :] = line[
+                    mixed_ref[m, pl.ds(quad * 4 + j, rows_count, stride=CG), :] = line[
                         :, m * 128:(m + 1) * 128
                     ]
-        for unit in range(ROWS):
+        for unit in range(rows_count):
             patch = block * together + unit // groups
             rows = slice((unit % groups) * CG, (unit % groups + 1) * CG)
             kernel = joined(mixed_ref, unit * CG, CG)[:, :ROW].astype(jnp.bfloat16)
@@ -266,7 +302,7 @@
         return carry
 
     lax.fori_loop(0, blocks, work, 0)
-    count = blocks * top_count * ROWS
+    count = blocks * top_count * rows_count
     sums = lax.dot_general(
         jnp.ones((DOT_ROWS, 128), jnp.float32),
         dots_ref[...],
@@ -276,8 +312,8 @@
     )
     row = lax.broadcasted_iota(jnp.int32, (count, 128), 0)
     lane = lax.broadcasted_iota(jnp.int32, (count, 128), 1)
-    row_patch = row // (top_count * ROWS) * together + row % ROWS // groups
-    row_rank = row // ROWS % top_count
+    row_patch = row // (top_count * rows_count) * together + row % rows_count // groups
+    row_rank = row // rows_count % top_count
     chosen = (lane == row_patch * top_count + row_rank).astype(jnp.float32)
     route_dots = lax.dot_general(
         sums,
@@ -317,35 +353,63 @@
     smem = pl.BlockSpec(memory_space=pltpu.SMEM)
     vmem = pl.BlockSpec(memory_space=pltpu.VMEM)
     hbm = pl.BlockSpec(memory_space=pltpu.HBM)
+    anywhere = pl.BlockSpec(memory_space=pl.ANY)
     params = pltpu.CompilerParams(vmem_limit_bytes=VMEM_LIMIT)
     routes_t = routes.transpose(0, 2, 1)
     logits_t = gate_logits.transpose(0, 2, 1)
-    wire_shape = jax.ShapeDtypeStruct((tiles, groups, width), jnp.bfloat16)
-
-    picked, to_send, local, logit = pl.pallas_call(
-        pick_kernel,
+    assert tiles & (tiles - 1) == 0 and tiles > 1
+    together = min(ROWS // groups, per_tile)
+    rows = together * groups
+
+    def blocks_shape(count):
+        return jax.ShapeDtypeStruct((count, groups, width), jnp.bfloat16)
+
+    def swap(blocks, step):
+        return lax.ppermute(blocks, "grid", [(i, i ^ step) for i in range(tiles)])
+
+    weights_beside = swap(weights, 1)
+    table = jax.ShapeDtypeStruct((tiles,), jnp.int32)
+    to_send, local, logit, beside = pl.pallas_call(
+        functools.partial(scan_kernel, owned),
         out_shape=(
-            wire_shape,
             jax.ShapeDtypeStruct((batch - 1, 2, channels, span), jnp.bfloat16),
-            jax.ShapeDtypeStruct((tiles,), jnp.int32),
+            table,
             jax.ShapeDtypeStruct((tiles,), jnp.float32),
+            table,
         ),
-        in_specs=[hbm] * 5,
-        out_specs=(hbm, hbm, smem, smem),
+        in_specs=[hbm] * 4,
+        out_specs=(hbm, smem, smem, smem),
         scratch_shapes=[
             pltpu.SMEM(routes_t.shape, jnp.int32),
             pltpu.SMEM(routes_t.shape, jnp.float32),
-            pltpu.VMEM(weights.shape, jnp.bfloat16),
             pltpu.VMEM((batch - 1, 2, channels, span), jnp.bfloat16),
             pltpu.SemaphoreType.DMA((2,)),
-            pltpu.SemaphoreType.DMA,
             pltpu.SemaphoreType.DMA((batch - 1, 2)),
-            pltpu.SemaphoreType.DMA((tiles,)),
             pltpu.SemaphoreType.DMA((batch - 1, 2)),
         ],
         compiler_params=pltpu.CompilerParams(vmem_limit_bytes=WHOLE_VMEM),
-        name="pick",
-    )(routes_t, logits_t, weights, inputs, cotangent)
+        cost_estimate=pl.CostEstimate(flops=COST, bytes_accessed=1, transcendentals=0),
+        name="scan",
+    )(routes_t, logits_t, inputs, cotangent)
+
+    pairs = pl.pallas_call(
+        pack_kernel,
+        out_shape=(blocks_shape(2),) * (tiles // 2),
+        in_specs=[smem, smem, hbm, hbm],
+        out_specs=(hbm,) * (tiles // 2),
+        scratch_shapes=[
+            pltpu.VMEM(weights.shape, jnp.bfloat16),
+            pltpu.VMEM(weights.shape, jnp.bfloat16),
+            pltpu.SemaphoreType.DMA((2,)),
+            pltpu.SemaphoreType.DMA((tiles // 2, 2)),
+        ],
+        compiler_params=pltpu.CompilerParams(vmem_limit_bytes=WHOLE_VMEM),
+        name="pack",
+    )(local, beside, weights, weights_beside)
+    pairs = [
+        blocks if pair == 0 else swap(blocks, 2 * pair)
+        for pair, blocks in zip(pair_order(tiles), pairs)
+    ]
 
     def exchange(blocks):
         return [
@@ -355,49 +419,47 @@
             for step in range(1, batch)
         ]
 
-    kernels = lax.all_to_all(picked, "grid", split_axis=0, concat_axis=0, tiled=True)
     got = jnp.stack(exchange([to_send[step] for step in range(batch - 1)]))
 
     work = samples * patches // tiles * groups * width * PIX * 2
-    grads, dy_all = pl.pallas_call(
+    wire, grads, dy_all = pl.pallas_call(
         functools.partial(grads_kernel, owned),
         out_shape=(
-            wire_shape,
+            blocks_shape(tiles),
+            blocks_shape(samples * per_tile),
             jax.ShapeDtypeStruct((samples * per_tile, channels, PIX), jnp.bfloat16),
         ),
         in_specs=[smem, vmem, vmem, vmem],
-        out_specs=(vmem, vmem),
+        out_specs=(vmem, vmem, vmem),
         scratch_shapes=[
             pltpu.VMEM((samples * per_tile, channels, PIX), jnp.bfloat16),
-            pltpu.VMEM((PIX // 128, ROWS * ROW, 128), jnp.float32),
-            pltpu.VMEM((WIDE // 128, ROWS * CG, 128), jnp.float32),
+            pltpu.VMEM((PIX // 128, rows * ROW, 128), jnp.float32),
+            pltpu.VMEM((WIDE // 128, rows * CG, 128), jnp.float32),
         ],
         compiler_params=params,
-        cost_estimate=pl.CostEstimate(
-            flops=work * 10, bytes_accessed=4 * 1024 * 1024, transcendentals=0
-        ),
+        cost_estimate=pl.CostEstimate(flops=COST, bytes_accessed=1, transcendentals=0),
         name="kernel_grads",
     )(routes_t, inputs, cotangent, got)
 
-    grads_back = lax.all_to_all(grads, "grid", split_axis=0, concat_axis=0, tiled=True)
+    grads_back = lax.all_to_all(wire, "grid", split_axis=0, concat_axis=0, tiled=True)
 
     parts = pl.pallas_call(
         functools.partial(adjoint_kernel, owned),
         out_shape=jax.ShapeDtypeStruct((batch, channels + DOT_ROWS, span), jnp.bfloat16),
-        in_specs=[smem, smem, vmem, vmem, vmem],
+        in_specs=[smem, smem, vmem, vmem] + [anywhere] * (tiles // 2),
         out_specs=vmem,
         scratch_shapes=[
-            pltpu.VMEM((ROWS, width), jnp.float32),
-            pltpu.VMEM((WIDE // 128, ROWS * CG, 128), jnp.float32),
-            pltpu.VMEM((PIX // 128, ROWS * ROW, 128), jnp.float32),
+            pltpu.VMEM((tiles, groups, width), jnp.bfloat16),
+            pltpu.VMEM((rows, width), jnp.float32),
+            pltpu.VMEM((WIDE // 128, rows * CG, 128), jnp.float32),
+            pltpu.VMEM((PIX // 128, rows * ROW, 128), jnp.float32),
             pltpu.VMEM((samples * per_tile * top_count * groups, 128), jnp.float32),
+            pltpu.SemaphoreType.DMA((tiles,)),
         ],
         compiler_params=params,
-        cost_estimate=pl.CostEstimate(
-            flops=work * 10, bytes_accessed=4 * 1024 * 1024, transcendentals=0
-        ),
+        cost_estimate=pl.CostEstimate(flops=COST, bytes_accessed=1, transcendentals=0),
         name="adjoint",
-    )(routes_t, logits_t, kernels, grads, dy_all)
+    )(routes_t, logits_t, grads, dy_all, *pairs)
 
     arrived = exchange([parts[step] for step in range(1, batch)])
     mine = lax.axis_index("batch")

time: 74 us -> 67.3 us (0.909)
  waiting for transfers between devices: 39.3 us -> 23 us
  starting transfers between devices: 14.3 us -> 18.2 us
  Pallas kernels: 18.3 us -> 21.2 us
  local copies, waits for them, and re-layouts: 1.15 us -> 3.78 us
    all_to_all x2 -> x1, waiting for transfers between devices: 20.6 us -> 9.59 us  [per_device(): lax.all_to_all(wire, 'grid', split_axis=0, concat_axis=0, tiled=True)]
    ppermute x0 -> x8, starting transfers between devices: none -> 8.92 us  [swap(): return lax.ppermute(blocks, 'grid', [(i, i ^ step) for i in range(tiles)])]
    ppermute x2, waiting for transfers between devices: 18.7 us -> 10.4 us  [exchange(): lax.ppermute(blocks[step - 1], 'batch', [(i, (i + step) % batch) for i in...]
    all_to_all x2 -> x1, starting transfers between devices: 11.7 us -> 7.7 us  [per_device(): lax.all_to_all(wire, 'grid', split_axis=0, concat_axis=0, tiled=True)]
    ppermute x0 -> x8, waiting for transfers between devices: none -> 3.06 us  [swap(): return lax.ppermute(blocks, 'grid', [(i, i ^ step) for i in range(tiles)])]
    unnamed x18 -> x24, local copies, waits for them, and re-layouts: 0.82 us -> 3.46 us
    pallas_call x2 -> x3, Pallas kernels: 8.33 us -> 10.2 us  [the longest x1 4.84 us: per_device(): pl.pallas_call(functools.partial(grads_kernel, owned), out_shape=(blocks_...]
    pallas_call x1, Pallas kernels: 7.58 us -> 8.61 us  [per_device(): pl.pallas_call(functools.partial(adjoint_kernel, owned), out_shape=jax.Sh...]
  transfers between devices with their start and end apart: 4 -> 11, of which waited for: 4 -> 4; matrix products, arithmetic and copies ran while one was open for 2% -> 2% of each run, Pallas kernels for 17% -> 28%
where the time goes in v2:
time: 67.3 us; the launch traced here: 67 us
  waiting for transfers between devices  23 us (34%)
  Pallas kernels  21.2 us (32%)
  starting transfers between devices  18.2 us (27%)
  local copies, waits for them, and re-layouts  3.78 us (6%)
  between operations  0.79 us (1%)
    ppermute x2, waiting for transfers between devices, exchange(): lax.ppermute(blocks[step - 1], 'batch', [(i, (i + step) % batch) for i in...  10.4 us
    all_to_all x1, waiting for transfers between devices, per_device(): lax.all_to_all(wire, 'grid', split_axis=0, concat_axis=0, tiled=True)  9.59 us
    ppermute x8, starting transfers between devices, swap(): return lax.ppermute(blocks, 'grid', [(i, i ^ step) for i in range(tiles)])  8.92 us
    pallas_call x1, Pallas kernels, per_device(): pl.pallas_call(functools.partial(adjoint_kernel, owned), out_shape=jax.Sh...  8.61 us
    all_to_all x1, starting transfers between devices, per_device(): lax.all_to_all(wire, 'grid', split_axis=0, concat_axis=0, tiled=True)  7.7 us
    pallas_call x1, Pallas kernels, per_device(): pl.pallas_call(functools.partial(grads_kernel, owned), out_shape=(blocks_...  4.84 us
    unnamed x24, local copies, waits for them, and re-layouts  3.46 us
    ppermute x8, waiting for transfers between devices, swap(): return lax.ppermute(blocks, 'grid', [(i, i ^ step) for i in range(tiles)])  3.06 us
  transfers between devices with their start and end apart: 11, of which 4 were waited for; matrix products, arithmetic and copies ran while one was open for 2% of the time, Pallas kernels for 28%

profile of v2, /device:TPU:13, one launch (start us, length us, event | category | flops | bytes accessed | tf_op | source)
XLA Modules:
  0.0 67.0 jit_solution(13993631416177282407)
XLA Ops:
  0.6 0.7 %collective-permute-start.1 = (bf16[8,4,9216]{2,1,0:T(4,128)(2,1)}, bf16[8,4,9216]{2,1,0:T(4,128)(2,1)S(1)}, u32[]{:S(2)}, u32[]{:S(2)}) collective-permute-start(bf16[8,4,9216]{2,1,0:T(4,128)(2,1)} %own_hbm.1), channel_id=1, source_target_pairs={{0,2},{2,0},{4,6},{6,4},{8,10},{10,8},{12,14},{14,12},{16,18},{18,... | collective-permute-start | bytes 1769480 | tf_op jit(solution)/shard_map/ppermute | solution.py:368
  1.4 2.5 %scan.1 = (bf16[1,2,128,1024]{3,2,1,0:T(8,128)(2,1)}, s32[16]{0:T(128)}, f32[16]{0:T(128)}, s32[16]{0:T(128)}) custom-call(s32[2,2,64]{2,1,0:T(2,128)} %bitcast.15, f32[2,2,64]{2,1,0:T(2,128)} %bitcast.12, bf16[1,256,1024]{2,1,0:T(8,128)(2,1)} %x_ref.1, bf16[1,256,1024]{2,1,0:T(8,128)(2,1)} %dy_ref.1), custom_call_target="tpu_custom_call" | custom-call | flops 20000000000 | bytes 1 | tf_op jit(solution)/shard_map/scan/pallas_call | solution.py:372
  3.9 0.0 copy-start.3
  3.9 0.0 copy-start.4
  3.9 0.0 copy-start.6
  3.9 1.3 %collective-permute-start = (bf16[2,128,1024]{2,1,0:T(8,128)(2,1)}, bf16[2,128,1024]{2,1,0:T(8,128)(2,1)S(1)}, u32[]{:S(2)}, u32[]{:S(2)}) collective-permute-start(bf16[2,128,1024]{2,1,0:T(8,128)(2,1)} %bitcast.18), channel_id=1, source_target_pairs={{0,1},{1,0},{2,3},{3,2},{4,5},{5,4},{6,7},{7,6},{8,9},{9,8},{10,11... | collective-permute-start | bytes 1572872 | tf_op jit(solution)/shard_map/ppermute | solution.py:416
  5.2 0.0 collective-permute-done.1.beside_hbm
  5.2 0.8 %copy-done.9 = bf16[8,4,9216]{2,1,0:T(4,128)(2,1)} copy-done((bf16[8,4,9216]{2,1,0:T(4,128)(2,1)}, bf16[8,4,9216]{2,1,0:T(4,128)(2,1)S(1)}, u32[]{:S(2)}) %copy-start.9) | copy-done | bytes 589848
  6.0 2.9 %pack.1 = (bf16[2,4,9216]{2,1,0:T(4,128)(2,1)}, bf16[2,4,9216]{2,1,0:T(4,128)(2,1)}, bf16[2,4,9216]{2,1,0:T(4,128)(2,1)}, bf16[2,4,9216]{2,1,0:T(4,128)(2,1)}, b...) custom-call(s32[16]{0:T(128)} %get-tuple-element.21.local_ref, ...), custom_call_target="tpu_custom_call" | custom-call | tf_op jit(solution)/shard_map/pack/pallas_call | solution.py:395
  8.9 0.3 collective-permute-start.2
  9.2 0.2 collective-permute-start.3
  9.4 2.3 %collective-permute-start.4 = (bf16[2,4,9216]{2,1,0:T(4,128)(2,1)}, bf16[2,4,9216]{2,1,0:T(4,128)(2,1)S(1)}, u32[]{:S(2)}, u32[]{:S(2)}) collective-permute-start(bf16[2,4,9216]{2,1,0:T(4,128)(2,1)} %get-tuple-element.25), channel_id=1, source_target_pairs={{0,16},{2,18},{4,20},{6,22},{8,24},{10,26},{12,28},{14,30},{16,0},... | collective-permute-start | bytes 442376 | tf_op jit(solution)/shard_map/ppermute | solution.py:368
  11.7 1.0 %collective-permute-start.5 = (bf16[2,4,9216]{2,1,0:T(4,128)(2,1)}, bf16[2,4,9216]{2,1,0:T(4,128)(2,1)S(1)}, u32[]{:S(2)}, u32[]{:S(2)}) collective-permute-start(bf16[2,4,9216]{2,1,0:T(4,128)(2,1)} %get-tuple-element.26), channel_id=1, source_target_pairs={{0,20},{2,22},{4,16},{6,18},{8,28},{10,30},{12,24},{14,26},{16,4},... | collective-permute-start | bytes 442376 | tf_op jit(solution)/shard_map/ppermute | solution.py:368
  12.7 5.0 %collective-permute-done = bf16[2,128,1024]{2,1,0:T(8,128)(2,1)S(1)} collective-permute-done((bf16[2,128,1024]{2,1,0:T(8,128)(2,1)}, bf16[2,128,1024]{2,1,0:T(8,128)(2,1)S(1)}, u32[]{:S(2)}, u32[]{:S(2)}) %collective-permute-start) | collective-permute-done | bytes 524320 | tf_op jit(solution)/shard_map/ppermute | solution.py:416
  17.7 1.3 %collective-permute-start.6 = (bf16[2,4,9216]{2,1,0:T(4,128)(2,1)}, bf16[2,4,9216]{2,1,0:T(4,128)(2,1)S(1)}, u32[]{:S(2)}, u32[]{:S(2)}) collective-permute-start(bf16[2,4,9216]{2,1,0:T(4,128)(2,1)} %get-tuple-element.27), channel_id=1, source_target_pairs={{0,24},{2,26},{4,28},{6,30},{8,16},{10,18},{12,20},{14,22},{16,8},... | collective-permute-start | bytes 442376 | tf_op jit(solution)/shard_map/ppermute | solution.py:368
  19.0 0.0 collective-permute-done.2.rest_0_
  19.0 0.1 collective-permute-start.7
  19.1 0.0 collective-permute-done.3.rest_1_
  19.1 3.0 %collective-permute-start.8 = (bf16[2,4,9216]{2,1,0:T(4,128)(2,1)}, bf16[2,4,9216]{2,1,0:T(4,128)(2,1)S(1)}, u32[]{:S(2)}, u32[]{:S(2)}) collective-permute-start(bf16[2,4,9216]{2,1,0:T(4,128)(2,1)} %get-tuple-element.29), channel_id=1, source_target_pairs={{0,12},{2,14},{4,8},{6,10},{8,4},{10,6},{12,0},{14,2},{16,28},{18,... | collective-permute-start | bytes 442376 | tf_op jit(solution)/shard_map/ppermute | solution.py:368
  22.1 0.0 copy-done.3
  22.1 0.0 copy-done.4
  22.1 0.0 copy-done.6
  22.1 4.8 %kernel_grads.1 = (bf16[16,4,9216]{2,1,0:T(4,128)(2,1)}, bf16[8,4,9216]{2,1,0:T(4,128)(2,1)S(1)}, bf16[8,128,256]{2,1,0:T(8,128)(2,1)S(1)}) custom-call(s32[2,2,64]{2,1,0:T(2,128)S(1)} %bitcast.16, bf16[1,256,1024]{2,1,0:T(8,128)(2,1)S(1)} %copy-done.3, bf16[1,256,1024]{2,1,0:T(8,128)(2,1)S(1)} %copy-done.4, bf16[1,2,128,1024]{3,2,1,0:T(8,128)(2,1)S(1)} %bitcast.14), custom_call_target="tpu_custom_call" | custom-call | flops 20000000000 | bytes 1 | tf_op jit(solution)/shard_map/kernel_grads/pallas_call | solution.py:425
  27.0 0.8 %copy-done.7 = bf16[8,128,256]{2,1,0:T(8,128)(2,1)} copy-done((bf16[8,128,256]{2,1,0:T(8,128)(2,1)}, bf16[8,128,256]{2,1,0:T(8,128)(2,1)S(1)}, u32[]{:S(2)}) %copy-start.7) | copy-done | bytes 524312
  27.7 7.7 %all-to-all-start = ((bf16[16,4,9216]{2,1,0:T(4,128)(2,1)}), bf16[16,4,9216]{2,1,0:T(4,128)(2,1)S(1)}, u32[]{:S(2)}, u32[]{:S(2)}) async-start(bf16[16,4,9216]{2,1,0:T(4,128)(2,1)} %get-tuple-element.32), calls=%async_computation | async-start | bytes 2359296 | tf_op jit(solution)/shard_map/all_to_all | solution.py:444
  35.5 0.0 collective-permute-done.4.rest_2_
  35.5 0.0 collective-permute-done.5.rest_3_
  35.5 0.0 collective-permute-done.6.rest_4_
  35.5 3.0 %collective-permute-done.7.rest_5_ = bf16[2,4,9216]{2,1,0:T(4,128)(2,1)S(1)} collective-permute-done((bf16[2,4,9216]{2,1,0:T(4,128)(2,1)}, bf16[2,4,9216]{2,1,0:T(4,128)(2,1)S(1)}, u32[]{:S(2)}, u32[]{:S(2)}) %collective-permute-start.7) | collective-permute-done | bytes 147488 | tf_op jit(solution)/shard_map/ppermute | solution.py:368
  38.5 0.0 collective-permute-done.8.rest_6_
  38.5 0.0 copy-done
  38.5 0.0 copy-done.5
  38.5 0.0 copy-start.8
  38.5 1.0 %copy-done.8 = bf16[8,128,256]{2,1,0:T(8,128)(2,1)S(1)} copy-done((bf16[8,128,256]{2,1,0:T(8,128)(2,1)S(1)}, bf16[8,128,256]{2,1,0:T(8,128)(2,1)}, u32[]{:S(2)}) %copy-start.8) | copy-done | bytes 524312
  39.6 8.6 %adjoint.1 = bf16[2,144,1024]{2,1,0:T(8,128)(2,1)S(1)} custom-call(s32[2,2,64]{2,1,0:T(2,128)S(1)} %bitcast.17, f32[2,2,64]{2,1,0:T(2,128)S(1)} %bitcast.13, bf16[8,4,9216]{2,1,0:T(4,128)(2,1)S(1)} %get-tuple-element.19.grads_ref, bf16[8,128,256]{2,1,0:T(8,128)(2,1)S(1)} %copy-done.8, bf16[2,4,9216]{2,1,0:T(4,128)(2,1)S(1)} %collective-permute-done.2.rest_0_, ...), custom_call_target="tpu_custom_call" | custom-call | flops 20000000000 | bytes 1 | tf_op jit(solution)/shard_map/adjoint/pallas_call | solution.py:446
  48.2 0.0 copy-start.1
  48.2 0.0 copy-start.2
  48.3 0.3 collective-permute-start.9
  48.6 0.1 constant_dynamic-slice_fusion
  48.7 0.1 copy.12
  48.8 0.1 broadcast_in_dim.7
  48.8 5.4 %collective-permute-done.9 = bf16[144,1024]{1,0:T(8,128)(2,1)S(1)} collective-permute-done((bf16[144,1024]{1,0:T(8,128)(2,1)S(1)}, bf16[144,1024]{1,0:T(8,128)(2,1)S(1)}, u32[]{:S(2)}, u32[]{:S(2)}) %collective-permute-start.9) | collective-permute-done | bytes 294944 | tf_op jit(solution)/shard_map/ppermute | solution.py:416
  54.2 0.1 slice.34
  54.3 0.7 %copy.11 = f32[2,4,2]{1,2,0:T(2,128)} copy(f32[2,4,2]{2,1,0:T(4,128)S(1)} %fusion.2) | data formatting | bytes 128
  55.0 0.0 copy-start.10
  55.1 9.6 %all-to-all-done.got_ref = bf16[16,4,9216]{2,1,0:T(4,128)(2,1)S(1)} async-done(((bf16[16,4,9216]{2,1,0:T(4,128)(2,1)}), bf16[16,4,9216]{2,1,0:T(4,128)(2,1)S(1)}, u32[]{:S(2)}, u32[]{:S(2)}) %all-to-all-start) | async-done | bytes 1179680 | tf_op jit(solution)/shard_map/all_to_all | solution.py:444
  64.6 0.0 copy-done.1
  64.7 2.3 %weight_sum.1 = f32[8,4,9216]{2,1,0:T(4,128)} custom-call(s32[16]{0:T(128)S(1)} %copy-done.1, f32[16]{0:T(128)S(1)} %copy-done.2, bf16[16,4,9216]{2,1,0:T(4,128)(2,1)S(1)} %all-to-all-done.got_ref), custom_call_target="tpu_custom_call" | custom-call | tf_op jit(solution)/shard_map/weight_sum/pallas_call | solution.py:480
  (12 shorter events, 0.1 us)
Async XLA Ops:
  0.6 4.5 %collective-permute-start.1 = (bf16[8,4,9216]{2,1,0:T(4,128)(2,1)}, bf16[8,4,9216]{2,1,0:T(4,128)(2,1)S(1)}, u32[]{:S(2)}, u32[]{:S(2)}) collective-permute-start(bf16[8,4,9216]{2,1,0:T(4,128)(2,1)} %own_hbm.1), channel_id=1, source_target_pairs={{0,2},{2,0},{4,6},{6,4},{8,10},{10,8},{12,14},{14,12},{16,18},{18,... | collective-permute-start | bytes 1769480 | tf_op jit(solution)/shard_map/ppermute | solution.py:368
  3.9 18.3 %copy-start.3 = (bf16[1,256,1024]{2,1,0:T(8,128)(2,1)S(1)}, bf16[1,256,1024]{2,1,0:T(8,128)(2,1)}, u32[]{:S(2)}) copy-start(bf16[1,256,1024]{2,1,0:T(8,128)(2,1)} %x_ref.1) | copy-start | bytes 1572868
  3.9 18.2 %copy-start.4 = (bf16[1,256,1024]{2,1,0:T(8,128)(2,1)S(1)}, bf16[1,256,1024]{2,1,0:T(8,128)(2,1)}, u32[]{:S(2)}) copy-start(bf16[1,256,1024]{2,1,0:T(8,128)(2,1)} %dy_ref.1) | copy-start | bytes 1572868
  3.9 18.2 %copy-start.6 = (s32[2,64,2]{1,2,0:T(2,128)S(1)}, s32[2,64,2]{1,2,0:T(2,128)}, u32[]{:S(2)}) copy-start(s32[2,64,2]{1,2,0:T(2,128)} %param.9) | copy-start | bytes 3076
  3.9 13.8 %collective-permute-start = (bf16[2,128,1024]{2,1,0:T(8,128)(2,1)}, bf16[2,128,1024]{2,1,0:T(8,128)(2,1)S(1)}, u32[]{:S(2)}, u32[]{:S(2)}) collective-permute-start(bf16[2,128,1024]{2,1,0:T(8,128)(2,1)} %bitcast.18), channel_id=1, source_target_pairs={{0,1},{1,0},{2,3},{3,2},{4,5},{5,4},{6,7},{7,6},{8,9},{9,8},{10,11... | collective-permute-start | bytes 1572872 | tf_op jit(solution)/shard_map/ppermute | solution.py:416
  5.2 0.8 %copy-start.9 = (bf16[8,4,9216]{2,1,0:T(4,128)(2,1)}, bf16[8,4,9216]{2,1,0:T(4,128)(2,1)S(1)}, u32[]{:S(2)}) copy-start(bf16[8,4,9216]{2,1,0:T(4,128)(2,1)S(1)} %collective-permute-done.1.beside_hbm) | copy-start | bytes 1769476
  8.9 10.1 %collective-permute-start.2 = (bf16[2,4,9216]{2,1,0:T(4,128)(2,1)}, bf16[2,4,9216]{2,1,0:T(4,128)(2,1)S(1)}, u32[]{:S(2)}, u32[]{:S(2)}) collective-permute-start(bf16[2,4,9216]{2,1,0:T(4,128)(2,1)} %get-tuple-element.23), channel_id=1, source_target_pairs={{0,4},{2,6},{4,0},{6,2},{8,12},{10,14},{12,8},{14,10},{16,20},{18,... | collective-permute-start | bytes 442376 | tf_op jit(solution)/shard_map/ppermute | solution.py:368
  9.2 9.9 %collective-permute-start.3 = (bf16[2,4,9216]{2,1,0:T(4,128)(2,1)}, bf16[2,4,9216]{2,1,0:T(4,128)(2,1)S(1)}, u32[]{:S(2)}, u32[]{:S(2)}) collective-permute-start(bf16[2,4,9216]{2,1,0:T(4,128)(2,1)} %get-tuple-element.24), channel_id=1, source_target_pairs={{0,8},{2,10},{4,12},{6,14},{8,0},{10,2},{12,4},{14,6},{16,24},{18,... | collective-permute-start | bytes 442376 | tf_op jit(solution)/shard_map/ppermute | solution.py:368
  9.4 26.1 %collective-permute-start.4 = (bf16[2,4,9216]{2,1,0:T(4,128)(2,1)}, bf16[2,4,9216]{2,1,0:T(4,128)(2,1)S(1)}, u32[]{:S(2)}, u32[]{:S(2)}) collective-permute-start(bf16[2,4,9216]{2,1,0:T(4,128)(2,1)} %get-tuple-element.25), channel_id=1, source_target_pairs={{0,16},{2,18},{4,20},{6,22},{8,24},{10,26},{12,28},{14,30},{16,0},... | collective-permute-start | bytes 442376 | tf_op jit(solution)/shard_map/ppermute | solution.py:368
  11.7 23.8 %collective-permute-start.5 = (bf16[2,4,9216]{2,1,0:T(4,128)(2,1)}, bf16[2,4,9216]{2,1,0:T(4,128)(2,1)S(1)}, u32[]{:S(2)}, u32[]{:S(2)}) collective-permute-start(bf16[2,4,9216]{2,1,0:T(4,128)(2,1)} %get-tuple-element.26), channel_id=1, source_target_pairs={{0,20},{2,22},{4,16},{6,18},{8,28},{10,30},{12,24},{14,26},{16,4},... | collective-permute-start | bytes 442376 | tf_op jit(solution)/shard_map/ppermute | solution.py:368
  17.7 17.8 %collective-permute-start.6 = (bf16[2,4,9216]{2,1,0:T(4,128)(2,1)}, bf16[2,4,9216]{2,1,0:T(4,128)(2,1)S(1)}, u32[]{:S(2)}, u32[]{:S(2)}) collective-permute-start(bf16[2,4,9216]{2,1,0:T(4,128)(2,1)} %get-tuple-element.27), channel_id=1, source_target_pairs={{0,24},{2,26},{4,28},{6,30},{8,16},{10,18},{12,20},{14,22},{16,8},... | collective-permute-start | bytes 442376 | tf_op jit(solution)/shard_map/ppermute | solution.py:368
  19.0 19.5 %collective-permute-start.7 = (bf16[2,4,9216]{2,1,0:T(4,128)(2,1)}, bf16[2,4,9216]{2,1,0:T(4,128)(2,1)S(1)}, u32[]{:S(2)}, u32[]{:S(2)}) collective-permute-start(bf16[2,4,9216]{2,1,0:T(4,128)(2,1)} %get-tuple-element.28), channel_id=1, source_target_pairs={{0,28},{2,30},{4,24},{6,26},{8,20},{10,22},{12,16},{14,18},{16,12}... | collective-permute-start | bytes 442376 | tf_op jit(solution)/shard_map/ppermute | solution.py:368
  19.1 19.4 %collective-permute-start.8 = (bf16[2,4,9216]{2,1,0:T(4,128)(2,1)}, bf16[2,4,9216]{2,1,0:T(4,128)(2,1)S(1)}, u32[]{:S(2)}, u32[]{:S(2)}) collective-permute-start(bf16[2,4,9216]{2,1,0:T(4,128)(2,1)} %get-tuple-element.29), channel_id=1, source_target_pairs={{0,12},{2,14},{4,8},{6,10},{8,4},{10,6},{12,0},{14,2},{16,28},{18,... | collective-permute-start | bytes 442376 | tf_op jit(solution)/shard_map/ppermute | solution.py:368
  27.0 0.8 %copy-start.7 = (bf16[8,128,256]{2,1,0:T(8,128)(2,1)}, bf16[8,128,256]{2,1,0:T(8,128)(2,1)S(1)}, u32[]{:S(2)}) copy-start(bf16[8,128,256]{2,1,0:T(8,128)(2,1)S(1)} %get-tuple-element.20.dy_all_ref) | copy-start | bytes 1572868
  27.7 10.8 %copy-start = (f32[2,64,2]{1,2,0:T(2,128)S(1)}, f32[2,64,2]{1,2,0:T(2,128)}, u32[]{:S(2)}) copy-start(f32[2,64,2]{1,2,0:T(2,128)} %param.8) | copy-start | bytes 3076
  27.7 10.8 %copy-start.5 = (bf16[2,4,9216]{2,1,0:T(4,128)(2,1)S(1)}, bf16[2,4,9216]{2,1,0:T(4,128)(2,1)}, u32[]{:S(2)}) copy-start(bf16[2,4,9216]{2,1,0:T(4,128)(2,1)} %get-tuple-element.30.rest_7_) | copy-start | bytes 442372
  27.7 36.9 %all-to-all-start = ((bf16[16,4,9216]{2,1,0:T(4,128)(2,1)}), bf16[16,4,9216]{2,1,0:T(4,128)(2,1)S(1)}, u32[]{:S(2)}, u32[]{:S(2)}) async-start(bf16[16,4,9216]{2,1,0:T(4,128)(2,1)} %get-tuple-element.32), calls=%async_computation | async-start | bytes 2359296 | tf_op jit(solution)/shard_map/all_to_all | solution.py:444
  38.5 1.0 %copy-start.8 = (bf16[8,128,256]{2,1,0:T(8,128)(2,1)S(1)}, bf16[8,128,256]{2,1,0:T(8,128)(2,1)}, u32[]{:S(2)}) copy-start(bf16[8,128,256]{2,1,0:T(8,128)(2,1)} %copy-done.7) | copy-start | bytes 1572868
  48.2 16.5 %copy-start.1 = (s32[16]{0:T(128)S(1)}, s32[16]{0:T(128)}, u32[]{:S(2)}) copy-start(s32[16]{0:T(128)} %get-tuple-element.21.local_ref) | copy-start | bytes 196
  48.2 16.4 %copy-start.2 = (f32[16]{0:T(128)S(1)}, f32[16]{0:T(128)}, u32[]{:S(2)}) copy-start(f32[16]{0:T(128)} %get-tuple-element.31.logit_ref) | copy-start | bytes 196
  48.3 5.9 %collective-permute-start.9 = (bf16[144,1024]{1,0:T(8,128)(2,1)S(1)}, bf16[144,1024]{1,0:T(8,128)(2,1)S(1)}, u32[]{:S(2)}, u32[]{:S(2)}) collective-permute-start(bf16[144,1024]{1,0:T(8,128)(2,1)S(1)} %get-tuple-element.40), channel_id=1, source_target_pairs={{0,1},{1,0},{2,3},{3,2},{4,5},{5,4},{6,7},{7,6},{8,9},{9,8},{10,11... | collective-permute-start | bytes 884744 | tf_op jit(solution)/shard_map/ppermute | solution.py:416
  55.0 12.0 %copy-start.10 = (bf16[1,256,1024]{2,1,0:T(8,128)(2,1)}, bf16[1,256,1024]{2,1,0:T(8,128)(2,1)S(1)}, u32[]{:S(2)}) copy-start(bf16[1,256,1024]{2,1,0:T(8,128)(2,1)S(1)} %fusion) | copy-start | bytes 1572868

commit v3 on v2

--- a/solution.py
+++ b/solution.py
@@ -16,9 +16,9 @@
 QUAD = 4 * ROW
 ROWS = 8
 DOT_ROWS = 16
-VMEM_LIMIT = 32 * 1024 * 1024
+VMEM_LIMIT = 16 * 1024 * 1024
+SUM_CHUNKS = 3
 COST = 20_000_000_000
-WHOLE_VMEM = 60 * 1024 * 1024
 
 
 def rolled(values, shift):
@@ -66,87 +66,52 @@
     return near[1:3] + far + near[3:] + near[:1]
 
 
-def scan_kernel(
-    owned, routes_hbm, logits_hbm, x_hbm, dy_hbm, send_ref, local_ref, logit_ref, beside_ref,
-    routes_ref, logits_ref, halves_ref, table_sem, halves_sem, send_sem,
-):
-    samples, top_count, patches = routes_ref.shape
-    tiles = local_ref.shape[0]
+def named(routes_ref, tile, per_tile, first, owned):
+    samples, top_count, _ = routes_ref.shape
+    for sample in range(samples):
+        for place in range(per_tile):
+            for rank in range(top_count):
+                at = (sample, rank, tile * per_tile + place)
+                inside = routes_ref[at] - first
+                yield at, inside, (inside >= 0) & (inside < owned)
+
+
+def scan_kernel(owned, per_tile, routes_ref, local_ref, beside_ref):
+    here = lax.axis_index("grid")
+
+    def scan(pair, carry):
+        tile = here ^ (2 * pair)
+        for owner, found_ref in ((here, local_ref), (here ^ 1, beside_ref)):
+            found = jnp.int32(0)
+            for _, inside, hit in named(routes_ref, tile, per_tile, owner * owned, owned):
+                found += jnp.where(hit, inside, 0)
+            found_ref[pair] = found
+        return carry
+
+    lax.fori_loop(0, local_ref.shape[0], scan, 0)
+
+
+def pack_kernel(local_ref, beside_ref, own_ref, next_ref, x_ref, dy_ref, send_ref, *rest):
+    pair_refs, (pair_sem, send_sem) = rest[:-2], rest[-2:]
     others, _, channels, _ = send_ref.shape
-    per_tile = patches // tiles
-    here = lax.axis_index("grid")
     mine = lax.axis_index("batch")
-    tables = [
-        pltpu.make_async_copy(routes_hbm, routes_ref, table_sem.at[0]),
-        pltpu.make_async_copy(logits_hbm, logits_ref, table_sem.at[1]),
+    copies = [
+        pltpu.make_async_copy(
+            source.at[ids[pair]], target.at[which], pair_sem.at[pair, which]
+        )
+        for pair, target in zip(pair_order(2 * len(pair_refs)), pair_refs)
+        for which, (ids, source) in enumerate(((local_ref, own_ref), (beside_ref, next_ref)))
     ]
-    taken, sent = [], []
     for step in range(1, others + 1):
         block = lax.rem(mine + step, others + 1)
         rows = pl.ds(pl.multiple_of(block * channels, channels), channels)
-        for which, source in enumerate((x_hbm, dy_hbm)):
+        for which, source in enumerate((x_ref, dy_ref)):
             at = (step - 1, which)
-            taken.append(
-                pltpu.make_async_copy(source.at[0, rows], halves_ref.at[at], halves_sem.at[at])
+            copies.append(
+                pltpu.make_async_copy(source.at[0, rows], send_ref.at[at], send_sem.at[at])
             )
-            sent.append(
-                pltpu.make_async_copy(halves_ref.at[at], send_ref.at[at], send_sem.at[at])
-            )
-    for copy in tables + taken:
+    for copy in copies:
         copy.start()
-    for copy in tables:
-        copy.wait()
-    for copy in taken:
-        copy.wait()
-    for copy in sent:
-        copy.start()
-    first = here * owned
-    first_beside = (here ^ 1) * owned
-
-    def scan(tile, carry):
-        local, beside = jnp.int32(0), jnp.int32(0)
-        logit = jnp.float32(0)
-        for sample in range(samples):
-            for place in range(per_tile):
-                for rank in range(top_count):
-                    patch = tile * per_tile + place
-                    expert = routes_ref[sample, rank, patch]
-                    inside = expert - first
-                    hit = (inside >= 0) & (inside < owned)
-                    local = jnp.where(hit, inside, local)
-                    logit = jnp.where(hit, logits_ref[sample, rank, patch], logit)
-                    inside = expert - first_beside
-                    hit = (inside >= 0) & (inside < owned)
-                    beside = jnp.where(hit, inside, beside)
-        local_ref[tile] = local
-        logit_ref[tile] = logit
-        beside_ref[tile] = beside
-        return carry
-
-    lax.fori_loop(0, tiles, scan, 0)
-    for copy in sent:
-        copy.wait()
-
-
-def pack_kernel(local_ref, beside_ref, own_hbm, beside_hbm, *rest):
-    pair_refs, (own_ref, next_ref, fetch_sem, pair_sem) = rest[:-4], rest[-4:]
-    here = lax.axis_index("grid")
-    fetches = [
-        pltpu.make_async_copy(own_hbm, own_ref, fetch_sem.at[0]),
-        pltpu.make_async_copy(beside_hbm, next_ref, fetch_sem.at[1]),
-    ]
-    for copy in fetches:
-        copy.start()
-    copies = []
-    for which, (ids, source) in enumerate(((local_ref, own_ref), (beside_ref, next_ref))):
-        fetches[which].wait()
-        for pair, target in zip(pair_order(2 * len(pair_refs)), pair_refs):
-            copies.append(
-                pltpu.make_async_copy(
-                    source.at[ids[here ^ (2 * pair)]], target.at[which], pair_sem.at[pair, which]
-                )
-            )
-            copies[-1].start()
     for copy in copies:
         copy.wait()
 
@@ -221,18 +186,48 @@
     lax.fori_loop(0, samples * per_tile // together, work, 0)
 
 
-def adjoint_kernel(
-    owned, routes_ref, logits_ref, grads_ref, dy_all_ref, *rest
-):
-    pair_refs, rest = rest[:-7], rest[-7:]
-    out_ref, kernels_ref, flat_ref, mixed_ref, spread_ref, dots_ref, place_sem = rest
+def tables_kernel(owned, per_tile, routes_ref, logits_ref, local_ref, gate_ref):
+    first = lax.axis_index("grid") * owned
+
+    def scan(tile, carry):
+        local, logit = jnp.int32(0), jnp.float32(0)
+        for at, inside, hit in named(routes_ref, tile, per_tile, first, owned):
+            local = jnp.where(hit, inside, local)
+            logit = jnp.where(hit, logits_ref[at], logit)
+        local_ref[tile] = local
+        gate = jax.nn.sigmoid(jnp.full(gate_ref.shape[1:], logit, jnp.float32))
+        gate_ref[tile] = gate / SIDE
+        return carry
+
+    lax.fori_loop(0, local_ref.shape[0], scan, 0)
+
+
+def adjoint_unit(mixed_ref, spread_ref, unit, dy, masks):
+    kernel = joined(mixed_ref, unit * CG, CG)[:, :ROW].astype(jnp.bfloat16)
+    spread = lax.dot_general(
+        kernel, dy, (((0,), (0,)), ((), ())), preferred_element_type=jnp.float32
+    )
+    put(spread_ref, unit * ROW, spread)
+    total = jnp.zeros((CG, PIX), jnp.float32)
+    for tap in range(TAPS):
+        part = strided(spread_ref, unit * ROW + tap, CG, TAPS)
+        total += moved(part, 1 - tap // 3, 1 - tap % 3, masks)
+    return total.astype(jnp.bfloat16)
+
+
+def adjoint_kernel(owned, routes_ref, logits_ref, grads_ref, dy_all_ref, *rest):
+    pair_refs, rest = rest[:-9], rest[-9:]
+    (
+        out_ref, own_dots_ref, own_mixed_ref,
+        kernels_ref, flat_ref, mixed_ref, spread_ref, dots_ref, place_sem,
+    ) = rest
     samples, top_count, patches = routes_ref.shape
     tiles, groups, _ = kernels_ref.shape
     channels = groups * CG
     per_tile = patches // tiles
     together = min(ROWS // groups, per_tile)
     rows_count = together * groups
-    blocks = samples * per_tile // together
+    per_sample = per_tile // together
     tile = lax.axis_index("grid")
     mine = lax.axis_index("batch")
     places = [
@@ -250,7 +245,7 @@
     for copy in copies:
         copy.wait()
 
-    def work(block, carry):
+    def mix(block, target_ref):
         for place in range(together):
             patch = block * together + place
             sample = lax.div(patch, per_tile)
@@ -278,31 +273,32 @@
                 start = quad * QUAD + 2 * j * 128
                 line = rolled(flat_ref[:, start:start + WIDE], -32 * j)
                 for m in range(WIDE // 128):
-                    mixed_ref[m, pl.ds(quad * 4 + j, rows_count, stride=CG), :] = line[
+                    target_ref[m, pl.ds(quad * 4 + j, rows_count, stride=CG), :] = line[
                         :, m * 128:(m + 1) * 128
                     ]
+
+    def work(number, carry):
+        step = 1 + lax.div(number, per_sample)
+        within = lax.rem(number, per_sample)
+        block = lax.rem(mine + step, samples) * per_sample + within
+        mix(block, mixed_ref)
         for unit in range(rows_count):
-            patch = block * together + unit // groups
+            place = unit // groups
             rows = slice((unit % groups) * CG, (unit % groups + 1) * CG)
-            kernel = joined(mixed_ref, unit * CG, CG)[:, :ROW].astype(jnp.bfloat16)
-            spread = lax.dot_general(
-                kernel,
-                dy_all_ref[patch, rows, :],
-                (((0,), (0,)), ((), ())),
-                preferred_element_type=jnp.float32,
+            dy = dy_all_ref[block * together + place, rows, :]
+            offset = pl.multiple_of((within * together + place) * PIX, PIX)
+            out_ref[step - 1, rows, pl.ds(offset, PIX)] = adjoint_unit(
+                mixed_ref, spread_ref, unit, dy, masks
             )
-            put(spread_ref, unit * ROW, spread)
-            total = jnp.zeros((CG, PIX), jnp.float32)
-            for tap in range(TAPS):
-                part = strided(spread_ref, unit * ROW + tap, CG, TAPS)
-                total += moved(part, 1 - tap // 3, 1 - tap % 3, masks)
-            step = lax.rem(lax.div(patch, per_tile) - mine + samples, samples)
-            offset = pl.multiple_of(lax.rem(patch, per_tile) * PIX, PIX)
-            out_ref[step, rows, pl.ds(offset, PIX)] = total.astype(jnp.bfloat16)
         return carry
 
-    lax.fori_loop(0, blocks, work, 0)
-    count = blocks * top_count * rows_count
+    def own(within, carry):
+        mix(mine * per_sample + within, own_mixed_ref.at[within])
+        return carry
+
+    lax.fori_loop(0, (samples - 1) * per_sample, work, 0)
+    lax.fori_loop(0, per_sample, own, 0)
+    count = samples * per_sample * top_count * rows_count
     sums = lax.dot_general(
         jnp.ones((DOT_ROWS, 128), jnp.float32),
         dots_ref[...],
@@ -322,23 +318,57 @@
         precision=lax.Precision.HIGHEST,
         preferred_element_type=jnp.float32,
     ).astype(jnp.bfloat16)
-    for step in range(samples):
-        out_ref[step, channels:channels + DOT_ROWS, :128] = route_dots
-
-
-def sum_kernel(local_ref, logit_ref, got_ref, out_ref):
+    own_dots_ref[...] = route_dots
+    for step in range(1, samples):
+        out_ref[step - 1, channels:channels + DOT_ROWS, :128] = route_dots
+
+
+def own_adjoint_kernel(mixed_ref, dy_all_ref, out_ref, spread_ref):
+    per_sample, _, mixed_rows, _ = mixed_ref.shape
+    rows_count = mixed_rows // CG
+    channels, span = out_ref.shape
+    groups = channels // CG
+    together = rows_count // groups
+    mine = lax.axis_index("batch")
+    masks = pixel_masks(CG)
+
+    def work(within, carry):
+        for unit in range(rows_count):
+            place = within * together + unit // groups
+            rows = slice((unit % groups) * CG, (unit % groups + 1) * CG)
+            dy = dy_all_ref[mine * (span // PIX) + place, rows, :]
+            out_ref[rows, pl.ds(pl.multiple_of(place * PIX, PIX), PIX)] = adjoint_unit(
+                mixed_ref.at[within], spread_ref, unit, dy, masks
+            )
+        return carry
+
+    lax.fori_loop(0, per_sample, work, 0)
+
+
+def sum_kernel(local_ref, gate_ref, got_ref, out_hbm, total_ref, sem):
     tiles, groups, width = got_ref.shape
-    out_ref[...] = jnp.zeros(out_ref.shape, jnp.float32)
-
-    def add(tile, carry):
-        local = local_ref[tile]
-        gate = jax.nn.sigmoid(jnp.full((groups, 128), logit_ref[tile], jnp.float32)) / SIDE
-        for at in range(0, width, 128):
-            lanes = slice(at, at + 128)
-            out_ref[local, :, lanes] += gate * got_ref[tile, :, lanes].astype(jnp.float32)
-        return carry
-
-    lax.fori_loop(0, tiles, add, 0)
+    chunk = width // SUM_CHUNKS
+    copies = []
+    for part in range(SUM_CHUNKS):
+        span = slice(part * chunk, (part + 1) * chunk)
+        total_ref[:, :, span] = jnp.zeros(total_ref.shape[:2] + (chunk,), jnp.float32)
+
+        def add(quad, carry):
+            for tile in (quad * 4 + i for i in range(4)):
+                local = local_ref[tile]
+                gate = gate_ref[tile]
+                for at in range(part * chunk, (part + 1) * chunk, 128):
+                    lanes = slice(at, at + 128)
+                    total_ref[local, :, lanes] += gate * got_ref[tile, :, lanes].astype(jnp.float32)
+            return carry
+
+        lax.fori_loop(0, tiles // 4, add, 0)
+        copies.append(
+            pltpu.make_async_copy(total_ref.at[:, :, span], out_hbm.at[:, :, span], sem.at[part])
+        )
+        copies[-1].start()
+    for copy in copies:
+        copy.wait()
 
 
 def per_device(inputs, cotangent, weights, gate_logits, routes):
@@ -357,7 +387,7 @@
     params = pltpu.CompilerParams(vmem_limit_bytes=VMEM_LIMIT)
     routes_t = routes.transpose(0, 2, 1)
     logits_t = gate_logits.transpose(0, 2, 1)
-    assert tiles & (tiles - 1) == 0 and tiles > 1
+    assert tiles & (tiles - 1) == 0 and tiles >= 4
     together = min(ROWS // groups, per_tile)
     rows = together * groups
 
@@ -368,44 +398,31 @@
         return lax.ppermute(blocks, "grid", [(i, i ^ step) for i in range(tiles)])
 
     weights_beside = swap(weights, 1)
-    table = jax.ShapeDtypeStruct((tiles,), jnp.int32)
-    to_send, local, logit, beside = pl.pallas_call(
-        functools.partial(scan_kernel, owned),
-        out_shape=(
-            jax.ShapeDtypeStruct((batch - 1, 2, channels, span), jnp.bfloat16),
-            table,
-            jax.ShapeDtypeStruct((tiles,), jnp.float32),
-            table,
-        ),
-        in_specs=[hbm] * 4,
-        out_specs=(hbm, smem, smem, smem),
+    pair_count = tiles // 2
+    table = jax.ShapeDtypeStruct((pair_count,), jnp.int32)
+    own_ids, beside_ids = pl.pallas_call(
+        functools.partial(scan_kernel, owned, per_tile),
+        out_shape=(table, table),
+        in_specs=[smem],
+        out_specs=(smem, smem),
+        compiler_params=params,
+        cost_estimate=pl.CostEstimate(flops=COST, bytes_accessed=1, transcendentals=0),
+        name="scan",
+    )(routes_t)
+
+    to_send, *pairs = pl.pallas_call(
+        pack_kernel,
+        out_shape=(jax.ShapeDtypeStruct((batch - 1, 2, channels, span), jnp.bfloat16),)
+        + (blocks_shape(2),) * pair_count,
+        in_specs=[smem, smem] + [vmem] * 4,
+        out_specs=(hbm,) * (1 + pair_count),
         scratch_shapes=[
-            pltpu.SMEM(routes_t.shape, jnp.int32),
-            pltpu.SMEM(routes_t.shape, jnp.float32),
-            pltpu.VMEM((batch - 1, 2, channels, span), jnp.bfloat16),
-            pltpu.SemaphoreType.DMA((2,)),
-            pltpu.SemaphoreType.DMA((batch - 1, 2)),
+            pltpu.SemaphoreType.DMA((pair_count, 2)),
             pltpu.SemaphoreType.DMA((batch - 1, 2)),
         ],
-        compiler_params=pltpu.CompilerParams(vmem_limit_bytes=WHOLE_VMEM),
-        cost_estimate=pl.CostEstimate(flops=COST, bytes_accessed=1, transcendentals=0),
-        name="scan",
-    )(routes_t, logits_t, inputs, cotangent)
-
-    pairs = pl.pallas_call(
-        pack_kernel,
-        out_shape=(blocks_shape(2),) * (tiles // 2),
-        in_specs=[smem, smem, hbm, hbm],
-        out_specs=(hbm,) * (tiles // 2),
-        scratch_shapes=[
-            pltpu.VMEM(weights.shape, jnp.bfloat16),
-            pltpu.VMEM(weights.shape, jnp.bfloat16),
-            pltpu.SemaphoreType.DMA((2,)),
-            pltpu.SemaphoreType.DMA((tiles // 2, 2)),
-        ],
-        compiler_params=pltpu.CompilerParams(vmem_limit_bytes=WHOLE_VMEM),
+        compiler_params=params,
         name="pack",
-    )(local, beside, weights, weights_beside)
+    )(own_ids, beside_ids, weights, weights_beside, inputs, cotangent)
     pairs = [
         blocks if pair == 0 else swap(blocks, 2 * pair)
         for pair, blocks in zip(pair_order(tiles), pairs)
@@ -443,11 +460,16 @@
 
     grads_back = lax.all_to_all(wire, "grid", split_axis=0, concat_axis=0, tiled=True)
 
-    parts = pl.pallas_call(
+    per_sample = per_tile // together
+    parts, own_dots, own_mixed = pl.pallas_call(
         functools.partial(adjoint_kernel, owned),
-        out_shape=jax.ShapeDtypeStruct((batch, channels + DOT_ROWS, span), jnp.bfloat16),
+        out_shape=(
+            jax.ShapeDtypeStruct((batch - 1, channels + DOT_ROWS, span), jnp.bfloat16),
+            jax.ShapeDtypeStruct((DOT_ROWS, 128), jnp.bfloat16),
+            jax.ShapeDtypeStruct((per_sample, WIDE // 128, rows * CG, 128), jnp.float32),
+        ),
         in_specs=[smem, smem, vmem, vmem] + [anywhere] * (tiles // 2),
-        out_specs=vmem,
+        out_specs=(vmem, vmem, vmem),
         scratch_shapes=[
             pltpu.VMEM((tiles, groups, width), jnp.bfloat16),
             pltpu.VMEM((rows, width), jnp.float32),
@@ -461,16 +483,41 @@
         name="adjoint",
     )(routes_t, logits_t, grads, dy_all, *pairs)
 
-    arrived = exchange([parts[step] for step in range(1, batch)])
+    own_part = pl.pallas_call(
+        own_adjoint_kernel,
+        out_shape=jax.ShapeDtypeStruct((channels, span), jnp.bfloat16),
+        in_specs=[vmem, vmem],
+        out_specs=vmem,
+        scratch_shapes=[pltpu.VMEM((PIX // 128, rows * ROW, 128), jnp.float32)],
+        compiler_params=params,
+        cost_estimate=pl.CostEstimate(flops=COST // 20, bytes_accessed=1, transcendentals=0),
+        name="own_adjoint",
+    )(own_mixed, dy_all)
+
+    late_routes, late_logits, _ = lax.optimization_barrier((routes_t, logits_t, own_dots))
+    local, gate_table = pl.pallas_call(
+        functools.partial(tables_kernel, owned, per_tile),
+        out_shape=(
+            jax.ShapeDtypeStruct((tiles,), jnp.int32),
+            jax.ShapeDtypeStruct((tiles, groups, 128), jnp.float32),
+        ),
+        in_specs=[smem, smem],
+        out_specs=(smem, vmem),
+        compiler_params=params,
+        name="tables",
+    )(late_routes, late_logits)
+
+    arrived = exchange([parts[step] for step in range(batch - 1)])
     mine = lax.axis_index("batch")
     d_inputs = jnp.zeros(inputs.shape, jnp.bfloat16)
-    dots = jnp.zeros((128,), jnp.float32)
-    for step, part in enumerate([parts[0]] + arrived):
+    dots = own_dots[0].astype(jnp.float32)
+    for step, part in enumerate([own_part] + arrived):
         block = lax.rem(mine - step + batch, batch)
         d_inputs = lax.dynamic_update_slice(
             d_inputs, part[None, :channels], (0, block * channels, 0)
         )
-        dots += part[channels, :128].astype(jnp.float32)
+        if step:
+            dots += part[channels, :128].astype(jnp.float32)
     dots = dots[:tiles].reshape(samples, per_tile, top_count)
     gates = jax.nn.sigmoid(
         lax.dynamic_slice_in_dim(gate_logits, lax.axis_index("grid") * per_tile, per_tile, 1)
@@ -480,11 +527,15 @@
     d_weights = pl.pallas_call(
         sum_kernel,
         out_shape=jax.ShapeDtypeStruct(weights.shape, jnp.float32),
-        in_specs=[smem, smem, vmem],
-        out_specs=vmem,
+        in_specs=[smem, vmem, vmem],
+        out_specs=hbm,
+        scratch_shapes=[
+            pltpu.VMEM(weights.shape, jnp.float32),
+            pltpu.SemaphoreType.DMA((SUM_CHUNKS,)),
+        ],
         compiler_params=params,
         name="weight_sum",
-    )(local, logit, grads_back)
+    )(local, gate_table, grads_back)
     return (d_inputs, d_weights, gate_grad)
 
 

time: 67.3 us -> 65.7 us (0.976)
  starting transfers between devices: 18.2 us -> 15.5 us
  local copies, waits for them, and re-layouts: 3.78 us -> 5.51 us
  waiting for transfers between devices: 23 us -> 21.8 us
    ppermute x2, waiting for transfers between devices: 10.4 us -> 6.47 us  [exchange(): lax.ppermute(blocks[step - 1], 'batch', [(i, (i + step) % batch) for i in...]
    ppermute x8, starting transfers between devices: 8.92 us -> 6.94 us  [swap(): return lax.ppermute(blocks, 'grid', [(i, i ^ step) for i in range(tiles)])]
    ppermute x8, waiting for transfers between devices: 3.06 us -> 5 us  [swap(): return lax.ppermute(blocks, 'grid', [(i, i ^ step) for i in range(tiles)])]
    unnamed x24, local copies, waits for them, and re-layouts: 3.46 us -> 5.23 us
    all_to_all x1, waiting for transfers between devices: 9.59 us -> 10.4 us  [per_device(): lax.all_to_all(wire, 'grid', split_axis=0, concat_axis=0, tiled=True)]
    pallas_call x3 -> x5, Pallas kernels: 14 us -> 14.7 us  [the longest x1 6.77 us: per_device(): pl.pallas_call(functools.partial(adjoint_kernel, owned), out_shape=(jax.S...]
  transfers between devices with their start and end apart: 11 -> 11, of which waited for: 4 -> 5; matrix products, arithmetic and copies ran while one was open for 2% -> 2% of each run, Pallas kernels for 28% -> 26%
where the time goes in v3:
time: 65.7 us; the launch traced here: 65.3 us
  waiting for transfers between devices  21.8 us (33%)
  Pallas kernels  21.6 us (33%)
  starting transfers between devices  15.5 us (24%)
  local copies, waits for them, and re-layouts  5.51 us (8%)
  between operations  0.8 us (1%)
    all_to_all x1, waiting for transfers between devices, per_device(): lax.all_to_all(wire, 'grid', split_axis=0, concat_axis=0, tiled=True)  10.4 us
    all_to_all x1, starting transfers between devices, per_device(): lax.all_to_all(wire, 'grid', split_axis=0, concat_axis=0, tiled=True)  7.06 us
    ppermute x8, starting transfers between devices, swap(): return lax.ppermute(blocks, 'grid', [(i, i ^ step) for i in range(tiles)])  6.94 us
    pallas_call x1, Pallas kernels, per_device(): pl.pallas_call(functools.partial(adjoint_kernel, owned), out_shape=(jax.S...  6.77 us
    ppermute x2, waiting for transfers between devices, exchange(): lax.ppermute(blocks[step - 1], 'batch', [(i, (i + step) % batch) for i in...  6.47 us
    unnamed x24, local copies, waits for them, and re-layouts  5.23 us
    ppermute x8, waiting for transfers between devices, swap(): return lax.ppermute(blocks, 'grid', [(i, i ^ step) for i in range(tiles)])  5 us
    pallas_call x1, Pallas kernels, per_device(): pl.pallas_call(functools.partial(grads_kernel, owned), out_shape=(blocks_...  4.84 us
  transfers between devices with their start and end apart: 11, of which 5 were waited for; matrix products, arithmetic and copies ran while one was open for 2% of the time, Pallas kernels for 26%

profile of v3, /device:TPU:13, one launch (start us, length us, event | category | flops | bytes accessed | tf_op | source)
XLA Modules:
  0.0 65.3 jit_solution(2048470192107096517)
XLA Ops:
  0.6 0.7 %collective-permute-start = (bf16[8,4,9216]{2,1,0:T(4,128)(2,1)}, bf16[8,4,9216]{2,1,0:T(4,128)(2,1)S(1)}, u32[]{:S(2)}, u32[]{:S(2)}) collective-permute-start(bf16[8,4,9216]{2,1,0:T(4,128)(2,1)} %own_ref.1), channel_id=1, source_target_pairs={{0,2},{2,0},{4,6},{6,4},{8,10},{10,8},{12,14},{14,12},{16,18},{18,... | collective-permute-start | bytes 1769480 | tf_op jit(solution)/shard_map/ppermute | solution.py:398
  1.4 0.7 %copy-done.4 = s32[2,64,2]{1,2,0:T(2,128)S(1)} copy-done((s32[2,64,2]{1,2,0:T(2,128)S(1)}, s32[2,64,2]{1,2,0:T(2,128)}, u32[]{:S(2)}) %copy-start.4) | copy-done | bytes 1048
  2.1 1.8 %scan.1 = (s32[8]{0:T(128)S(1)}, s32[8]{0:T(128)S(1)}) custom-call(s32[2,2,64]{2,1,0:T(2,128)S(1)} %bitcast.13), custom_call_target="tpu_custom_call" | custom-call | flops 20000000000 | bytes 1 | tf_op jit(solution)/shard_map/scan/pallas_call | solution.py:403
  3.9 0.0 copy-start.3
  3.9 0.0 copy-start.5
  3.9 0.0 collective-permute-done.next_ref
  3.9 0.0 copy-done
  3.9 0.0 copy-done.1
  3.9 0.0 copy-done.2
  4.0 2.3 %pack.1 = (bf16[1,2,128,1024]{3,2,1,0:T(8,128)(2,1)S(1)}, bf16[2,4,9216]{2,1,0:T(4,128)(2,1)}, bf16[2,4,9216]{2,1,0:T(4,128)(2,1)S(1)}, bf16[2,4,9216]{2,1,0:T(4...) custom-call(s32[8]{0:T(128)S(1)} %get-tuple-element.24.local_ref, ...), custom_call_target="tpu_custom_call" | custom-call | tf_op jit(solution)/shard_map/pack/pallas_call | solution.py:413
  6.3 1.3 %collective-permute-start.1 = (bf16[2,128,1024]{2,1,0:T(8,128)(2,1)S(1)}, bf16[2,128,1024]{2,1,0:T(8,128)(2,1)S(1)}, u32[]{:S(2)}, u32[]{:S(2)}) collective-permute-start(bf16[2,128,1024]{2,1,0:T(8,128)(2,1)S(1)} %bitcast.17), channel_id=1, source_target_pairs={{0,1},{1,0},{2,3},{3,2},{4,5},{5,4},{6,7},{7,6},{8,9},{9,8},{10,11... | collective-permute-start | bytes 1572872 | tf_op jit(solution)/shard_map/ppermute | solution.py:433
  7.5 0.2 collective-permute-start.2
  7.8 0.2 collective-permute-start.3
  7.9 0.0 copy-done.3
  7.9 0.1 constant_dynamic-slice_fusion
  8.0 0.1 copy.12
  8.1 2.3 %collective-permute-start.4 = (bf16[2,4,9216]{2,1,0:T(4,128)(2,1)S(1)}, bf16[2,4,9216]{2,1,0:T(4,128)(2,1)}, u32[]{:S(2)}, u32[]{:S(2)}) collective-permute-start(bf16[2,4,9216]{2,1,0:T(4,128)(2,1)S(1)} %get-tuple-element.31), channel_id=1, source_target_pairs={{0,16},{2,18},{4,20},{6,22},{8,24},{10,26},{12,28},{14,30},{16,0},... | collective-permute-start | bytes 442376 | tf_op jit(solution)/shard_map/ppermute | solution.py:398
  10.4 1.0 %collective-permute-start.5 = (bf16[2,4,9216]{2,1,0:T(4,128)(2,1)S(1)}, bf16[2,4,9216]{2,1,0:T(4,128)(2,1)}, u32[]{:S(2)}, u32[]{:S(2)}) collective-permute-start(bf16[2,4,9216]{2,1,0:T(4,128)(2,1)S(1)} %get-tuple-element.32), channel_id=1, source_target_pairs={{0,20},{2,22},{4,16},{6,18},{8,28},{10,30},{12,24},{14,26},{16,4},... | collective-permute-start | bytes 442376 | tf_op jit(solution)/shard_map/ppermute | solution.py:398
  11.5 1.5 %collective-permute-done.2.rest_0_ = bf16[2,4,9216]{2,1,0:T(4,128)(2,1)S(1)} collective-permute-done((bf16[2,4,9216]{2,1,0:T(4,128)(2,1)}, bf16[2,4,9216]{2,1,0:T(4,128)(2,1)S(1)}, u32[]{:S(2)}, u32[]{:S(2)}) %collective-permute-start.2) | collective-permute-done | bytes 147488 | tf_op jit(solution)/shard_map/ppermute | solution.py:398
  12.9 1.3 %collective-permute-start.6 = (bf16[2,4,9216]{2,1,0:T(4,128)(2,1)S(1)}, bf16[2,4,9216]{2,1,0:T(4,128)(2,1)}, u32[]{:S(2)}, u32[]{:S(2)}) collective-permute-start(bf16[2,4,9216]{2,1,0:T(4,128)(2,1)S(1)} %get-tuple-element.33), channel_id=1, source_target_pairs={{0,24},{2,26},{4,28},{6,30},{8,16},{10,18},{12,20},{14,22},{16,8},... | collective-permute-start | bytes 442376 | tf_op jit(solution)/shard_map/ppermute | solution.py:398
  14.2 0.0 collective-permute-done.3.rest_1_
  14.2 1.1 %collective-permute-start.7 = (bf16[2,4,9216]{2,1,0:T(4,128)(2,1)S(1)}, bf16[2,4,9216]{2,1,0:T(4,128)(2,1)}, u32[]{:S(2)}, u32[]{:S(2)}) collective-permute-start(bf16[2,4,9216]{2,1,0:T(4,128)(2,1)S(1)} %get-tuple-element.34), channel_id=1, source_target_pairs={{0,28},{2,30},{4,24},{6,26},{8,20},{10,22},{12,16},{14,18},{16,12}... | collective-permute-start | bytes 442376 | tf_op jit(solution)/shard_map/ppermute | solution.py:398
  15.3 4.7 %collective-permute-done.1 = bf16[2,128,1024]{2,1,0:T(8,128)(2,1)S(1)} collective-permute-done((bf16[2,128,1024]{2,1,0:T(8,128)(2,1)S(1)}, bf16[2,128,1024]{2,1,0:T(8,128)(2,1)S(1)}, u32[]{:S(2)}, u32[]{:S(2)}) %collective-permute-start.1) | collective-permute-done | bytes 524320 | tf_op jit(solution)/shard_map/ppermute | solution.py:433
  20.0 0.1 collective-permute-start.8
  20.1 0.0 copy-done.5
  20.1 4.8 %kernel_grads.1 = (bf16[16,4,9216]{2,1,0:T(4,128)(2,1)}, bf16[8,4,9216]{2,1,0:T(4,128)(2,1)S(1)}, bf16[8,128,256]{2,1,0:T(8,128)(2,1)S(1)}) custom-call(s32[2,2,64]{2,1,0:T(2,128)S(1)} %bitcast.14, bf16[1,256,1024]{2,1,0:T(8,128)(2,1)S(1)} %copy-done.1, bf16[1,256,1024]{2,1,0:T(8,128)(2,1)S(1)} %copy-done.2, bf16[1,2,128,1024]{3,2,1,0:T(8,128)(2,1)S(1)} %bitcast.18), custom_call_target="tpu_custom_call" | custom-call | flops 20000000000 | bytes 1 | tf_op jit(solution)/shard_map/kernel_grads/pallas_call | solution.py:442
  24.9 0.8 %copy-done.6 = bf16[8,128,256]{2,1,0:T(8,128)(2,1)} copy-done((bf16[8,128,256]{2,1,0:T(8,128)(2,1)}, bf16[8,128,256]{2,1,0:T(8,128)(2,1)S(1)}, u32[]{:S(2)}) %copy-start.6) | copy-done | bytes 524312
  25.7 0.8 %copy-done.8 = bf16[8,4,9216]{2,1,0:T(4,128)(2,1)} copy-done((bf16[8,4,9216]{2,1,0:T(4,128)(2,1)}, bf16[8,4,9216]{2,1,0:T(4,128)(2,1)S(1)}, u32[]{:S(2)}) %copy-start.8) | copy-done | bytes 589848
  26.5 7.1 %all-to-all-start = ((bf16[16,4,9216]{2,1,0:T(4,128)(2,1)}), bf16[16,4,9216]{2,1,0:T(4,128)(2,1)S(1)}, u32[]{:S(2)}, u32[]{:S(2)}) async-start(bf16[16,4,9216]{2,1,0:T(4,128)(2,1)} %get-tuple-element.44), calls=%async_computation | async-start | bytes 2359296 | tf_op jit(solution)/shard_map/all_to_all | solution.py:461
  33.6 0.0 collective-permute-done.4.rest_2_
  33.6 0.0 collective-permute-done.5.rest_3_
  33.6 0.0 collective-permute-done.6.rest_4_
  33.6 3.5 %collective-permute-done.7.rest_5_ = bf16[2,4,9216]{2,1,0:T(4,128)(2,1)} collective-permute-done((bf16[2,4,9216]{2,1,0:T(4,128)(2,1)S(1)}, bf16[2,4,9216]{2,1,0:T(4,128)(2,1)}, u32[]{:S(2)}, u32[]{:S(2)}) %collective-permute-start.7) | collective-permute-done | bytes 147488 | tf_op jit(solution)/shard_map/ppermute | solution.py:398
  37.1 0.0 collective-permute-done.8.rest_6_
  37.2 1.0 %copy-done.7 = bf16[8,128,256]{2,1,0:T(8,128)(2,1)S(1)} copy-done((bf16[8,128,256]{2,1,0:T(8,128)(2,1)S(1)}, bf16[8,128,256]{2,1,0:T(8,128)(2,1)}, u32[]{:S(2)}) %copy-start.7) | copy-done | bytes 524312
  38.2 1.1 %copy-done.9 = bf16[8,4,9216]{2,1,0:T(4,128)(2,1)S(1)} copy-done((bf16[8,4,9216]{2,1,0:T(4,128)(2,1)S(1)}, bf16[8,4,9216]{2,1,0:T(4,128)(2,1)}, u32[]{:S(2)}) %copy-start.9) | copy-done | bytes 589848
  39.3 6.8 %adjoint.1 = (bf16[1,144,1024]{2,1,0:T(8,128)(2,1)S(1)}, bf16[16,128]{1,0:T(8,128)(2,1)S(1)}, f32[2,3,256,128]{3,2,1,0:T(8,128)S(1)}) custom-call(s32[2,2,64]{2,1,0:T(2,128)S(1)} %bitcast.15, f32[2,2,64]{2,1,0:T(2,128)S(1)} %bitcast.11, bf16[8,4,9216]{2,1,0:T(4,128)(2,1)S(1)} %copy-done.9, bf16[8,128,256]{2,1,0:T(8,128)(2,1)S(1)} %copy-done.7, ...), custom_call_target="tpu_custom_call" | custom-call | flops 20000000000 | bytes 1 | tf_op jit(solution)/shard_map/adjoint/pallas_call | solution.py:464
  46.0 0.2 collective-permute-start.9
  46.3 2.0 %tables.1 = (s32[16]{0:T(128)S(1)}, f32[16,4,128]{2,1,0:T(4,128)S(1)}) custom-call(s32[2,2,64]{2,1,0:T(2,128)S(1)} %bitcast.16, f32[2,2,64]{2,1,0:T(2,128)S(1)} %bitcast.12), custom_call_target="tpu_custom_call" | custom-call | tf_op jit(solution)/shard_map/tables/pallas_call | solution.py:498
  48.3 1.7 %own_adjoint.1 = bf16[128,1024]{1,0:T(8,128)(2,1)S(1)} custom-call(f32[2,3,256,128]{3,2,1,0:T(8,128)S(1)} %get-tuple-element.37.mixed_ref, bf16[8,128,256]{2,1,0:T(8,128)(2,1)S(1)} %copy-done.7), custom_call_target="tpu_custom_call" | custom-call | flops 1000000000 | bytes 1 | tf_op jit(solution)/shard_map/own_adjoint/pallas_call | solution.py:486
  50.1 0.1 broadcast_in_dim.9
  50.2 1.8 %collective-permute-done.9 = bf16[144,1024]{1,0:T(8,128)(2,1)S(1)} collective-permute-done((bf16[144,1024]{1,0:T(8,128)(2,1)S(1)}, bf16[144,1024]{1,0:T(8,128)(2,1)S(1)}, u32[]{:S(2)}, u32[]{:S(2)}) %collective-permute-start.9) | collective-permute-done | bytes 294944 | tf_op jit(solution)/shard_map/ppermute | solution.py:433
  52.0 0.1 slice.20
  52.1 0.7 %copy.11 = f32[2,4,2]{1,2,0:T(2,128)} copy(f32[2,4,2]{2,1,0:T(4,128)S(1)} %fusion.2) | data formatting | bytes 128
  52.8 0.0 copy-start.10
  52.8 10.4 %all-to-all-done.got_ref = bf16[16,4,9216]{2,1,0:T(4,128)(2,1)S(1)} async-done(((bf16[16,4,9216]{2,1,0:T(4,128)(2,1)}), bf16[16,4,9216]{2,1,0:T(4,128)(2,1)S(1)}, u32[]{:S(2)}, u32[]{:S(2)}) %all-to-all-start) | async-done | bytes 1179680 | tf_op jit(solution)/shard_map/all_to_all | solution.py:461
  63.2 2.1 %weight_sum.1 = f32[8,4,9216]{2,1,0:T(4,128)} custom-call(s32[16]{0:T(128)S(1)} %get-tuple-element.42.local_ref, f32[16,4,128]{2,1,0:T(4,128)S(1)} %get-tuple-element.43.gate_ref, bf16[16,4,9216]{2,1,0:T(4,128)(2,1)S(1)} %all-to-all-done.got_ref), custom_call_target="tpu_custom_call" | custom-call | tf_op jit(solution)/shard_map/weight_sum/pallas_call | solution.py:527
  65.3 0.0 copy-done.10
  (13 shorter events, 0.1 us)
Async XLA Ops:
  0.6 3.3 %collective-permute-start = (bf16[8,4,9216]{2,1,0:T(4,128)(2,1)}, bf16[8,4,9216]{2,1,0:T(4,128)(2,1)S(1)}, u32[]{:S(2)}, u32[]{:S(2)}) collective-permute-start(bf16[8,4,9216]{2,1,0:T(4,128)(2,1)} %own_ref.1), channel_id=1, source_target_pairs={{0,2},{2,0},{4,6},{6,4},{8,10},{10,8},{12,14},{14,12},{16,18},{18,... | collective-permute-start | bytes 1769480 | tf_op jit(solution)/shard_map/ppermute | solution.py:398
  1.4 0.7 %copy-start.4 = (s32[2,64,2]{1,2,0:T(2,128)S(1)}, s32[2,64,2]{1,2,0:T(2,128)}, u32[]{:S(2)}) copy-start(s32[2,64,2]{1,2,0:T(2,128)} %param.9) | copy-start | bytes 3076
  2.1 1.9 %copy-start = (bf16[8,4,9216]{2,1,0:T(4,128)(2,1)S(1)}, bf16[8,4,9216]{2,1,0:T(4,128)(2,1)}, u32[]{:S(2)}) copy-start(bf16[8,4,9216]{2,1,0:T(4,128)(2,1)} %own_ref.1) | copy-start | bytes 1769476
  2.1 1.9 %copy-start.1 = (bf16[1,256,1024]{2,1,0:T(8,128)(2,1)S(1)}, bf16[1,256,1024]{2,1,0:T(8,128)(2,1)}, u32[]{:S(2)}) copy-start(bf16[1,256,1024]{2,1,0:T(8,128)(2,1)} %x_ref.3) | copy-start | bytes 1572868
  2.1 1.9 %copy-start.2 = (bf16[1,256,1024]{2,1,0:T(8,128)(2,1)S(1)}, bf16[1,256,1024]{2,1,0:T(8,128)(2,1)}, u32[]{:S(2)}) copy-start(bf16[1,256,1024]{2,1,0:T(8,128)(2,1)} %dy_ref.3) | copy-start | bytes 1572868
  3.9 4.1 %copy-start.3 = (f32[2,64,2]{1,2,0:T(2,128)S(1)}, f32[2,64,2]{1,2,0:T(2,128)}, u32[]{:S(2)}) copy-start(f32[2,64,2]{1,2,0:T(2,128)} %param.8) | copy-start | bytes 3076
  3.9 16.2 %copy-start.5 = (s32[2,64,2]{1,2,0:T(2,128)S(1)}, s32[2,64,2]{1,2,0:T(2,128)}, u32[]{:S(2)}) copy-start(s32[2,64,2]{1,2,0:T(2,128)} %param.9) | copy-start | bytes 3076
  6.3 13.7 %collective-permute-start.1 = (bf16[2,128,1024]{2,1,0:T(8,128)(2,1)S(1)}, bf16[2,128,1024]{2,1,0:T(8,128)(2,1)S(1)}, u32[]{:S(2)}, u32[]{:S(2)}) collective-permute-start(bf16[2,128,1024]{2,1,0:T(8,128)(2,1)S(1)} %bitcast.17), channel_id=1, source_target_pairs={{0,1},{1,0},{2,3},{3,2},{4,5},{5,4},{6,7},{7,6},{8,9},{9,8},{10,11... | collective-permute-start | bytes 1572872 | tf_op jit(solution)/shard_map/ppermute | solution.py:433
  7.5 5.4 %collective-permute-start.2 = (bf16[2,4,9216]{2,1,0:T(4,128)(2,1)}, bf16[2,4,9216]{2,1,0:T(4,128)(2,1)S(1)}, u32[]{:S(2)}, u32[]{:S(2)}) collective-permute-start(bf16[2,4,9216]{2,1,0:T(4,128)(2,1)} %get-tuple-element.29), channel_id=1, source_target_pairs={{0,4},{2,6},{4,0},{6,2},{8,12},{10,14},{12,8},{14,10},{16,20},{18,... | collective-permute-start | bytes 442376 | tf_op jit(solution)/shard_map/ppermute | solution.py:398
  7.8 6.4 %collective-permute-start.3 = (bf16[2,4,9216]{2,1,0:T(4,128)(2,1)S(1)}, bf16[2,4,9216]{2,1,0:T(4,128)(2,1)S(1)}, u32[]{:S(2)}, u32[]{:S(2)}) collective-permute-start(bf16[2,4,9216]{2,1,0:T(4,128)(2,1)S(1)} %get-tuple-element.30), channel_id=1, source_target_pairs={{0,8},{2,10},{4,12},{6,14},{8,0},{10,2},{12,4},{14,6},{16,24},{18,... | collective-permute-start | bytes 442376 | tf_op jit(solution)/shard_map/ppermute | solution.py:398
  8.1 25.5 %collective-permute-start.4 = (bf16[2,4,9216]{2,1,0:T(4,128)(2,1)S(1)}, bf16[2,4,9216]{2,1,0:T(4,128)(2,1)}, u32[]{:S(2)}, u32[]{:S(2)}) collective-permute-start(bf16[2,4,9216]{2,1,0:T(4,128)(2,1)S(1)} %get-tuple-element.31), channel_id=1, source_target_pairs={{0,16},{2,18},{4,20},{6,22},{8,24},{10,26},{12,28},{14,30},{16,0},... | collective-permute-start | bytes 442376 | tf_op jit(solution)/shard_map/ppermute | solution.py:398
  10.4 23.2 %collective-permute-start.5 = (bf16[2,4,9216]{2,1,0:T(4,128)(2,1)S(1)}, bf16[2,4,9216]{2,1,0:T(4,128)(2,1)}, u32[]{:S(2)}, u32[]{:S(2)}) collective-permute-start(bf16[2,4,9216]{2,1,0:T(4,128)(2,1)S(1)} %get-tuple-element.32), channel_id=1, source_target_pairs={{0,20},{2,22},{4,16},{6,18},{8,28},{10,30},{12,24},{14,26},{16,4},... | collective-permute-start | bytes 442376 | tf_op jit(solution)/shard_map/ppermute | solution.py:398
  12.9 20.7 %collective-permute-start.6 = (bf16[2,4,9216]{2,1,0:T(4,128)(2,1)S(1)}, bf16[2,4,9216]{2,1,0:T(4,128)(2,1)}, u32[]{:S(2)}, u32[]{:S(2)}) collective-permute-start(bf16[2,4,9216]{2,1,0:T(4,128)(2,1)S(1)} %get-tuple-element.33), channel_id=1, source_target_pairs={{0,24},{2,26},{4,28},{6,30},{8,16},{10,18},{12,20},{14,22},{16,8},... | collective-permute-start | bytes 442376 | tf_op jit(solution)/shard_map/ppermute | solution.py:398
  14.2 22.9 %collective-permute-start.7 = (bf16[2,4,9216]{2,1,0:T(4,128)(2,1)S(1)}, bf16[2,4,9216]{2,1,0:T(4,128)(2,1)}, u32[]{:S(2)}, u32[]{:S(2)}) collective-permute-start(bf16[2,4,9216]{2,1,0:T(4,128)(2,1)S(1)} %get-tuple-element.34), channel_id=1, source_target_pairs={{0,28},{2,30},{4,24},{6,26},{8,20},{10,22},{12,16},{14,18},{16,12}... | collective-permute-start | bytes 442376 | tf_op jit(solution)/shard_map/ppermute | solution.py:398
  20.0 17.2 %collective-permute-start.8 = (bf16[2,4,9216]{2,1,0:T(4,128)(2,1)S(1)}, bf16[2,4,9216]{2,1,0:T(4,128)(2,1)S(1)}, u32[]{:S(2)}, u32[]{:S(2)}) collective-permute-start(bf16[2,4,9216]{2,1,0:T(4,128)(2,1)S(1)} %get-tuple-element.35), channel_id=1, source_target_pairs={{0,12},{2,14},{4,8},{6,10},{8,4},{10,6},{12,0},{14,2},{16,28},{18,... | collective-permute-start | bytes 442376 | tf_op jit(solution)/shard_map/ppermute | solution.py:398
  24.9 0.8 %copy-start.6 = (bf16[8,128,256]{2,1,0:T(8,128)(2,1)}, bf16[8,128,256]{2,1,0:T(8,128)(2,1)S(1)}, u32[]{:S(2)}) copy-start(bf16[8,128,256]{2,1,0:T(8,128)(2,1)S(1)} %get-tuple-element.28.dy_all_ref) | copy-start | bytes 1572868
  25.7 0.8 %copy-start.8 = (bf16[8,4,9216]{2,1,0:T(4,128)(2,1)}, bf16[8,4,9216]{2,1,0:T(4,128)(2,1)S(1)}, u32[]{:S(2)}) copy-start(bf16[8,4,9216]{2,1,0:T(4,128)(2,1)S(1)} %get-tuple-element.27.grads_ref) | copy-start | bytes 1769476
  26.5 36.7 %all-to-all-start = ((bf16[16,4,9216]{2,1,0:T(4,128)(2,1)}), bf16[16,4,9216]{2,1,0:T(4,128)(2,1)S(1)}, u32[]{:S(2)}, u32[]{:S(2)}) async-start(bf16[16,4,9216]{2,1,0:T(4,128)(2,1)} %get-tuple-element.44), calls=%async_computation | async-start | bytes 2359296 | tf_op jit(solution)/shard_map/all_to_all | solution.py:461
  37.2 1.0 %copy-start.7 = (bf16[8,128,256]{2,1,0:T(8,128)(2,1)S(1)}, bf16[8,128,256]{2,1,0:T(8,128)(2,1)}, u32[]{:S(2)}) copy-start(bf16[8,128,256]{2,1,0:T(8,128)(2,1)} %copy-done.6) | copy-start | bytes 1572868
  38.2 1.1 %copy-start.9 = (bf16[8,4,9216]{2,1,0:T(4,128)(2,1)S(1)}, bf16[8,4,9216]{2,1,0:T(4,128)(2,1)}, u32[]{:S(2)}) copy-start(bf16[8,4,9216]{2,1,0:T(4,128)(2,1)} %copy-done.8) | copy-start | bytes 1769476
  46.0 5.9 %collective-permute-start.9 = (bf16[144,1024]{1,0:T(8,128)(2,1)S(1)}, bf16[144,1024]{1,0:T(8,128)(2,1)S(1)}, u32[]{:S(2)}, u32[]{:S(2)}) collective-permute-start(bf16[144,1024]{1,0:T(8,128)(2,1)S(1)} %bitcast.19), channel_id=1, source_target_pairs={{0,1},{1,0},{2,3},{3,2},{4,5},{5,4},{6,7},{7,6},{8,9},{9,8},{10,11... | collective-permute-start | bytes 884744 | tf_op jit(solution)/shard_map/ppermute | solution.py:433
  52.8 12.5 %copy-start.10 = (bf16[1,256,1024]{2,1,0:T(8,128)(2,1)}, bf16[1,256,1024]{2,1,0:T(8,128)(2,1)S(1)}, u32[]{:S(2)}) copy-start(bf16[1,256,1024]{2,1,0:T(8,128)(2,1)S(1)} %fusion) | copy-start | bytes 1572868

commit v4 on v3

--- a/solution.py
+++ b/solution.py
@@ -17,6 +17,8 @@
 ROWS = 8
 DOT_ROWS = 16
 VMEM_LIMIT = 16 * 1024 * 1024
+WHOLE_VMEM = 60 * 1024 * 1024
+EARLY = 3
 SUM_CHUNKS = 3
 COST = 20_000_000_000
 
@@ -63,139 +65,160 @@
 
 def pair_order(tiles):
     near, far = list(range(tiles // 4)), list(range(tiles // 4, tiles // 2))
-    return near[1:3] + far + near[3:] + near[:1]
-
-
-def named(routes_ref, tile, per_tile, first, owned):
-    samples, top_count, _ = routes_ref.shape
-    for sample in range(samples):
-        for place in range(per_tile):
-            for rank in range(top_count):
-                at = (sample, rank, tile * per_tile + place)
-                inside = routes_ref[at] - first
-                yield at, inside, (inside >= 0) & (inside < owned)
-
-
-def scan_kernel(owned, per_tile, routes_ref, local_ref, beside_ref):
-    here = lax.axis_index("grid")
-
-    def scan(pair, carry):
-        tile = here ^ (2 * pair)
-        for owner, found_ref in ((here, local_ref), (here ^ 1, beside_ref)):
-            found = jnp.int32(0)
-            for _, inside, hit in named(routes_ref, tile, per_tile, owner * owned, owned):
-                found += jnp.where(hit, inside, 0)
-            found_ref[pair] = found
-        return carry
-
-    lax.fori_loop(0, local_ref.shape[0], scan, 0)
-
-
-def pack_kernel(local_ref, beside_ref, own_ref, next_ref, x_ref, dy_ref, send_ref, *rest):
-    pair_refs, (pair_sem, send_sem) = rest[:-2], rest[-2:]
+    first = far.pop(len(far) // 2)
+    return near[1:2] + [first] + near[2:] + far + near[:1]
+
+
+def tree_sum(values):
+    while len(values) > 1:
+        values = [sum(values[at:at + 2]) for at in range(0, len(values), 2)]
+    return values[0]
+
+
+def stage_kernel(x_hbm, dy_hbm, send_ref, halves_ref, halves_sem, send_sem):
     others, _, channels, _ = send_ref.shape
     mine = lax.axis_index("batch")
-    copies = [
-        pltpu.make_async_copy(
-            source.at[ids[pair]], target.at[which], pair_sem.at[pair, which]
-        )
-        for pair, target in zip(pair_order(2 * len(pair_refs)), pair_refs)
-        for which, (ids, source) in enumerate(((local_ref, own_ref), (beside_ref, next_ref)))
-    ]
+    taken, sent = [], []
     for step in range(1, others + 1):
         block = lax.rem(mine + step, others + 1)
         rows = pl.ds(pl.multiple_of(block * channels, channels), channels)
-        for which, source in enumerate((x_ref, dy_ref)):
+        for which, source in enumerate((x_hbm, dy_hbm)):
             at = (step - 1, which)
+            taken.append(
+                pltpu.make_async_copy(source.at[0, rows], halves_ref.at[at], halves_sem.at[at])
+            )
+            sent.append(
+                pltpu.make_async_copy(halves_ref.at[at], send_ref.at[at], send_sem.at[at])
+            )
+    for copy in taken:
+        copy.start()
+    for copy, then in zip(taken, sent):
+        copy.wait()
+        then.start()
+    for copy in sent:
+        copy.wait()
+
+
+def pack_kernel(owned, per_tile, pairs, routes_ref, own_ref, beside_ref, *rest):
+    pair_refs, sem = rest[:-1], rest[-1]
+    samples, top_count, _ = routes_ref.shape
+    here = lax.axis_index("grid")
+    copies = []
+    for pair, target in zip(pairs, pair_refs):
+        column = (here ^ (2 * pair)) * per_tile
+        experts = [
+            routes_ref[sample, rank, column + place]
+            for sample in range(samples)
+            for rank in range(top_count)
+            for place in range(per_tile)
+        ]
+        for which, source in enumerate((own_ref, beside_ref)):
+            inside = [expert - (here ^ which) * owned for expert in experts]
+            found = tree_sum([jnp.where((at >= 0) & (at < owned), at, 0) for at in inside])
             copies.append(
-                pltpu.make_async_copy(source.at[0, rows], send_ref.at[at], send_sem.at[at])
-            )
-    for copy in copies:
-        copy.start()
+                pltpu.make_async_copy(source.at[found], target.at[which], sem.at[pair, which])
+            )
+            copies[-1].start()
     for copy in copies:
         copy.wait()
 
 
-def grads_kernel(
-    owned, routes_ref, x_ref, dy_ref, got_ref, wire_ref, grads_ref, dy_all_ref, x_all_ref, taps_ref,
-    grad_ref,
-):
-    samples, top_count, patches = routes_ref.shape
-    tiles, groups, _ = wire_ref.shape
-    others, _, channels, _ = got_ref.shape
-    per_tile = patches // tiles
+def unit_grad(x, dy, unit, taps_ref, grad_ref, masks):
+    x = x.astype(jnp.float32)
+    for tap in range(TAPS):
+        part = moved(x, tap // 3 - 1, tap % 3 - 1, masks)
+        for half in range(PIX // 128):
+            taps_ref[half, pl.ds(unit * ROW + tap, CG, stride=TAPS), :] = part[
+                :, half * 128:(half + 1) * 128
+            ]
+    grad = lax.dot_general(
+        dy,
+        joined(taps_ref, unit * ROW, ROW).astype(jnp.bfloat16),
+        (((1,), (1,)), ((), ())),
+        preferred_element_type=jnp.float32,
+    )
+    put(grad_ref, unit * CG, grad)
+
+
+def flat_quads(grad_ref, rows_count):
+    for quad in range(CG // 4):
+        parts = [None] * TAPS
+        for j in range(4):
+            line = rolled(strided(grad_ref, quad * 4 + j, rows_count, CG), 32 * j)
+            for m in range(3):
+                piece = line[:, m * 128:(m + 1) * 128]
+                at = 2 * j + m
+                parts[at] = piece if parts[at] is None else parts[at] + piece
+        flat = jnp.concatenate(parts, axis=1).astype(jnp.bfloat16)
+        yield slice(quad * QUAD, (quad + 1) * QUAD), flat
+
+
+def grads_kernel(owned, per_tile, routes_ref, x_ref, dy_ref, got_ref, wire_ref, taps_ref, grad_ref):
+    samples, top_count, _ = routes_ref.shape
+    groups = wire_ref.shape[1]
     together = min(ROWS // groups, per_tile)
     rows_count = together * groups
+    per_sample = per_tile // together
     tile = lax.axis_index("grid")
     mine = lax.axis_index("batch")
-    own_rows = pl.ds(pl.multiple_of(mine * channels, channels), channels)
-    for place in range(per_tile):
-        span = slice(place * PIX, (place + 1) * PIX)
-        x_all_ref[mine * per_tile + place] = x_ref[0, own_rows, span]
-        dy_all_ref[mine * per_tile + place] = dy_ref[0, own_rows, span]
-        for step in range(1, others + 1):
-            sample = lax.rem(mine - step + others + 1, others + 1)
-            x_all_ref[sample * per_tile + place] = got_ref[step - 1, 0, :, span]
-            dy_all_ref[sample * per_tile + place] = got_ref[step - 1, 1, :, span]
     grad_ref[WIDE // 128 - 1] = jnp.zeros((rows_count * CG, 128), jnp.float32)
     masks = pixel_masks(CG)
 
-    def work(block, carry):
+    def work(sample, block, read):
         for unit in range(rows_count):
-            patch = block * together + unit // groups
-            rows = slice((unit % groups) * CG, (unit % groups + 1) * CG)
-            x_unit = x_all_ref[patch, rows, :].astype(jnp.float32)
-            for tap in range(TAPS):
-                part = moved(x_unit, tap // 3 - 1, tap % 3 - 1, masks)
-                for half in range(PIX // 128):
-                    taps_ref[half, pl.ds(unit * ROW + tap, CG, stride=TAPS), :] = part[
-                        :, half * 128:(half + 1) * 128
-                    ]
-            grad = lax.dot_general(
-                dy_all_ref[patch, rows, :],
-                joined(taps_ref, unit * ROW, ROW).astype(jnp.bfloat16),
-                (((1,), (1,)), ((), ())),
-                preferred_element_type=jnp.float32,
-            )
-            put(grad_ref, unit * CG, grad)
+            place = block * together + unit // groups
+            span = pl.ds(pl.multiple_of(place * PIX, PIX), PIX)
+            x, dy = read(unit % groups, span)
+            unit_grad(x, dy, unit, taps_ref, grad_ref, masks)
         slots = []
         for place in range(together):
-            patch = block * together + place
-            column = tile * per_tile + lax.rem(patch, per_tile)
-            slots.append([])
+            column = tile * per_tile + block * together + place
+            slots.append(
+                [lax.div(routes_ref[sample, rank, column], owned) for rank in range(top_count)]
+            )
+        for lanes, flat in flat_quads(grad_ref, rows_count):
+            for place in range(together):
+                for slot in slots[place]:
+                    wire_ref[slot, :, lanes] = flat[place * groups:(place + 1) * groups]
+
+    def own(block, carry):
+        def read(group, span):
+            row = pl.multiple_of((mine * groups + group) * CG, CG)
+            return tuple(ref[0, pl.ds(row, CG), span] for ref in (x_ref, dy_ref))
+
+        work(mine, block, read)
+        return carry
+
+    def other(number, carry):
+        step = lax.div(number, per_sample)
+
+        def read(group, span):
+            rows = slice(group * CG, (group + 1) * CG)
+            return tuple(got_ref[step, which, rows, span] for which in range(2))
+
+        work(lax.rem(mine - step - 1 + samples, samples), lax.rem(number, per_sample), read)
+        return carry
+
+    lax.fori_loop(0, per_sample, own, 0)
+    lax.fori_loop(0, (samples - 1) * per_sample, other, 0)
+
+
+def tables_kernel(owned, per_tile, routes_ref, logits_ref, local_ref, gate_ref):
+    samples, top_count, _ = routes_ref.shape
+    first = lax.axis_index("grid") * owned
+
+    def scan(tile, carry):
+        locals_hit, logits_hit = [], []
+        for sample in range(samples):
             for rank in range(top_count):
-                expert = routes_ref[lax.div(patch, per_tile), rank, column]
-                slots[-1].append(lax.div(expert, owned))
-        for quad in range(CG // 4):
-            parts = [None] * TAPS
-            for j in range(4):
-                line = rolled(strided(grad_ref, quad * 4 + j, rows_count, CG), 32 * j)
-                for m in range(3):
-                    piece = line[:, m * 128:(m + 1) * 128]
-                    at = 2 * j + m
-                    parts[at] = piece if parts[at] is None else parts[at] + piece
-            flat = jnp.concatenate(parts, axis=1)
-            for place in range(together):
-                value = flat[place * groups:(place + 1) * groups].astype(jnp.bfloat16)
-                lanes = slice(quad * QUAD, (quad + 1) * QUAD)
-                grads_ref[block * together + place, :, lanes] = value
-                for slot in slots[place]:
-                    wire_ref[slot, :, lanes] = value
-        return carry
-
-    lax.fori_loop(0, samples * per_tile // together, work, 0)
-
-
-def tables_kernel(owned, per_tile, routes_ref, logits_ref, local_ref, gate_ref):
-    first = lax.axis_index("grid") * owned
-
-    def scan(tile, carry):
-        local, logit = jnp.int32(0), jnp.float32(0)
-        for at, inside, hit in named(routes_ref, tile, per_tile, first, owned):
-            local = jnp.where(hit, inside, local)
-            logit = jnp.where(hit, logits_ref[at], logit)
-        local_ref[tile] = local
-        gate = jax.nn.sigmoid(jnp.full(gate_ref.shape[1:], logit, jnp.float32))
+                for place in range(per_tile):
+                    at = (sample, rank, tile * per_tile + place)
+                    inside = routes_ref[at] - first
+                    hit = (inside >= 0) & (inside < owned)
+                    locals_hit.append(jnp.where(hit, inside, 0))
+                    logits_hit.append(jnp.where(hit, logits_ref[at], 0.0))
+        local_ref[tile] = tree_sum(locals_hit)
+        gate = jax.nn.sigmoid(jnp.full(gate_ref.shape[1:], tree_sum(logits_hit), jnp.float32))
         gate_ref[tile] = gate / SIDE
         return carry
 
@@ -215,11 +238,12 @@
     return total.astype(jnp.bfloat16)
 
 
-def adjoint_kernel(owned, routes_ref, logits_ref, grads_ref, dy_all_ref, *rest):
-    pair_refs, rest = rest[:-9], rest[-9:]
+def adjoint_kernel(owned, routes_ref, logits_ref, wire_ref, got_ref, *rest):
+    pair_refs, rest = rest[:-12], rest[-12:]
     (
         out_ref, own_dots_ref, own_mixed_ref,
-        kernels_ref, flat_ref, mixed_ref, spread_ref, dots_ref, place_sem,
+        grads_ref, dy_ref, kernels_ref, flat_ref, mixed_ref, spread_ref, dots_ref, place_sem,
+        fetch_sem,
     ) = rest
     samples, top_count, patches = routes_ref.shape
     tiles, groups, _ = kernels_ref.shape
@@ -239,6 +263,8 @@
         pltpu.make_async_copy(source, target, place_sem.at[number])
         for number, (source, target) in enumerate(places)
     ]
+    copies.append(pltpu.make_async_copy(wire_ref, grads_ref, fetch_sem.at[0]))
+    copies.append(pltpu.make_async_copy(got_ref.at[:, 1], dy_ref, fetch_sem.at[1]))
     for copy in copies:
         copy.start()
     masks = pixel_masks(CG)
@@ -259,7 +285,7 @@
             for at in range(0, CG * ROW, 128):
                 lanes = slice(at, at + 128)
                 mixed = jnp.zeros((groups, 128), jnp.float32)
-                grad = grads_ref[patch, :, lanes].astype(jnp.float32)
+                grad = grads_ref[slots[0], :, lanes].astype(jnp.float32)
                 for rank in range(top_count):
                     kernel = kernels_ref[slots[rank], :, lanes].astype(jnp.float32)
                     dots[rank] += kernel * grad
@@ -285,9 +311,9 @@
         for unit in range(rows_count):
             place = unit // groups
             rows = slice((unit % groups) * CG, (unit % groups + 1) * CG)
-            dy = dy_all_ref[block * together + place, rows, :]
-            offset = pl.multiple_of((within * together + place) * PIX, PIX)
-            out_ref[step - 1, rows, pl.ds(offset, PIX)] = adjoint_unit(
+            span = pl.ds(pl.multiple_of((within * together + place) * PIX, PIX), PIX)
+            dy = dy_ref[samples - 1 - step, rows, span]
+            out_ref[step - 1, rows, span] = adjoint_unit(
                 mixed_ref, spread_ref, unit, dy, masks
             )
         return carry
@@ -323,11 +349,10 @@
         out_ref[step - 1, channels:channels + DOT_ROWS, :128] = route_dots
 
 
-def own_adjoint_kernel(mixed_ref, dy_all_ref, out_ref, spread_ref):
+def own_adjoint_kernel(mixed_ref, dy_ref, out_ref, spread_ref):
     per_sample, _, mixed_rows, _ = mixed_ref.shape
     rows_count = mixed_rows // CG
-    channels, span = out_ref.shape
-    groups = channels // CG
+    groups = out_ref.shape[0] // CG
     together = rows_count // groups
     mine = lax.axis_index("batch")
     masks = pixel_masks(CG)
@@ -335,10 +360,11 @@
     def work(within, carry):
         for unit in range(rows_count):
             place = within * together + unit // groups
-            rows = slice((unit % groups) * CG, (unit % groups + 1) * CG)
-            dy = dy_all_ref[mine * (span // PIX) + place, rows, :]
-            out_ref[rows, pl.ds(pl.multiple_of(place * PIX, PIX), PIX)] = adjoint_unit(
-                mixed_ref.at[within], spread_ref, unit, dy, masks
+            group = unit % groups
+            lanes = pl.ds(pl.multiple_of(place * PIX, PIX), PIX)
+            row = pl.multiple_of((mine * groups + group) * CG, CG)
+            out_ref[group * CG:(group + 1) * CG, lanes] = adjoint_unit(
+                mixed_ref.at[within], spread_ref, unit, dy_ref[0, pl.ds(row, CG), lanes], masks
             )
         return carry
 
@@ -399,30 +425,18 @@
 
     weights_beside = swap(weights, 1)
     pair_count = tiles // 2
-    table = jax.ShapeDtypeStruct((pair_count,), jnp.int32)
-    own_ids, beside_ids = pl.pallas_call(
-        functools.partial(scan_kernel, owned, per_tile),
-        out_shape=(table, table),
-        in_specs=[smem],
-        out_specs=(smem, smem),
-        compiler_params=params,
-        cost_estimate=pl.CostEstimate(flops=COST, bytes_accessed=1, transcendentals=0),
-        name="scan",
-    )(routes_t)
-
-    to_send, *pairs = pl.pallas_call(
-        pack_kernel,
-        out_shape=(jax.ShapeDtypeStruct((batch - 1, 2, channels, span), jnp.bfloat16),)
-        + (blocks_shape(2),) * pair_count,
-        in_specs=[smem, smem] + [vmem] * 4,
-        out_specs=(hbm,) * (1 + pair_count),
-        scratch_shapes=[
-            pltpu.SemaphoreType.DMA((pair_count, 2)),
-            pltpu.SemaphoreType.DMA((batch - 1, 2)),
-        ],
-        compiler_params=params,
-        name="pack",
-    )(own_ids, beside_ids, weights, weights_beside, inputs, cotangent)
+    pairs = []
+    order = pair_order(tiles)
+    for some in (order[:EARLY], order[EARLY:]):
+        pairs += pl.pallas_call(
+            functools.partial(pack_kernel, owned, per_tile, some),
+            out_shape=(blocks_shape(2),) * len(some),
+            in_specs=[smem, vmem, vmem],
+            out_specs=(hbm,) * len(some),
+            scratch_shapes=[pltpu.SemaphoreType.DMA((pair_count, 2))],
+            compiler_params=params,
+            name="pack",
+        )(routes_t, weights, weights_beside)
     pairs = [
         blocks if pair == 0 else swap(blocks, 2 * pair)
         for pair, blocks in zip(pair_order(tiles), pairs)
@@ -436,28 +450,39 @@
             for step in range(1, batch)
         ]
 
+    mine = lax.axis_index("batch")
+    to_send = pl.pallas_call(
+        stage_kernel,
+        out_shape=jax.ShapeDtypeStruct((batch - 1, 2, channels, span), jnp.bfloat16),
+        in_specs=[hbm] * 2,
+        out_specs=hbm,
+        scratch_shapes=[
+            pltpu.VMEM((batch - 1, 2, channels, span), jnp.bfloat16),
+            pltpu.SemaphoreType.DMA((batch - 1, 2)),
+            pltpu.SemaphoreType.DMA((batch - 1, 2)),
+        ],
+        compiler_params=pltpu.CompilerParams(vmem_limit_bytes=WHOLE_VMEM),
+        cost_estimate=pl.CostEstimate(flops=COST, bytes_accessed=1, transcendentals=0),
+        name="stage",
+    )(inputs, cotangent)
     got = jnp.stack(exchange([to_send[step] for step in range(batch - 1)]))
 
-    work = samples * patches // tiles * groups * width * PIX * 2
-    wire, grads, dy_all = pl.pallas_call(
-        functools.partial(grads_kernel, owned),
-        out_shape=(
-            blocks_shape(tiles),
-            blocks_shape(samples * per_tile),
-            jax.ShapeDtypeStruct((samples * per_tile, channels, PIX), jnp.bfloat16),
-        ),
+    grad_scratch = [
+        pltpu.VMEM((PIX // 128, rows * ROW, 128), jnp.float32),
+        pltpu.VMEM((WIDE // 128, rows * CG, 128), jnp.float32),
+    ]
+    wire = pl.pallas_call(
+        functools.partial(grads_kernel, owned, per_tile),
+        out_shape=blocks_shape(tiles),
         in_specs=[smem, vmem, vmem, vmem],
-        out_specs=(vmem, vmem, vmem),
-        scratch_shapes=[
-            pltpu.VMEM((samples * per_tile, channels, PIX), jnp.bfloat16),
-            pltpu.VMEM((PIX // 128, rows * ROW, 128), jnp.float32),
-            pltpu.VMEM((WIDE // 128, rows * CG, 128), jnp.float32),
-        ],
+        out_specs=vmem,
+        scratch_shapes=grad_scratch,
         compiler_params=params,
         cost_estimate=pl.CostEstimate(flops=COST, bytes_accessed=1, transcendentals=0),
         name="kernel_grads",
     )(routes_t, inputs, cotangent, got)
 
+    wire, _ = lax.optimization_barrier((wire, pairs[:2]))
     grads_back = lax.all_to_all(wire, "grid", split_axis=0, concat_axis=0, tiled=True)
 
     per_sample = per_tile // together
@@ -468,20 +493,23 @@
             jax.ShapeDtypeStruct((DOT_ROWS, 128), jnp.bfloat16),
             jax.ShapeDtypeStruct((per_sample, WIDE // 128, rows * CG, 128), jnp.float32),
         ),
-        in_specs=[smem, smem, vmem, vmem] + [anywhere] * (tiles // 2),
+        in_specs=[smem, smem] + [anywhere] * (2 + pair_count),
         out_specs=(vmem, vmem, vmem),
         scratch_shapes=[
+            pltpu.VMEM((tiles, groups, width), jnp.bfloat16),
+            pltpu.VMEM((batch - 1, channels, span), jnp.bfloat16),
             pltpu.VMEM((tiles, groups, width), jnp.bfloat16),
             pltpu.VMEM((rows, width), jnp.float32),
             pltpu.VMEM((WIDE // 128, rows * CG, 128), jnp.float32),
             pltpu.VMEM((PIX // 128, rows * ROW, 128), jnp.float32),
             pltpu.VMEM((samples * per_tile * top_count * groups, 128), jnp.float32),
             pltpu.SemaphoreType.DMA((tiles,)),
+            pltpu.SemaphoreType.DMA((2,)),
         ],
         compiler_params=params,
         cost_estimate=pl.CostEstimate(flops=COST, bytes_accessed=1, transcendentals=0),
         name="adjoint",
-    )(routes_t, logits_t, grads, dy_all, *pairs)
+    )(routes_t, logits_t, wire, got, *pairs)
 
     own_part = pl.pallas_call(
         own_adjoint_kernel,
@@ -492,7 +520,7 @@
         compiler_params=params,
         cost_estimate=pl.CostEstimate(flops=COST // 20, bytes_accessed=1, transcendentals=0),
         name="own_adjoint",
-    )(own_mixed, dy_all)
+    )(own_mixed, cotangent)
 
     late_routes, late_logits, _ = lax.optimization_barrier((routes_t, logits_t, own_dots))
     local, gate_table = pl.pallas_call(
@@ -508,7 +536,6 @@
     )(late_routes, late_logits)
 
     arrived = exchange([parts[step] for step in range(batch - 1)])
-    mine = lax.axis_index("batch")
     d_inputs = jnp.zeros(inputs.shape, jnp.bfloat16)
     dots = own_dots[0].astype(jnp.float32)
     for step, part in enumerate([own_part] + arrived):
@@ -520,8 +547,8 @@
             dots += part[channels, :128].astype(jnp.float32)
     dots = dots[:tiles].reshape(samples, per_tile, top_count)
     gates = jax.nn.sigmoid(
-        lax.dynamic_slice_in_dim(gate_logits, lax.axis_index("grid") * per_tile, per_tile, 1)
-    )
+        lax.dynamic_slice_in_dim(late_logits, lax.axis_index("grid") * per_tile, per_tile, 2)
+    ).transpose(0, 2, 1)
     gate_grad = gates * (1.0 - gates) * dots / SIDE
 
     d_weights = pl.pallas_call(

time: 65.7 us -> 63.1 us (0.960)
  local copies, waits for them, and re-layouts: 5.51 us -> 1 us
  waiting for transfers between devices: 21.8 us -> 18.2 us
  starting transfers between devices: 15.5 us -> 18.2 us
  Pallas kernels: 21.6 us -> 23.9 us
  other arithmetic: 0.02 us -> 0.68 us
    unnamed x24 -> x16, local copies, waits for them, and re-layouts: 5.23 us -> 0.69 us
    ppermute x8, waiting for transfers between devices: 5 us -> 1.55 us  [swap(): return lax.ppermute(blocks, 'grid', [(i, i ^ step) for i in range(tiles)])]
    ppermute x8, starting transfers between devices: 6.94 us -> 9.93 us  [swap(): return lax.ppermute(blocks, 'grid', [(i, i ^ step) for i in range(tiles)])]
    pallas_call x3 -> x4, Pallas kernels: 8.97 us -> 10 us  [the longest x1 4.78 us: per_device(): pl.pallas_call(functools.partial(grads_kernel, owned, per_tile), out_shap...]
    div x1, other arithmetic: 0.01 us -> 0.68 us  [per_device(): gate_grad = gates * (1.0 - gates) * dots / SIDE]
  transfers between devices with their start and end apart: 11 -> 11, of which waited for: 5 -> 4; matrix products, arithmetic and copies ran while one was open for 2% -> 2% of each run, Pallas kernels for 26% -> 35%
where the time goes in v4:
time: 63.1 us; the launch traced here: 62.9 us
  Pallas kernels  23.9 us (38%)
  starting transfers between devices  18.2 us (29%)
  waiting for transfers between devices  18.2 us (29%)
  local copies, waits for them, and re-layouts  1 us (2%)
  between operations  0.8 us (1%)
  other arithmetic  0.68 us (1%)
    all_to_all x1, waiting for transfers between devices, per_device(): lax.all_to_all(wire, 'grid', split_axis=0, concat_axis=0, tiled=True)  10.6 us
    ppermute x8, starting transfers between devices, swap(): return lax.ppermute(blocks, 'grid', [(i, i ^ step) for i in range(tiles)])  9.93 us
    pallas_call x1, Pallas kernels, per_device(): pl.pallas_call(functools.partial(adjoint_kernel, owned), out_shape=(jax.S...  7.42 us
    all_to_all x1, starting transfers between devices, per_device(): lax.all_to_all(wire, 'grid', split_axis=0, concat_axis=0, tiled=True)  6.7 us
    ppermute x2, waiting for transfers between devices, exchange(): lax.ppermute(blocks[step - 1], 'batch', [(i, (i + step) % batch) for i in...  6.02 us
    pallas_call x1, Pallas kernels, per_device(): pl.pallas_call(functools.partial(grads_kernel, owned, per_tile), out_shap...  4.78 us
    pallas_call x2, Pallas kernels, per_device(): pl.pallas_call(functools.partial(pack_kernel, owned, per_tile, some), out...  3.47 us
    pallas_call x1, Pallas kernels, per_device(): pl.pallas_call(functools.partial(tables_kernel, owned, per_tile), out_sha...  2.67 us
  transfers between devices with their start and end apart: 11, of which 4 were waited for; matrix products, arithmetic and copies ran while one was open for 2% of the time, Pallas kernels for 35%

profile of v4, /device:TPU:13, one launch (start us, length us, event | category | flops | bytes accessed | tf_op | source)
XLA Modules:
  0.0 62.9 jit_solution(1304712533741601197)
XLA Ops:
  0.6 0.0 copy-start
  0.6 0.0 copy-start.1
  0.7 0.7 %collective-permute-start.1 = (bf16[8,4,9216]{2,1,0:T(4,128)(2,1)}, bf16[8,4,9216]{2,1,0:T(4,128)(2,1)S(1)}, u32[]{:S(2)}, u32[]{:S(2)}) collective-permute-start(bf16[8,4,9216]{2,1,0:T(4,128)(2,1)} %own_ref.3), channel_id=1, source_target_pairs={{0,2},{2,0},{4,6},{6,4},{8,10},{10,8},{12,14},{14,12},{16,18},{18,... | collective-permute-start | bytes 1769480 | tf_op jit(solution)/shard_map/ppermute | solution.py:424
  1.4 1.8 %stage.1 = bf16[1,2,128,1024]{3,2,1,0:T(8,128)(2,1)} custom-call(bf16[1,256,1024]{2,1,0:T(8,128)(2,1)} %x_ref.1, bf16[1,256,1024]{2,1,0:T(8,128)(2,1)} %dy_ref.3), custom_call_target="tpu_custom_call" | custom-call | flops 20000000000 | bytes 1 | tf_op jit(solution)/shard_map/stage/pallas_call | solution.py:454
  3.2 1.3 %collective-permute-start = (bf16[2,128,1024]{2,1,0:T(8,128)(2,1)}, bf16[2,128,1024]{2,1,0:T(8,128)(2,1)S(1)}, u32[]{:S(2)}, u32[]{:S(2)}) collective-permute-start(bf16[2,128,1024]{2,1,0:T(8,128)(2,1)} %bitcast.24), channel_id=1, source_target_pairs={{0,1},{1,0},{2,3},{3,2},{4,5},{5,4},{6,7},{7,6},{8,9},{9,8},{10,11... | collective-permute-start | bytes 1572872 | tf_op jit(solution)/shard_map/ppermute | solution.py:447
  4.5 0.0 collective-permute-done.1.beside_ref
  4.5 0.0 copy-done
  4.5 0.0 copy-done.1
  4.5 0.0 copy-start.3
  4.5 0.0 copy-start.4
  4.5 1.7 %pack.2 = (bf16[2,4,9216]{2,1,0:T(4,128)(2,1)S(1)}, bf16[2,4,9216]{2,1,0:T(4,128)(2,1)S(1)}, bf16[2,4,9216]{2,1,0:T(4,128)(2,1)S(1)}) custom-call(s32[2,2,64]{2,1,0:T(2,128)S(1)} %bitcast.13, bf16[8,4,9216]{2,1,0:T(4,128)(2,1)S(1)} %copy-done, bf16[8,4,9216]{2,1,0:T(4,128)(2,1)S(1)} %collective-permute-done.1.beside_ref), custom_call_target="tpu_custom_call" | custom-call | tf_op jit(solution)/shard_map/pack/pallas_call | solution.py:431
  6.2 0.3 collective-permute-start.2
  6.5 1.3 %collective-permute-start.3 = (bf16[2,4,9216]{2,1,0:T(4,128)(2,1)S(1)}, bf16[2,4,9216]{2,1,0:T(4,128)(2,1)S(1)}, u32[]{:S(2)}, u32[]{:S(2)}) collective-permute-start(bf16[2,4,9216]{2,1,0:T(4,128)(2,1)S(1)} %get-tuple-element.20), channel_id=1, source_target_pairs={{0,24},{2,26},{4,28},{6,30},{8,16},{10,18},{12,20},{14,22},{16,8},... | collective-permute-start | bytes 442376 | tf_op jit(solution)/shard_map/ppermute | solution.py:424
  7.8 1.8 %pack.3 = (bf16[2,4,9216]{2,1,0:T(4,128)(2,1)}, bf16[2,4,9216]{2,1,0:T(4,128)(2,1)}, bf16[2,4,9216]{2,1,0:T(4,128)(2,1)}, bf16[2,4,9216]{2,1,0:T(4,128)(2,1)}, bf16[2,4,9216]{2,1,0:T(4,128)(2,1)S(1)}) custom-call(s32[2,2,64]{2,1,0:T(2,128)S(1)} %bitcast.14, bf16[8,4,9216]{2,1,0:T(4,128)(2,1)S(1)} %copy-done, ...), custom_call_target="tpu_custom_call" | custom-call | tf_op jit(solution)/shard_map/pack/pallas_call | solution.py:431
  9.6 0.0 copy-start.5
  9.6 0.7 %copy-done.5 = bf16[2,4,9216]{2,1,0:T(4,128)(2,1)} copy-done((bf16[2,4,9216]{2,1,0:T(4,128)(2,1)}, bf16[2,4,9216]{2,1,0:T(4,128)(2,1)S(1)}, u32[]{:S(2)}) %copy-start.5) | copy-done | bytes 147480
  10.2 3.2 %collective-permute-start.5 = (bf16[2,4,9216]{2,1,0:T(4,128)(2,1)}, bf16[2,4,9216]{2,1,0:T(4,128)(2,1)}, u32[]{:S(2)}, u32[]{:S(2)}) collective-permute-start(bf16[2,4,9216]{2,1,0:T(4,128)(2,1)} %get-tuple-element.23), channel_id=1, source_target_pairs={{0,12},{2,14},{4,8},{6,10},{8,4},{10,6},{12,0},{14,2},{16,28},{18,... | collective-permute-start | bytes 442376 | tf_op jit(solution)/shard_map/ppermute | solution.py:424
  13.4 0.0 collective-permute-start.6
  13.4 3.7 %collective-permute-done = bf16[2,128,1024]{2,1,0:T(8,128)(2,1)S(1)} collective-permute-done((bf16[2,128,1024]{2,1,0:T(8,128)(2,1)}, bf16[2,128,1024]{2,1,0:T(8,128)(2,1)S(1)}, u32[]{:S(2)}, u32[]{:S(2)}) %collective-permute-start) | collective-permute-done | bytes 524320 | tf_op jit(solution)/shard_map/ppermute | solution.py:447
  17.1 2.3 %collective-permute-start.7 = (bf16[2,4,9216]{2,1,0:T(4,128)(2,1)}, bf16[2,4,9216]{2,1,0:T(4,128)(2,1)}, u32[]{:S(2)}, u32[]{:S(2)}) collective-permute-start(bf16[2,4,9216]{2,1,0:T(4,128)(2,1)} %get-tuple-element.25), channel_id=1, source_target_pairs={{0,20},{2,22},{4,16},{6,18},{8,28},{10,30},{12,24},{14,26},{16,4},... | collective-permute-start | bytes 442376 | tf_op jit(solution)/shard_map/ppermute | solution.py:424
  19.3 0.0 collective-permute-done.2.rest_0_
  19.3 0.0 collective-permute-start.8
  19.3 0.0 collective-permute-done.3.rest_1_
  19.3 2.2 %collective-permute-start.4 = (bf16[2,4,9216]{2,1,0:T(4,128)(2,1)S(1)}, bf16[2,4,9216]{2,1,0:T(4,128)(2,1)S(1)}, u32[]{:S(2)}, u32[]{:S(2)}) collective-permute-start(bf16[2,4,9216]{2,1,0:T(4,128)(2,1)S(1)} %get-tuple-element.22), channel_id=1, source_target_pairs={{0,8},{2,10},{4,12},{6,14},{8,0},{10,2},{12,4},{14,6},{16,24},{18,... | collective-permute-start | bytes 442376 | tf_op jit(solution)/shard_map/ppermute | solution.py:424
  21.5 0.0 copy-done.3
  21.5 0.0 copy-done.4
  21.5 4.8 %kernel_grads.1.wire_ref = bf16[16,4,9216]{2,1,0:T(4,128)(2,1)} custom-call(s32[2,2,64]{2,1,0:T(2,128)S(1)} %bitcast.15, bf16[1,256,1024]{2,1,0:T(8,128)(2,1)S(1)} %copy-done.3, bf16[1,256,1024]{2,1,0:T(8,128)(2,1)S(1)} %copy-done.4, bf16[1,2,128,1024]{3,2,1,0:T(8,128)(2,1)S(1)} %bitcast.21), custom_call_target="tpu_custom_call" | custom-call | flops 20000000000 | bytes 1 | tf_op jit(solution)/shard_map/kernel_grads/pallas_call | solution.py:474
  26.3 6.7 %all-to-all-start = ((bf16[16,4,9216]{2,1,0:T(4,128)(2,1)}), bf16[16,4,9216]{2,1,0:T(4,128)(2,1)S(1)}, u32[]{:S(2)}, u32[]{:S(2)}) async-start(bf16[16,4,9216]{2,1,0:T(4,128)(2,1)} %kernel_grads.1.wire_ref), calls=%async_computation | async-start | bytes 2359296 | tf_op jit(solution)/shard_map/all_to_all | solution.py:486
  33.0 0.0 collective-permute-done.5.rest_3_
  33.0 0.0 collective-permute-done.6.rest_4_
  33.0 0.0 collective-permute-done.7.rest_5_
  33.0 1.5 %collective-permute-done.8.rest_6_ = bf16[2,4,9216]{2,1,0:T(4,128)(2,1)S(1)} collective-permute-done((bf16[2,4,9216]{2,1,0:T(4,128)(2,1)}, bf16[2,4,9216]{2,1,0:T(4,128)(2,1)S(1)}, u32[]{:S(2)}, u32[]{:S(2)}) %collective-permute-start.8) | collective-permute-done | bytes 147488 | tf_op jit(solution)/shard_map/ppermute | solution.py:424
  34.6 0.0 collective-permute-done.4.rest_2_
  34.6 0.0 copy-done.2
  34.6 0.0 copy-done.6
  34.6 7.4 %adjoint.1 = (bf16[1,144,1024]{2,1,0:T(8,128)(2,1)S(1)}, bf16[16,128]{1,0:T(8,128)(2,1)S(1)}, f32[2,3,256,128]{3,2,1,0:T(8,128)S(1)}) custom-call(s32[2,2,64]{2,1,0:T(2,128)S(1)} %bitcast.16, f32[2,2,64]{2,1,0:T(2,128)S(1)} %bitcast.18, bf16[16,4,9216]{2,1,0:T(4,128)(2,1)} %kernel_grads.1.wire_ref, bf16[1,2,128,1024]{3,2,1,0:T(8,128)(2,1)S(1)} %bitcast.22, ...), custom_call_target="tpu_custom_call" | custom-call | flops 20000000000 | bytes 1 | tf_op jit(solution)/shard_map/adjoint/pallas_call | solution.py:489
  42.0 0.3 collective-permute-start.9
  42.3 2.7 %tables.1 = (s32[16]{0:T(128)S(1)}, f32[16,4,128]{2,1,0:T(4,128)S(1)}) custom-call(s32[2,2,64]{2,1,0:T(2,128)S(1)} %bitcast.17, f32[2,2,64]{2,1,0:T(2,128)S(1)} %bitcast.19), custom_call_target="tpu_custom_call" | custom-call | tf_op jit(solution)/shard_map/tables/pallas_call | solution.py:526
  45.0 1.7 %own_adjoint.1 = bf16[128,1024]{1,0:T(8,128)(2,1)S(1)} custom-call(f32[2,3,256,128]{3,2,1,0:T(8,128)S(1)} %get-tuple-element.28.mixed_ref, bf16[1,256,1024]{2,1,0:T(8,128)(2,1)S(1)} %copy-done.4), custom_call_target="tpu_custom_call" | custom-call | flops 1000000000 | bytes 1 | tf_op jit(solution)/shard_map/own_adjoint/pallas_call | solution.py:514
  46.8 0.1 broadcast_in_dim.9
  46.8 2.4 %collective-permute-done.9 = bf16[144,1024]{1,0:T(8,128)(2,1)S(1)} collective-permute-done((bf16[144,1024]{1,0:T(8,128)(2,1)S(1)}, bf16[144,1024]{1,0:T(8,128)(2,1)S(1)}, u32[]{:S(2)}, u32[]{:S(2)}) %collective-permute-start.9) | collective-permute-done | bytes 294944 | tf_op jit(solution)/shard_map/ppermute | solution.py:447
  49.2 0.1 slice.20
  49.3 0.1 copy.9
  49.4 0.7 %fusion.2 = f32[2,4,2]{1,2,0:T(2,128)} fusion(f32[2,4,2]{1,2,0:T(2,128)S(1)} %copy.9, f32[2,2,64]{2,1,0:T(2,128)S(1)} %bitcast.20, s32[]{:T(128)S(6)} %select_n.11), kind=kLoop, calls=%fused_computation.5 | loop fusion | flops 112 | bytes 196 | tf_op jit(solution)/shard_map/div | solution.py:552
  50.1 0.0 copy-start.7
  50.1 10.6 %all-to-all-done.got_ref = bf16[16,4,9216]{2,1,0:T(4,128)(2,1)S(1)} async-done(((bf16[16,4,9216]{2,1,0:T(4,128)(2,1)}), bf16[16,4,9216]{2,1,0:T(4,128)(2,1)S(1)}, u32[]{:S(2)}, u32[]{:S(2)}) %all-to-all-start) | async-done | bytes 1179680 | tf_op jit(solution)/shard_map/all_to_all | solution.py:486
  60.8 2.1 %weight_sum.1 = f32[8,4,9216]{2,1,0:T(4,128)} custom-call(s32[16]{0:T(128)S(1)} %get-tuple-element.33.local_ref, f32[16,4,128]{2,1,0:T(4,128)S(1)} %get-tuple-element.34.gate_ref, bf16[16,4,9216]{2,1,0:T(4,128)(2,1)S(1)} %all-to-all-done.got_ref), custom_call_target="tpu_custom_call" | custom-call | tf_op jit(solution)/shard_map/weight_sum/pallas_call | solution.py:554
  62.8 0.0 copy-done.7
  (6 shorter events, 0.1 us)
Async XLA Ops:
  0.6 3.8 %copy-start = (bf16[8,4,9216]{2,1,0:T(4,128)(2,1)S(1)}, bf16[8,4,9216]{2,1,0:T(4,128)(2,1)}, u32[]{:S(2)}) copy-start(bf16[8,4,9216]{2,1,0:T(4,128)(2,1)} %own_ref.3) | copy-start | bytes 1769476
  0.6 3.8 %copy-start.1 = (s32[2,64,2]{1,2,0:T(2,128)S(1)}, s32[2,64,2]{1,2,0:T(2,128)}, u32[]{:S(2)}) copy-start(s32[2,64,2]{1,2,0:T(2,128)} %param.9) | copy-start | bytes 3076
  0.7 3.8 %collective-permute-start.1 = (bf16[8,4,9216]{2,1,0:T(4,128)(2,1)}, bf16[8,4,9216]{2,1,0:T(4,128)(2,1)S(1)}, u32[]{:S(2)}, u32[]{:S(2)}) collective-permute-start(bf16[8,4,9216]{2,1,0:T(4,128)(2,1)} %own_ref.3), channel_id=1, source_target_pairs={{0,2},{2,0},{4,6},{6,4},{8,10},{10,8},{12,14},{14,12},{16,18},{18,... | collective-permute-start | bytes 1769480 | tf_op jit(solution)/shard_map/ppermute | solution.py:424
  3.2 13.9 %collective-permute-start = (bf16[2,128,1024]{2,1,0:T(8,128)(2,1)}, bf16[2,128,1024]{2,1,0:T(8,128)(2,1)S(1)}, u32[]{:S(2)}, u32[]{:S(2)}) collective-permute-start(bf16[2,128,1024]{2,1,0:T(8,128)(2,1)} %bitcast.24), channel_id=1, source_target_pairs={{0,1},{1,0},{2,3},{3,2},{4,5},{5,4},{6,7},{7,6},{8,9},{9,8},{10,11... | collective-permute-start | bytes 1572872 | tf_op jit(solution)/shard_map/ppermute | solution.py:447
  4.5 17.0 %copy-start.3 = (bf16[1,256,1024]{2,1,0:T(8,128)(2,1)S(1)}, bf16[1,256,1024]{2,1,0:T(8,128)(2,1)}, u32[]{:S(2)}) copy-start(bf16[1,256,1024]{2,1,0:T(8,128)(2,1)} %x_ref.1) | copy-start | bytes 1572868
  4.5 17.0 %copy-start.4 = (bf16[1,256,1024]{2,1,0:T(8,128)(2,1)S(1)}, bf16[1,256,1024]{2,1,0:T(8,128)(2,1)}, u32[]{:S(2)}) copy-start(bf16[1,256,1024]{2,1,0:T(8,128)(2,1)} %dy_ref.3) | copy-start | bytes 1572868
  6.2 13.1 %collective-permute-start.2 = (bf16[2,4,9216]{2,1,0:T(4,128)(2,1)S(1)}, bf16[2,4,9216]{2,1,0:T(4,128)(2,1)S(1)}, u32[]{:S(2)}, u32[]{:S(2)}) collective-permute-start(bf16[2,4,9216]{2,1,0:T(4,128)(2,1)S(1)} %get-tuple-element.19), channel_id=1, source_target_pairs={{0,4},{2,6},{4,0},{6,2},{8,12},{10,14},{12,8},{14,10},{16,20},{18,... | collective-permute-start | bytes 442376 | tf_op jit(solution)/shard_map/ppermute | solution.py:424
  6.5 12.8 %collective-permute-start.3 = (bf16[2,4,9216]{2,1,0:T(4,128)(2,1)S(1)}, bf16[2,4,9216]{2,1,0:T(4,128)(2,1)S(1)}, u32[]{:S(2)}, u32[]{:S(2)}) collective-permute-start(bf16[2,4,9216]{2,1,0:T(4,128)(2,1)S(1)} %get-tuple-element.20), channel_id=1, source_target_pairs={{0,24},{2,26},{4,28},{6,30},{8,16},{10,18},{12,20},{14,22},{16,8},... | collective-permute-start | bytes 442376 | tf_op jit(solution)/shard_map/ppermute | solution.py:424
  9.6 0.7 %copy-start.5 = (bf16[2,4,9216]{2,1,0:T(4,128)(2,1)}, bf16[2,4,9216]{2,1,0:T(4,128)(2,1)S(1)}, u32[]{:S(2)}) copy-start(bf16[2,4,9216]{2,1,0:T(4,128)(2,1)S(1)} %get-tuple-element.27.rest_7_) | copy-start | bytes 442372
  10.2 22.8 %collective-permute-start.5 = (bf16[2,4,9216]{2,1,0:T(4,128)(2,1)}, bf16[2,4,9216]{2,1,0:T(4,128)(2,1)}, u32[]{:S(2)}, u32[]{:S(2)}) collective-permute-start(bf16[2,4,9216]{2,1,0:T(4,128)(2,1)} %get-tuple-element.23), channel_id=1, source_target_pairs={{0,12},{2,14},{4,8},{6,10},{8,4},{10,6},{12,0},{14,2},{16,28},{18,... | collective-permute-start | bytes 442376 | tf_op jit(solution)/shard_map/ppermute | solution.py:424
  13.4 19.6 %collective-permute-start.6 = (bf16[2,4,9216]{2,1,0:T(4,128)(2,1)}, bf16[2,4,9216]{2,1,0:T(4,128)(2,1)}, u32[]{:S(2)}, u32[]{:S(2)}) collective-permute-start(bf16[2,4,9216]{2,1,0:T(4,128)(2,1)} %get-tuple-element.24), channel_id=1, source_target_pairs={{0,16},{2,18},{4,20},{6,22},{8,24},{10,26},{12,28},{14,30},{16,0},... | collective-permute-start | bytes 442376 | tf_op jit(solution)/shard_map/ppermute | solution.py:424
  17.1 16.0 %collective-permute-start.7 = (bf16[2,4,9216]{2,1,0:T(4,128)(2,1)}, bf16[2,4,9216]{2,1,0:T(4,128)(2,1)}, u32[]{:S(2)}, u32[]{:S(2)}) collective-permute-start(bf16[2,4,9216]{2,1,0:T(4,128)(2,1)} %get-tuple-element.25), channel_id=1, source_target_pairs={{0,20},{2,22},{4,16},{6,18},{8,28},{10,30},{12,24},{14,26},{16,4},... | collective-permute-start | bytes 442376 | tf_op jit(solution)/shard_map/ppermute | solution.py:424
  19.3 15.2 %collective-permute-start.8 = (bf16[2,4,9216]{2,1,0:T(4,128)(2,1)}, bf16[2,4,9216]{2,1,0:T(4,128)(2,1)S(1)}, u32[]{:S(2)}, u32[]{:S(2)}) collective-permute-start(bf16[2,4,9216]{2,1,0:T(4,128)(2,1)} %get-tuple-element.26), channel_id=1, source_target_pairs={{0,28},{2,30},{4,24},{6,26},{8,20},{10,22},{12,16},{14,18},{16,12}... | collective-permute-start | bytes 442376 | tf_op jit(solution)/shard_map/ppermute | solution.py:424
  19.3 15.2 %collective-permute-start.4 = (bf16[2,4,9216]{2,1,0:T(4,128)(2,1)S(1)}, bf16[2,4,9216]{2,1,0:T(4,128)(2,1)S(1)}, u32[]{:S(2)}, u32[]{:S(2)}) collective-permute-start(bf16[2,4,9216]{2,1,0:T(4,128)(2,1)S(1)} %get-tuple-element.22), channel_id=1, source_target_pairs={{0,8},{2,10},{4,12},{6,14},{8,0},{10,2},{12,4},{14,6},{16,24},{18,... | collective-permute-start | bytes 442376 | tf_op jit(solution)/shard_map/ppermute | solution.py:424
  26.3 8.3 %copy-start.2 = (f32[2,64,2]{1,2,0:T(2,128)S(1)}, f32[2,64,2]{1,2,0:T(2,128)}, u32[]{:S(2)}) copy-start(f32[2,64,2]{1,2,0:T(2,128)} %param.8) | copy-start | bytes 3076
  26.3 8.3 %copy-start.6 = (bf16[2,4,9216]{2,1,0:T(4,128)(2,1)S(1)}, bf16[2,4,9216]{2,1,0:T(4,128)(2,1)}, u32[]{:S(2)}) copy-start(bf16[2,4,9216]{2,1,0:T(4,128)(2,1)} %copy-done.5) | copy-start | bytes 442372
  26.3 34.5 %all-to-all-start = ((bf16[16,4,9216]{2,1,0:T(4,128)(2,1)}), bf16[16,4,9216]{2,1,0:T(4,128)(2,1)S(1)}, u32[]{:S(2)}, u32[]{:S(2)}) async-start(bf16[16,4,9216]{2,1,0:T(4,128)(2,1)} %kernel_grads.1.wire_ref), calls=%async_computation | async-start | bytes 2359296 | tf_op jit(solution)/shard_map/all_to_all | solution.py:486
  42.0 7.2 %collective-permute-start.9 = (bf16[144,1024]{1,0:T(8,128)(2,1)S(1)}, bf16[144,1024]{1,0:T(8,128)(2,1)S(1)}, u32[]{:S(2)}, u32[]{:S(2)}) collective-permute-start(bf16[144,1024]{1,0:T(8,128)(2,1)S(1)} %bitcast.23), channel_id=1, source_target_pairs={{0,1},{1,0},{2,3},{3,2},{4,5},{5,4},{6,7},{7,6},{8,9},{9,8},{10,11... | collective-permute-start | bytes 884744 | tf_op jit(solution)/shard_map/ppermute | solution.py:447
  50.1 12.7 %copy-start.7 = (bf16[1,256,1024]{2,1,0:T(8,128)(2,1)}, bf16[1,256,1024]{2,1,0:T(8,128)(2,1)S(1)}, u32[]{:S(2)}) copy-start(bf16[1,256,1024]{2,1,0:T(8,128)(2,1)S(1)} %fusion) | copy-start | bytes 1572868

commit v5 on v4

--- a/solution.py
+++ b/solution.py
@@ -32,19 +32,20 @@
 def pixel_masks(rows):
     pixel = lax.broadcasted_iota(jnp.int32, (rows, PIX), 1)
     column = pixel % SIDE
-    return {
-        "row": {-1: pixel >= SIDE, 1: pixel < PIX - SIDE},
-        "column": {-1: column > 0, 1: column < SIDE - 1},
-    }
+    in_row = {-1: pixel >= SIDE, 0: None, 1: pixel < PIX - SIDE}
+    in_column = {-1: column > 0, 0: None, 1: column < SIDE - 1}
+    masks = {}
+    for row_shift, row_mask in in_row.items():
+        for column_shift, column_mask in in_column.items():
+            both = [mask for mask in (row_mask, column_mask) if mask is not None]
+            masks[row_shift, column_shift] = both[0] & both[-1] if both else None
+    return masks
 
 
 def moved(values, row_shift, column_shift, masks):
     out = rolled(values, -(row_shift * SIDE + column_shift))
-    if row_shift:
-        out = jnp.where(masks["row"][row_shift], out, 0.0)
-    if column_shift:
-        out = jnp.where(masks["column"][column_shift], out, 0.0)
-    return out
+    mask = masks[row_shift, column_shift]
+    return out if mask is None else jnp.where(mask, out, 0.0)
 
 
 def joined(ref, start, count):

time: 63.1 us -> 63.1 us (level)
  no operation moved by 1% of the time
where the time goes in v5:
time: 63.1 us; the launch traced here: 62.8 us
  Pallas kernels  23.9 us (38%)
  starting transfers between devices  18.2 us (29%)
  waiting for transfers between devices  18.2 us (29%)
  local copies, waits for them, and re-layouts  1 us (2%)
  between operations  0.8 us (1%)
  other arithmetic  0.68 us (1%)
    all_to_all x1, waiting for transfers between devices, per_device(): lax.all_to_all(wire, 'grid', split_axis=0, concat_axis=0, tiled=True)  10.6 us
    ppermute x8, starting transfers between devices, swap(): return lax.ppermute(blocks, 'grid', [(i, i ^ step) for i in range(tiles)])  9.93 us
    pallas_call x1, Pallas kernels, per_device(): pl.pallas_call(functools.partial(adjoint_kernel, owned), out_shape=(jax.S...  7.41 us
    all_to_all x1, starting transfers between devices, per_device(): lax.all_to_all(wire, 'grid', split_axis=0, concat_axis=0, tiled=True)  6.7 us
    ppermute x2, waiting for transfers between devices, exchange(): lax.ppermute(blocks[step - 1], 'batch', [(i, (i + step) % batch) for i in...  6.02 us
    pallas_call x1, Pallas kernels, per_device(): pl.pallas_call(functools.partial(grads_kernel, owned, per_tile), out_shap...  4.77 us
    pallas_call x2, Pallas kernels, per_device(): pl.pallas_call(functools.partial(pack_kernel, owned, per_tile, some), out...  3.47 us
    pallas_call x1, Pallas kernels, per_device(): pl.pallas_call(functools.partial(tables_kernel, owned, per_tile), out_sha...  2.67 us
  transfers between devices with their start and end apart: 11, of which 4 were waited for; matrix products, arithmetic and copies ran while one was open for 2% of the time, Pallas kernels for 35%

profile of v5, /device:TPU:13, one launch (start us, length us, event | category | flops | bytes accessed | tf_op | source)
XLA Modules:
  0.0 62.8 jit_solution(12230253782612945361)
XLA Ops:
  0.6 0.0 copy-start
  0.6 0.0 copy-start.1
  0.7 0.7 %collective-permute-start.1 = (bf16[8,4,9216]{2,1,0:T(4,128)(2,1)}, bf16[8,4,9216]{2,1,0:T(4,128)(2,1)S(1)}, u32[]{:S(2)}, u32[]{:S(2)}) collective-permute-start(bf16[8,4,9216]{2,1,0:T(4,128)(2,1)} %own_ref.3), channel_id=1, source_target_pairs={{0,2},{2,0},{4,6},{6,4},{8,10},{10,8},{12,14},{14,12},{16,18},{18,... | collective-permute-start | bytes 1769480 | tf_op jit(solution)/shard_map/ppermute | solution.py:425
  1.4 1.8 %stage.1 = bf16[1,2,128,1024]{3,2,1,0:T(8,128)(2,1)} custom-call(bf16[1,256,1024]{2,1,0:T(8,128)(2,1)} %x_ref.1, bf16[1,256,1024]{2,1,0:T(8,128)(2,1)} %dy_ref.3), custom_call_target="tpu_custom_call" | custom-call | flops 20000000000 | bytes 1 | tf_op jit(solution)/shard_map/stage/pallas_call | solution.py:455
  3.2 1.3 %collective-permute-start = (bf16[2,128,1024]{2,1,0:T(8,128)(2,1)}, bf16[2,128,1024]{2,1,0:T(8,128)(2,1)S(1)}, u32[]{:S(2)}, u32[]{:S(2)}) collective-permute-start(bf16[2,128,1024]{2,1,0:T(8,128)(2,1)} %bitcast.24), channel_id=1, source_target_pairs={{0,1},{1,0},{2,3},{3,2},{4,5},{5,4},{6,7},{7,6},{8,9},{9,8},{10,11... | collective-permute-start | bytes 1572872 | tf_op jit(solution)/shard_map/ppermute | solution.py:448
  4.5 0.0 collective-permute-done.1.beside_ref
  4.5 0.0 copy-done
  4.5 0.0 copy-done.1
  4.5 0.0 copy-start.3
  4.5 0.0 copy-start.4
  4.5 1.7 %pack.2 = (bf16[2,4,9216]{2,1,0:T(4,128)(2,1)S(1)}, bf16[2,4,9216]{2,1,0:T(4,128)(2,1)S(1)}, bf16[2,4,9216]{2,1,0:T(4,128)(2,1)S(1)}) custom-call(s32[2,2,64]{2,1,0:T(2,128)S(1)} %bitcast.13, bf16[8,4,9216]{2,1,0:T(4,128)(2,1)S(1)} %copy-done, bf16[8,4,9216]{2,1,0:T(4,128)(2,1)S(1)} %collective-permute-done.1.beside_ref), custom_call_target="tpu_custom_call" | custom-call | tf_op jit(solution)/shard_map/pack/pallas_call | solution.py:432
  6.2 0.3 collective-permute-start.2
  6.5 1.3 %collective-permute-start.3 = (bf16[2,4,9216]{2,1,0:T(4,128)(2,1)S(1)}, bf16[2,4,9216]{2,1,0:T(4,128)(2,1)S(1)}, u32[]{:S(2)}, u32[]{:S(2)}) collective-permute-start(bf16[2,4,9216]{2,1,0:T(4,128)(2,1)S(1)} %get-tuple-element.20), channel_id=1, source_target_pairs={{0,24},{2,26},{4,28},{6,30},{8,16},{10,18},{12,20},{14,22},{16,8},... | collective-permute-start | bytes 442376 | tf_op jit(solution)/shard_map/ppermute | solution.py:425
  7.8 1.8 %pack.3 = (bf16[2,4,9216]{2,1,0:T(4,128)(2,1)}, bf16[2,4,9216]{2,1,0:T(4,128)(2,1)}, bf16[2,4,9216]{2,1,0:T(4,128)(2,1)}, bf16[2,4,9216]{2,1,0:T(4,128)(2,1)}, bf16[2,4,9216]{2,1,0:T(4,128)(2,1)S(1)}) custom-call(s32[2,2,64]{2,1,0:T(2,128)S(1)} %bitcast.14, bf16[8,4,9216]{2,1,0:T(4,128)(2,1)S(1)} %copy-done, ...), custom_call_target="tpu_custom_call" | custom-call | tf_op jit(solution)/shard_map/pack/pallas_call | solution.py:432
  9.6 0.0 copy-start.5
  9.6 0.7 %copy-done.5 = bf16[2,4,9216]{2,1,0:T(4,128)(2,1)} copy-done((bf16[2,4,9216]{2,1,0:T(4,128)(2,1)}, bf16[2,4,9216]{2,1,0:T(4,128)(2,1)S(1)}, u32[]{:S(2)}) %copy-start.5) | copy-done | bytes 147480
  10.2 3.2 %collective-permute-start.5 = (bf16[2,4,9216]{2,1,0:T(4,128)(2,1)}, bf16[2,4,9216]{2,1,0:T(4,128)(2,1)}, u32[]{:S(2)}, u32[]{:S(2)}) collective-permute-start(bf16[2,4,9216]{2,1,0:T(4,128)(2,1)} %get-tuple-element.23), channel_id=1, source_target_pairs={{0,12},{2,14},{4,8},{6,10},{8,4},{10,6},{12,0},{14,2},{16,28},{18,... | collective-permute-start | bytes 442376 | tf_op jit(solution)/shard_map/ppermute | solution.py:425
  13.4 0.0 collective-permute-start.6
  13.4 3.7 %collective-permute-done = bf16[2,128,1024]{2,1,0:T(8,128)(2,1)S(1)} collective-permute-done((bf16[2,128,1024]{2,1,0:T(8,128)(2,1)}, bf16[2,128,1024]{2,1,0:T(8,128)(2,1)S(1)}, u32[]{:S(2)}, u32[]{:S(2)}) %collective-permute-start) | collective-permute-done | bytes 524320 | tf_op jit(solution)/shard_map/ppermute | solution.py:448
  17.1 2.3 %collective-permute-start.7 = (bf16[2,4,9216]{2,1,0:T(4,128)(2,1)}, bf16[2,4,9216]{2,1,0:T(4,128)(2,1)}, u32[]{:S(2)}, u32[]{:S(2)}) collective-permute-start(bf16[2,4,9216]{2,1,0:T(4,128)(2,1)} %get-tuple-element.25), channel_id=1, source_target_pairs={{0,20},{2,22},{4,16},{6,18},{8,28},{10,30},{12,24},{14,26},{16,4},... | collective-permute-start | bytes 442376 | tf_op jit(solution)/shard_map/ppermute | solution.py:425
  19.3 0.0 collective-permute-done.2.rest_0_
  19.3 0.0 collective-permute-start.8
  19.3 0.0 collective-permute-done.3.rest_1_
  19.3 2.2 %collective-permute-start.4 = (bf16[2,4,9216]{2,1,0:T(4,128)(2,1)S(1)}, bf16[2,4,9216]{2,1,0:T(4,128)(2,1)S(1)}, u32[]{:S(2)}, u32[]{:S(2)}) collective-permute-start(bf16[2,4,9216]{2,1,0:T(4,128)(2,1)S(1)} %get-tuple-element.22), channel_id=1, source_target_pairs={{0,8},{2,10},{4,12},{6,14},{8,0},{10,2},{12,4},{14,6},{16,24},{18,... | collective-permute-start | bytes 442376 | tf_op jit(solution)/shard_map/ppermute | solution.py:425
  21.5 0.0 copy-done.3
  21.5 0.0 copy-done.4
  21.5 4.8 %kernel_grads.1.wire_ref = bf16[16,4,9216]{2,1,0:T(4,128)(2,1)} custom-call(s32[2,2,64]{2,1,0:T(2,128)S(1)} %bitcast.15, bf16[1,256,1024]{2,1,0:T(8,128)(2,1)S(1)} %copy-done.3, bf16[1,256,1024]{2,1,0:T(8,128)(2,1)S(1)} %copy-done.4, bf16[1,2,128,1024]{3,2,1,0:T(8,128)(2,1)S(1)} %bitcast.21), custom_call_target="tpu_custom_call" | custom-call | flops 20000000000 | bytes 1 | tf_op jit(solution)/shard_map/kernel_grads/pallas_call | solution.py:475
  26.3 6.7 %all-to-all-start = ((bf16[16,4,9216]{2,1,0:T(4,128)(2,1)}), bf16[16,4,9216]{2,1,0:T(4,128)(2,1)S(1)}, u32[]{:S(2)}, u32[]{:S(2)}) async-start(bf16[16,4,9216]{2,1,0:T(4,128)(2,1)} %kernel_grads.1.wire_ref), calls=%async_computation | async-start | bytes 2359296 | tf_op jit(solution)/shard_map/all_to_all | solution.py:487
  33.0 0.0 collective-permute-done.5.rest_3_
  33.0 0.0 collective-permute-done.6.rest_4_
  33.0 0.0 collective-permute-done.7.rest_5_
  33.0 1.5 %collective-permute-done.8.rest_6_ = bf16[2,4,9216]{2,1,0:T(4,128)(2,1)S(1)} collective-permute-done((bf16[2,4,9216]{2,1,0:T(4,128)(2,1)}, bf16[2,4,9216]{2,1,0:T(4,128)(2,1)S(1)}, u32[]{:S(2)}, u32[]{:S(2)}) %collective-permute-start.8) | collective-permute-done | bytes 147488 | tf_op jit(solution)/shard_map/ppermute | solution.py:425
  34.6 0.0 collective-permute-done.4.rest_2_
  34.6 0.0 copy-done.2
  34.6 0.0 copy-done.6
  34.6 7.4 %adjoint.1 = (bf16[1,144,1024]{2,1,0:T(8,128)(2,1)S(1)}, bf16[16,128]{1,0:T(8,128)(2,1)S(1)}, f32[2,3,256,128]{3,2,1,0:T(8,128)S(1)}) custom-call(s32[2,2,64]{2,1,0:T(2,128)S(1)} %bitcast.16, f32[2,2,64]{2,1,0:T(2,128)S(1)} %bitcast.18, bf16[16,4,9216]{2,1,0:T(4,128)(2,1)} %kernel_grads.1.wire_ref, bf16[1,2,128,1024]{3,2,1,0:T(8,128)(2,1)S(1)} %bitcast.22, ...), custom_call_target="tpu_custom_call" | custom-call | flops 20000000000 | bytes 1 | tf_op jit(solution)/shard_map/adjoint/pallas_call | solution.py:490
  42.0 0.3 collective-permute-start.9
  42.3 2.7 %tables.1 = (s32[16]{0:T(128)S(1)}, f32[16,4,128]{2,1,0:T(4,128)S(1)}) custom-call(s32[2,2,64]{2,1,0:T(2,128)S(1)} %bitcast.17, f32[2,2,64]{2,1,0:T(2,128)S(1)} %bitcast.19), custom_call_target="tpu_custom_call" | custom-call | tf_op jit(solution)/shard_map/tables/pallas_call | solution.py:527
  45.0 1.7 %own_adjoint.1 = bf16[128,1024]{1,0:T(8,128)(2,1)S(1)} custom-call(f32[2,3,256,128]{3,2,1,0:T(8,128)S(1)} %get-tuple-element.28.mixed_ref, bf16[1,256,1024]{2,1,0:T(8,128)(2,1)S(1)} %copy-done.4), custom_call_target="tpu_custom_call" | custom-call | flops 1000000000 | bytes 1 | tf_op jit(solution)/shard_map/own_adjoint/pallas_call | solution.py:515
  46.7 0.1 broadcast_in_dim.9
  46.8 2.4 %collective-permute-done.9 = bf16[144,1024]{1,0:T(8,128)(2,1)S(1)} collective-permute-done((bf16[144,1024]{1,0:T(8,128)(2,1)S(1)}, bf16[144,1024]{1,0:T(8,128)(2,1)S(1)}, u32[]{:S(2)}, u32[]{:S(2)}) %collective-permute-start.9) | collective-permute-done | bytes 294944 | tf_op jit(solution)/shard_map/ppermute | solution.py:448
  49.2 0.1 slice.20
  49.3 0.1 copy.9
  49.4 0.7 %fusion.2 = f32[2,4,2]{1,2,0:T(2,128)} fusion(f32[2,4,2]{1,2,0:T(2,128)S(1)} %copy.9, f32[2,2,64]{2,1,0:T(2,128)S(1)} %bitcast.20, s32[]{:T(128)S(6)} %select_n.11), kind=kLoop, calls=%fused_computation.5 | loop fusion | flops 112 | bytes 196 | tf_op jit(solution)/shard_map/div | solution.py:553
  50.1 0.0 copy-start.7
  50.1 10.6 %all-to-all-done.got_ref = bf16[16,4,9216]{2,1,0:T(4,128)(2,1)S(1)} async-done(((bf16[16,4,9216]{2,1,0:T(4,128)(2,1)}), bf16[16,4,9216]{2,1,0:T(4,128)(2,1)S(1)}, u32[]{:S(2)}, u32[]{:S(2)}) %all-to-all-start) | async-done | bytes 1179680 | tf_op jit(solution)/shard_map/all_to_all | solution.py:487
  60.7 2.1 %weight_sum.1 = f32[8,4,9216]{2,1,0:T(4,128)} custom-call(s32[16]{0:T(128)S(1)} %get-tuple-element.33.local_ref, f32[16,4,128]{2,1,0:T(4,128)S(1)} %get-tuple-element.34.gate_ref, bf16[16,4,9216]{2,1,0:T(4,128)(2,1)S(1)} %all-to-all-done.got_ref), custom_call_target="tpu_custom_call" | custom-call | tf_op jit(solution)/shard_map/weight_sum/pallas_call | solution.py:555
  62.8 0.0 copy-done.7
  (6 shorter events, 0.1 us)
Async XLA Ops:
  0.6 3.8 %copy-start = (bf16[8,4,9216]{2,1,0:T(4,128)(2,1)S(1)}, bf16[8,4,9216]{2,1,0:T(4,128)(2,1)}, u32[]{:S(2)}) copy-start(bf16[8,4,9216]{2,1,0:T(4,128)(2,1)} %own_ref.3) | copy-start | bytes 1769476
  0.6 3.8 %copy-start.1 = (s32[2,64,2]{1,2,0:T(2,128)S(1)}, s32[2,64,2]{1,2,0:T(2,128)}, u32[]{:S(2)}) copy-start(s32[2,64,2]{1,2,0:T(2,128)} %param.9) | copy-start | bytes 3076
  0.7 3.8 %collective-permute-start.1 = (bf16[8,4,9216]{2,1,0:T(4,128)(2,1)}, bf16[8,4,9216]{2,1,0:T(4,128)(2,1)S(1)}, u32[]{:S(2)}, u32[]{:S(2)}) collective-permute-start(bf16[8,4,9216]{2,1,0:T(4,128)(2,1)} %own_ref.3), channel_id=1, source_target_pairs={{0,2},{2,0},{4,6},{6,4},{8,10},{10,8},{12,14},{14,12},{16,18},{18,... | collective-permute-start | bytes 1769480 | tf_op jit(solution)/shard_map/ppermute | solution.py:425
  3.2 13.9 %collective-permute-start = (bf16[2,128,1024]{2,1,0:T(8,128)(2,1)}, bf16[2,128,1024]{2,1,0:T(8,128)(2,1)S(1)}, u32[]{:S(2)}, u32[]{:S(2)}) collective-permute-start(bf16[2,128,1024]{2,1,0:T(8,128)(2,1)} %bitcast.24), channel_id=1, source_target_pairs={{0,1},{1,0},{2,3},{3,2},{4,5},{5,4},{6,7},{7,6},{8,9},{9,8},{10,11... | collective-permute-start | bytes 1572872 | tf_op jit(solution)/shard_map/ppermute | solution.py:448
  4.5 17.0 %copy-start.3 = (bf16[1,256,1024]{2,1,0:T(8,128)(2,1)S(1)}, bf16[1,256,1024]{2,1,0:T(8,128)(2,1)}, u32[]{:S(2)}) copy-start(bf16[1,256,1024]{2,1,0:T(8,128)(2,1)} %x_ref.1) | copy-start | bytes 1572868
  4.5 17.0 %copy-start.4 = (bf16[1,256,1024]{2,1,0:T(8,128)(2,1)S(1)}, bf16[1,256,1024]{2,1,0:T(8,128)(2,1)}, u32[]{:S(2)}) copy-start(bf16[1,256,1024]{2,1,0:T(8,128)(2,1)} %dy_ref.3) | copy-start | bytes 1572868
  6.2 13.1 %collective-permute-start.2 = (bf16[2,4,9216]{2,1,0:T(4,128)(2,1)S(1)}, bf16[2,4,9216]{2,1,0:T(4,128)(2,1)S(1)}, u32[]{:S(2)}, u32[]{:S(2)}) collective-permute-start(bf16[2,4,9216]{2,1,0:T(4,128)(2,1)S(1)} %get-tuple-element.19), channel_id=1, source_target_pairs={{0,4},{2,6},{4,0},{6,2},{8,12},{10,14},{12,8},{14,10},{16,20},{18,... | collective-permute-start | bytes 442376 | tf_op jit(solution)/shard_map/ppermute | solution.py:425
  6.5 12.8 %collective-permute-start.3 = (bf16[2,4,9216]{2,1,0:T(4,128)(2,1)S(1)}, bf16[2,4,9216]{2,1,0:T(4,128)(2,1)S(1)}, u32[]{:S(2)}, u32[]{:S(2)}) collective-permute-start(bf16[2,4,9216]{2,1,0:T(4,128)(2,1)S(1)} %get-tuple-element.20), channel_id=1, source_target_pairs={{0,24},{2,26},{4,28},{6,30},{8,16},{10,18},{12,20},{14,22},{16,8},... | collective-permute-start | bytes 442376 | tf_op jit(solution)/shard_map/ppermute | solution.py:425
  9.6 0.7 %copy-start.5 = (bf16[2,4,9216]{2,1,0:T(4,128)(2,1)}, bf16[2,4,9216]{2,1,0:T(4,128)(2,1)S(1)}, u32[]{:S(2)}) copy-start(bf16[2,4,9216]{2,1,0:T(4,128)(2,1)S(1)} %get-tuple-element.27.rest_7_) | copy-start | bytes 442372
  10.2 22.8 %collective-permute-start.5 = (bf16[2,4,9216]{2,1,0:T(4,128)(2,1)}, bf16[2,4,9216]{2,1,0:T(4,128)(2,1)}, u32[]{:S(2)}, u32[]{:S(2)}) collective-permute-start(bf16[2,4,9216]{2,1,0:T(4,128)(2,1)} %get-tuple-element.23), channel_id=1, source_target_pairs={{0,12},{2,14},{4,8},{6,10},{8,4},{10,6},{12,0},{14,2},{16,28},{18,... | collective-permute-start | bytes 442376 | tf_op jit(solution)/shard_map/ppermute | solution.py:425
  13.4 19.6 %collective-permute-start.6 = (bf16[2,4,9216]{2,1,0:T(4,128)(2,1)}, bf16[2,4,9216]{2,1,0:T(4,128)(2,1)}, u32[]{:S(2)}, u32[]{:S(2)}) collective-permute-start(bf16[2,4,9216]{2,1,0:T(4,128)(2,1)} %get-tuple-element.24), channel_id=1, source_target_pairs={{0,16},{2,18},{4,20},{6,22},{8,24},{10,26},{12,28},{14,30},{16,0},... | collective-permute-start | bytes 442376 | tf_op jit(solution)/shard_map/ppermute | solution.py:425
  17.1 16.0 %collective-permute-start.7 = (bf16[2,4,9216]{2,1,0:T(4,128)(2,1)}, bf16[2,4,9216]{2,1,0:T(4,128)(2,1)}, u32[]{:S(2)}, u32[]{:S(2)}) collective-permute-start(bf16[2,4,9216]{2,1,0:T(4,128)(2,1)} %get-tuple-element.25), channel_id=1, source_target_pairs={{0,20},{2,22},{4,16},{6,18},{8,28},{10,30},{12,24},{14,26},{16,4},... | collective-permute-start | bytes 442376 | tf_op jit(solution)/shard_map/ppermute | solution.py:425
  19.3 15.2 %collective-permute-start.8 = (bf16[2,4,9216]{2,1,0:T(4,128)(2,1)}, bf16[2,4,9216]{2,1,0:T(4,128)(2,1)S(1)}, u32[]{:S(2)}, u32[]{:S(2)}) collective-permute-start(bf16[2,4,9216]{2,1,0:T(4,128)(2,1)} %get-tuple-element.26), channel_id=1, source_target_pairs={{0,28},{2,30},{4,24},{6,26},{8,20},{10,22},{12,16},{14,18},{16,12}... | collective-permute-start | bytes 442376 | tf_op jit(solution)/shard_map/ppermute | solution.py:425
  19.3 15.2 %collective-permute-start.4 = (bf16[2,4,9216]{2,1,0:T(4,128)(2,1)S(1)}, bf16[2,4,9216]{2,1,0:T(4,128)(2,1)S(1)}, u32[]{:S(2)}, u32[]{:S(2)}) collective-permute-start(bf16[2,4,9216]{2,1,0:T(4,128)(2,1)S(1)} %get-tuple-element.22), channel_id=1, source_target_pairs={{0,8},{2,10},{4,12},{6,14},{8,0},{10,2},{12,4},{14,6},{16,24},{18,... | collective-permute-start | bytes 442376 | tf_op jit(solution)/shard_map/ppermute | solution.py:425
  26.3 8.3 %copy-start.2 = (f32[2,64,2]{1,2,0:T(2,128)S(1)}, f32[2,64,2]{1,2,0:T(2,128)}, u32[]{:S(2)}) copy-start(f32[2,64,2]{1,2,0:T(2,128)} %param.8) | copy-start | bytes 3076
  26.3 8.3 %copy-start.6 = (bf16[2,4,9216]{2,1,0:T(4,128)(2,1)S(1)}, bf16[2,4,9216]{2,1,0:T(4,128)(2,1)}, u32[]{:S(2)}) copy-start(bf16[2,4,9216]{2,1,0:T(4,128)(2,1)} %copy-done.5) | copy-start | bytes 442372
  26.3 34.5 %all-to-all-start = ((bf16[16,4,9216]{2,1,0:T(4,128)(2,1)}), bf16[16,4,9216]{2,1,0:T(4,128)(2,1)S(1)}, u32[]{:S(2)}, u32[]{:S(2)}) async-start(bf16[16,4,9216]{2,1,0:T(4,128)(2,1)} %kernel_grads.1.wire_ref), calls=%async_computation | async-start | bytes 2359296 | tf_op jit(solution)/shard_map/all_to_all | solution.py:487
  42.0 7.2 %collective-permute-start.9 = (bf16[144,1024]{1,0:T(8,128)(2,1)S(1)}, bf16[144,1024]{1,0:T(8,128)(2,1)S(1)}, u32[]{:S(2)}, u32[]{:S(2)}) collective-permute-start(bf16[144,1024]{1,0:T(8,128)(2,1)S(1)} %bitcast.23), channel_id=1, source_target_pairs={{0,1},{1,0},{2,3},{3,2},{4,5},{5,4},{6,7},{7,6},{8,9},{9,8},{10,11... | collective-permute-start | bytes 884744 | tf_op jit(solution)/shard_map/ppermute | solution.py:448
  50.1 12.7 %copy-start.7 = (bf16[1,256,1024]{2,1,0:T(8,128)(2,1)}, bf16[1,256,1024]{2,1,0:T(8,128)(2,1)S(1)}, u32[]{:S(2)}) copy-start(bf16[1,256,1024]{2,1,0:T(8,128)(2,1)S(1)} %fusion) | copy-start | bytes 1572868

commit v6 on v5

--- a/solution.py
+++ b/solution.py
@@ -16,7 +16,7 @@
 QUAD = 4 * ROW
 ROWS = 8
 DOT_ROWS = 16
-VMEM_LIMIT = 16 * 1024 * 1024
+VMEM_LIMIT = 40 * 1024 * 1024
 WHOLE_VMEM = 60 * 1024 * 1024
 EARLY = 3
 SUM_CHUNKS = 3
@@ -67,7 +67,7 @@
 def pair_order(tiles):
     near, far = list(range(tiles // 4)), list(range(tiles // 4, tiles // 2))
     first = far.pop(len(far) // 2)
-    return near[1:2] + [first] + near[2:] + far + near[:1]
+    return [first] + near[1:2] + near[2:] + far + near[:1]
 
 
 def tree_sum(values):

time: 63.1 us -> 63.1 us (level)
    all_to_all x1, waiting for transfers between devices: 10.6 us -> 11.7 us  [per_device(): lax.all_to_all(wire, 'grid', split_axis=0, concat_axis=0, tiled=True)]
    ppermute x2, waiting for transfers between devices: 6.02 us -> 5.2 us  [exchange(): lax.ppermute(blocks[step - 1], 'batch', [(i, (i + step) % batch) for i in...]
    ppermute x8, waiting for transfers between devices: 1.56 us -> 0.8 us  [swap(): return lax.ppermute(blocks, 'grid', [(i, i ^ step) for i in range(tiles)])]
where the time goes in v6:
time: 63.1 us; the launch traced here: 62.8 us
  Pallas kernels  23.9 us (38%)
  starting transfers between devices  18.8 us (30%)
  waiting for transfers between devices  17.7 us (28%)
  local copies, waits for them, and re-layouts  1 us (2%)
  between operations  0.8 us (1%)
  other arithmetic  0.68 us (1%)
    all_to_all x1, waiting for transfers between devices, per_device(): lax.all_to_all(wire, 'grid', split_axis=0, concat_axis=0, tiled=True)  11.7 us
    ppermute x8, starting transfers between devices, swap(): return lax.ppermute(blocks, 'grid', [(i, i ^ step) for i in range(tiles)])  9.93 us
    pallas_call x1, Pallas kernels, per_device(): pl.pallas_call(functools.partial(adjoint_kernel, owned), out_shape=(jax.S...  7.42 us
    all_to_all x1, starting transfers between devices, per_device(): lax.all_to_all(wire, 'grid', split_axis=0, concat_axis=0, tiled=True)  6.7 us
    ppermute x2, waiting for transfers between devices, exchange(): lax.ppermute(blocks[step - 1], 'batch', [(i, (i + step) % batch) for i in...  5.2 us
    pallas_call x1, Pallas kernels, per_device(): pl.pallas_call(functools.partial(grads_kernel, owned, per_tile), out_shap...  4.77 us
    pallas_call x2, Pallas kernels, per_device(): pl.pallas_call(functools.partial(pack_kernel, owned, per_tile, some), out...  3.47 us
    pallas_call x1, Pallas kernels, per_device(): pl.pallas_call(functools.partial(tables_kernel, owned, per_tile), out_sha...  2.67 us
  transfers between devices with their start and end apart: 11, of which 4 were waited for; matrix products, arithmetic and copies ran while one was open for 2% of the time, Pallas kernels for 35%

profile of v6, /device:TPU:13, one launch (start us, length us, event | category | flops | bytes accessed | tf_op | source)
XLA Modules:
  0.0 62.8 jit_solution(15181218545213038349)
XLA Ops:
  0.6 0.0 copy-start
  0.6 0.0 copy-start.1
  0.7 0.7 %collective-permute-start.1 = (bf16[8,4,9216]{2,1,0:T(4,128)(2,1)}, bf16[8,4,9216]{2,1,0:T(4,128)(2,1)S(1)}, u32[]{:S(2)}, u32[]{:S(2)}) collective-permute-start(bf16[8,4,9216]{2,1,0:T(4,128)(2,1)} %own_ref.3), channel_id=1, source_target_pairs={{0,2},{2,0},{4,6},{6,4},{8,10},{10,8},{12,14},{14,12},{16,18},{18,... | collective-permute-start | bytes 1769480 | tf_op jit(solution)/shard_map/ppermute | solution.py:425
  1.4 1.8 %stage.1 = bf16[1,2,128,1024]{3,2,1,0:T(8,128)(2,1)} custom-call(bf16[1,256,1024]{2,1,0:T(8,128)(2,1)} %x_ref.1, bf16[1,256,1024]{2,1,0:T(8,128)(2,1)} %dy_ref.3), custom_call_target="tpu_custom_call" | custom-call | flops 20000000000 | bytes 1 | tf_op jit(solution)/shard_map/stage/pallas_call | solution.py:455
  3.2 1.3 %collective-permute-start = (bf16[2,128,1024]{2,1,0:T(8,128)(2,1)}, bf16[2,128,1024]{2,1,0:T(8,128)(2,1)S(1)}, u32[]{:S(2)}, u32[]{:S(2)}) collective-permute-start(bf16[2,128,1024]{2,1,0:T(8,128)(2,1)} %bitcast.24), channel_id=1, source_target_pairs={{0,1},{1,0},{2,3},{3,2},{4,5},{5,4},{6,7},{7,6},{8,9},{9,8},{10,11... | collective-permute-start | bytes 1572872 | tf_op jit(solution)/shard_map/ppermute | solution.py:448
  4.5 0.0 collective-permute-done.1.beside_ref
  4.5 0.0 copy-done
  4.5 0.0 copy-done.1
  4.5 0.0 copy-start.3
  4.5 0.0 copy-start.4
  4.5 1.7 %pack.2 = (bf16[2,4,9216]{2,1,0:T(4,128)(2,1)S(1)}, bf16[2,4,9216]{2,1,0:T(4,128)(2,1)S(1)}, bf16[2,4,9216]{2,1,0:T(4,128)(2,1)S(1)}) custom-call(s32[2,2,64]{2,1,0:T(2,128)S(1)} %bitcast.13, bf16[8,4,9216]{2,1,0:T(4,128)(2,1)S(1)} %copy-done, bf16[8,4,9216]{2,1,0:T(4,128)(2,1)S(1)} %collective-permute-done.1.beside_ref), custom_call_target="tpu_custom_call" | custom-call | tf_op jit(solution)/shard_map/pack/pallas_call | solution.py:432
  6.2 1.4 %collective-permute-start.2 = (bf16[2,4,9216]{2,1,0:T(4,128)(2,1)S(1)}, bf16[2,4,9216]{2,1,0:T(4,128)(2,1)S(1)}, u32[]{:S(2)}, u32[]{:S(2)}) collective-permute-start(bf16[2,4,9216]{2,1,0:T(4,128)(2,1)S(1)} %get-tuple-element.19), channel_id=1, source_target_pairs={{0,24},{2,26},{4,28},{6,30},{8,16},{10,18},{12,20},{14,22},{16,8},... | collective-permute-start | bytes 442376 | tf_op jit(solution)/shard_map/ppermute | solution.py:425
  7.6 0.2 collective-permute-start.3
  7.8 1.8 %pack.3 = (bf16[2,4,9216]{2,1,0:T(4,128)(2,1)}, bf16[2,4,9216]{2,1,0:T(4,128)(2,1)}, bf16[2,4,9216]{2,1,0:T(4,128)(2,1)}, bf16[2,4,9216]{2,1,0:T(4,128)(2,1)}, bf16[2,4,9216]{2,1,0:T(4,128)(2,1)S(1)}) custom-call(s32[2,2,64]{2,1,0:T(2,128)S(1)} %bitcast.14, bf16[8,4,9216]{2,1,0:T(4,128)(2,1)S(1)} %copy-done, ...), custom_call_target="tpu_custom_call" | custom-call | tf_op jit(solution)/shard_map/pack/pallas_call | solution.py:432
  9.6 0.0 copy-start.5
  9.6 0.7 %copy-done.5 = bf16[2,4,9216]{2,1,0:T(4,128)(2,1)} copy-done((bf16[2,4,9216]{2,1,0:T(4,128)(2,1)}, bf16[2,4,9216]{2,1,0:T(4,128)(2,1)S(1)}, u32[]{:S(2)}) %copy-start.5) | copy-done | bytes 147480
  10.2 3.2 %collective-permute-start.5 = (bf16[2,4,9216]{2,1,0:T(4,128)(2,1)}, bf16[2,4,9216]{2,1,0:T(4,128)(2,1)}, u32[]{:S(2)}, u32[]{:S(2)}) collective-permute-start(bf16[2,4,9216]{2,1,0:T(4,128)(2,1)} %get-tuple-element.23), channel_id=1, source_target_pairs={{0,12},{2,14},{4,8},{6,10},{8,4},{10,6},{12,0},{14,2},{16,28},{18,... | collective-permute-start | bytes 442376 | tf_op jit(solution)/shard_map/ppermute | solution.py:425
  13.4 0.0 collective-permute-start.6
  13.4 3.7 %collective-permute-done = bf16[2,128,1024]{2,1,0:T(8,128)(2,1)S(1)} collective-permute-done((bf16[2,128,1024]{2,1,0:T(8,128)(2,1)}, bf16[2,128,1024]{2,1,0:T(8,128)(2,1)S(1)}, u32[]{:S(2)}, u32[]{:S(2)}) %collective-permute-start) | collective-permute-done | bytes 524320 | tf_op jit(solution)/shard_map/ppermute | solution.py:448
  17.1 2.3 %collective-permute-start.7 = (bf16[2,4,9216]{2,1,0:T(4,128)(2,1)}, bf16[2,4,9216]{2,1,0:T(4,128)(2,1)}, u32[]{:S(2)}, u32[]{:S(2)}) collective-permute-start(bf16[2,4,9216]{2,1,0:T(4,128)(2,1)} %get-tuple-element.25), channel_id=1, source_target_pairs={{0,20},{2,22},{4,16},{6,18},{8,28},{10,30},{12,24},{14,26},{16,4},... | collective-permute-start | bytes 442376 | tf_op jit(solution)/shard_map/ppermute | solution.py:425
  19.3 0.0 collective-permute-done.2.rest_0_
  19.3 0.0 collective-permute-start.8
  19.3 0.0 collective-permute-done.3.rest_1_
  19.3 2.2 %collective-permute-start.4 = (bf16[2,4,9216]{2,1,0:T(4,128)(2,1)S(1)}, bf16[2,4,9216]{2,1,0:T(4,128)(2,1)S(1)}, u32[]{:S(2)}, u32[]{:S(2)}) collective-permute-start(bf16[2,4,9216]{2,1,0:T(4,128)(2,1)S(1)} %get-tuple-element.22), channel_id=1, source_target_pairs={{0,8},{2,10},{4,12},{6,14},{8,0},{10,2},{12,4},{14,6},{16,24},{18,... | collective-permute-start | bytes 442376 | tf_op jit(solution)/shard_map/ppermute | solution.py:425
  21.5 0.0 copy-done.3
  21.5 0.0 copy-done.4
  21.5 4.8 %kernel_grads.1.wire_ref = bf16[16,4,9216]{2,1,0:T(4,128)(2,1)} custom-call(s32[2,2,64]{2,1,0:T(2,128)S(1)} %bitcast.15, bf16[1,256,1024]{2,1,0:T(8,128)(2,1)S(1)} %copy-done.3, bf16[1,256,1024]{2,1,0:T(8,128)(2,1)S(1)} %copy-done.4, bf16[1,2,128,1024]{3,2,1,0:T(8,128)(2,1)S(1)} %bitcast.21), custom_call_target="tpu_custom_call" | custom-call | flops 20000000000 | bytes 1 | tf_op jit(solution)/shard_map/kernel_grads/pallas_call | solution.py:475
  26.3 6.7 %all-to-all-start = ((bf16[16,4,9216]{2,1,0:T(4,128)(2,1)}), bf16[16,4,9216]{2,1,0:T(4,128)(2,1)S(1)}, u32[]{:S(2)}, u32[]{:S(2)}) async-start(bf16[16,4,9216]{2,1,0:T(4,128)(2,1)} %kernel_grads.1.wire_ref), calls=%async_computation | async-start | bytes 2359296 | tf_op jit(solution)/shard_map/all_to_all | solution.py:487
  33.0 0.0 collective-permute-done.5.rest_3_
  33.0 0.0 collective-permute-done.6.rest_4_
  33.0 0.0 collective-permute-done.7.rest_5_
  33.0 0.8 %collective-permute-done.8.rest_6_ = bf16[2,4,9216]{2,1,0:T(4,128)(2,1)S(1)} collective-permute-done((bf16[2,4,9216]{2,1,0:T(4,128)(2,1)}, bf16[2,4,9216]{2,1,0:T(4,128)(2,1)S(1)}, u32[]{:S(2)}, u32[]{:S(2)}) %collective-permute-start.8) | collective-permute-done | bytes 147488 | tf_op jit(solution)/shard_map/ppermute | solution.py:425
  33.8 0.0 collective-permute-done.4.rest_2_
  33.8 0.0 copy-done.2
  33.8 0.0 copy-done.6
  33.8 7.4 %adjoint.1 = (bf16[1,144,1024]{2,1,0:T(8,128)(2,1)S(1)}, bf16[16,128]{1,0:T(8,128)(2,1)S(1)}, f32[2,3,256,128]{3,2,1,0:T(8,128)S(1)}) custom-call(s32[2,2,64]{2,1,0:T(2,128)S(1)} %bitcast.16, f32[2,2,64]{2,1,0:T(2,128)S(1)} %bitcast.18, bf16[16,4,9216]{2,1,0:T(4,128)(2,1)} %kernel_grads.1.wire_ref, bf16[1,2,128,1024]{3,2,1,0:T(8,128)(2,1)S(1)} %bitcast.22, ...), custom_call_target="tpu_custom_call" | custom-call | flops 20000000000 | bytes 1 | tf_op jit(solution)/shard_map/adjoint/pallas_call | solution.py:490
  41.2 0.8 %collective-permute-start.9 = (bf16[144,1024]{1,0:T(8,128)(2,1)S(1)}, bf16[144,1024]{1,0:T(8,128)(2,1)S(1)}, u32[]{:S(2)}, u32[]{:S(2)}) collective-permute-start(bf16[144,1024]{1,0:T(8,128)(2,1)S(1)} %bitcast.23), channel_id=1, source_target_pairs={{0,1},{1,0},{2,3},{3,2},{4,5},{5,4},{6,7},{7,6},{8,9},{9,8},{10,11... | collective-permute-start | bytes 884744 | tf_op jit(solution)/shard_map/ppermute | solution.py:448
  42.1 2.7 %tables.1 = (s32[16]{0:T(128)S(1)}, f32[16,4,128]{2,1,0:T(4,128)S(1)}) custom-call(s32[2,2,64]{2,1,0:T(2,128)S(1)} %bitcast.17, f32[2,2,64]{2,1,0:T(2,128)S(1)} %bitcast.19), custom_call_target="tpu_custom_call" | custom-call | tf_op jit(solution)/shard_map/tables/pallas_call | solution.py:527
  44.8 1.7 %own_adjoint.1 = bf16[128,1024]{1,0:T(8,128)(2,1)S(1)} custom-call(f32[2,3,256,128]{3,2,1,0:T(8,128)S(1)} %get-tuple-element.28.mixed_ref, bf16[1,256,1024]{2,1,0:T(8,128)(2,1)S(1)} %copy-done.4), custom_call_target="tpu_custom_call" | custom-call | flops 1000000000 | bytes 1 | tf_op jit(solution)/shard_map/own_adjoint/pallas_call | solution.py:515
  46.5 0.1 broadcast_in_dim.9
  46.6 1.5 %collective-permute-done.9 = bf16[144,1024]{1,0:T(8,128)(2,1)S(1)} collective-permute-done((bf16[144,1024]{1,0:T(8,128)(2,1)S(1)}, bf16[144,1024]{1,0:T(8,128)(2,1)S(1)}, u32[]{:S(2)}, u32[]{:S(2)}) %collective-permute-start.9) | collective-permute-done | bytes 294944 | tf_op jit(solution)/shard_map/ppermute | solution.py:448
  48.2 0.1 slice.20
  48.3 0.1 copy.9
  48.4 0.7 %fusion.2 = f32[2,4,2]{1,2,0:T(2,128)} fusion(f32[2,4,2]{1,2,0:T(2,128)S(1)} %copy.9, f32[2,2,64]{2,1,0:T(2,128)S(1)} %bitcast.20, s32[]{:T(128)S(6)} %select_n.11), kind=kLoop, calls=%fused_computation.5 | loop fusion | flops 112 | bytes 196 | tf_op jit(solution)/shard_map/div | solution.py:553
  49.1 0.0 copy-start.7
  49.1 11.7 %all-to-all-done.got_ref = bf16[16,4,9216]{2,1,0:T(4,128)(2,1)S(1)} async-done(((bf16[16,4,9216]{2,1,0:T(4,128)(2,1)}), bf16[16,4,9216]{2,1,0:T(4,128)(2,1)S(1)}, u32[]{:S(2)}, u32[]{:S(2)}) %all-to-all-start) | async-done | bytes 1179680 | tf_op jit(solution)/shard_map/all_to_all | solution.py:487
  60.7 2.1 %weight_sum.1 = f32[8,4,9216]{2,1,0:T(4,128)} custom-call(s32[16]{0:T(128)S(1)} %get-tuple-element.33.local_ref, f32[16,4,128]{2,1,0:T(4,128)S(1)} %get-tuple-element.34.gate_ref, bf16[16,4,9216]{2,1,0:T(4,128)(2,1)S(1)} %all-to-all-done.got_ref), custom_call_target="tpu_custom_call" | custom-call | tf_op jit(solution)/shard_map/weight_sum/pallas_call | solution.py:555
  62.8 0.0 copy-done.7
  (6 shorter events, 0.1 us)
Async XLA Ops:
  0.6 3.8 %copy-start = (bf16[8,4,9216]{2,1,0:T(4,128)(2,1)S(1)}, bf16[8,4,9216]{2,1,0:T(4,128)(2,1)}, u32[]{:S(2)}) copy-start(bf16[8,4,9216]{2,1,0:T(4,128)(2,1)} %own_ref.3) | copy-start | bytes 1769476
  0.6 3.8 %copy-start.1 = (s32[2,64,2]{1,2,0:T(2,128)S(1)}, s32[2,64,2]{1,2,0:T(2,128)}, u32[]{:S(2)}) copy-start(s32[2,64,2]{1,2,0:T(2,128)} %param.9) | copy-start | bytes 3076
  0.7 3.8 %collective-permute-start.1 = (bf16[8,4,9216]{2,1,0:T(4,128)(2,1)}, bf16[8,4,9216]{2,1,0:T(4,128)(2,1)S(1)}, u32[]{:S(2)}, u32[]{:S(2)}) collective-permute-start(bf16[8,4,9216]{2,1,0:T(4,128)(2,1)} %own_ref.3), channel_id=1, source_target_pairs={{0,2},{2,0},{4,6},{6,4},{8,10},{10,8},{12,14},{14,12},{16,18},{18,... | collective-permute-start | bytes 1769480 | tf_op jit(solution)/shard_map/ppermute | solution.py:425
  3.2 13.9 %collective-permute-start = (bf16[2,128,1024]{2,1,0:T(8,128)(2,1)}, bf16[2,128,1024]{2,1,0:T(8,128)(2,1)S(1)}, u32[]{:S(2)}, u32[]{:S(2)}) collective-permute-start(bf16[2,128,1024]{2,1,0:T(8,128)(2,1)} %bitcast.24), channel_id=1, source_target_pairs={{0,1},{1,0},{2,3},{3,2},{4,5},{5,4},{6,7},{7,6},{8,9},{9,8},{10,11... | collective-permute-start | bytes 1572872 | tf_op jit(solution)/shard_map/ppermute | solution.py:448
  4.5 17.0 %copy-start.3 = (bf16[1,256,1024]{2,1,0:T(8,128)(2,1)S(1)}, bf16[1,256,1024]{2,1,0:T(8,128)(2,1)}, u32[]{:S(2)}) copy-start(bf16[1,256,1024]{2,1,0:T(8,128)(2,1)} %x_ref.1) | copy-start | bytes 1572868
  4.5 17.0 %copy-start.4 = (bf16[1,256,1024]{2,1,0:T(8,128)(2,1)S(1)}, bf16[1,256,1024]{2,1,0:T(8,128)(2,1)}, u32[]{:S(2)}) copy-start(bf16[1,256,1024]{2,1,0:T(8,128)(2,1)} %dy_ref.3) | copy-start | bytes 1572868
  6.2 13.1 %collective-permute-start.2 = (bf16[2,4,9216]{2,1,0:T(4,128)(2,1)S(1)}, bf16[2,4,9216]{2,1,0:T(4,128)(2,1)S(1)}, u32[]{:S(2)}, u32[]{:S(2)}) collective-permute-start(bf16[2,4,9216]{2,1,0:T(4,128)(2,1)S(1)} %get-tuple-element.19), channel_id=1, source_target_pairs={{0,24},{2,26},{4,28},{6,30},{8,16},{10,18},{12,20},{14,22},{16,8},... | collective-permute-start | bytes 442376 | tf_op jit(solution)/shard_map/ppermute | solution.py:425
  7.6 11.8 %collective-permute-start.3 = (bf16[2,4,9216]{2,1,0:T(4,128)(2,1)S(1)}, bf16[2,4,9216]{2,1,0:T(4,128)(2,1)S(1)}, u32[]{:S(2)}, u32[]{:S(2)}) collective-permute-start(bf16[2,4,9216]{2,1,0:T(4,128)(2,1)S(1)} %get-tuple-element.20), channel_id=1, source_target_pairs={{0,4},{2,6},{4,0},{6,2},{8,12},{10,14},{12,8},{14,10},{16,20},{18,... | collective-permute-start | bytes 442376 | tf_op jit(solution)/shard_map/ppermute | solution.py:425
  9.6 0.7 %copy-start.5 = (bf16[2,4,9216]{2,1,0:T(4,128)(2,1)}, bf16[2,4,9216]{2,1,0:T(4,128)(2,1)S(1)}, u32[]{:S(2)}) copy-start(bf16[2,4,9216]{2,1,0:T(4,128)(2,1)S(1)} %get-tuple-element.27.rest_7_) | copy-start | bytes 442372
  10.2 22.8 %collective-permute-start.5 = (bf16[2,4,9216]{2,1,0:T(4,128)(2,1)}, bf16[2,4,9216]{2,1,0:T(4,128)(2,1)}, u32[]{:S(2)}, u32[]{:S(2)}) collective-permute-start(bf16[2,4,9216]{2,1,0:T(4,128)(2,1)} %get-tuple-element.23), channel_id=1, source_target_pairs={{0,12},{2,14},{4,8},{6,10},{8,4},{10,6},{12,0},{14,2},{16,28},{18,... | collective-permute-start | bytes 442376 | tf_op jit(solution)/shard_map/ppermute | solution.py:425
  13.4 19.6 %collective-permute-start.6 = (bf16[2,4,9216]{2,1,0:T(4,128)(2,1)}, bf16[2,4,9216]{2,1,0:T(4,128)(2,1)}, u32[]{:S(2)}, u32[]{:S(2)}) collective-permute-start(bf16[2,4,9216]{2,1,0:T(4,128)(2,1)} %get-tuple-element.24), channel_id=1, source_target_pairs={{0,16},{2,18},{4,20},{6,22},{8,24},{10,26},{12,28},{14,30},{16,0},... | collective-permute-start | bytes 442376 | tf_op jit(solution)/shard_map/ppermute | solution.py:425
  17.1 16.0 %collective-permute-start.7 = (bf16[2,4,9216]{2,1,0:T(4,128)(2,1)}, bf16[2,4,9216]{2,1,0:T(4,128)(2,1)}, u32[]{:S(2)}, u32[]{:S(2)}) collective-permute-start(bf16[2,4,9216]{2,1,0:T(4,128)(2,1)} %get-tuple-element.25), channel_id=1, source_target_pairs={{0,20},{2,22},{4,16},{6,18},{8,28},{10,30},{12,24},{14,26},{16,4},... | collective-permute-start | bytes 442376 | tf_op jit(solution)/shard_map/ppermute | solution.py:425
  19.3 14.5 %collective-permute-start.8 = (bf16[2,4,9216]{2,1,0:T(4,128)(2,1)}, bf16[2,4,9216]{2,1,0:T(4,128)(2,1)S(1)}, u32[]{:S(2)}, u32[]{:S(2)}) collective-permute-start(bf16[2,4,9216]{2,1,0:T(4,128)(2,1)} %get-tuple-element.26), channel_id=1, source_target_pairs={{0,28},{2,30},{4,24},{6,26},{8,20},{10,22},{12,16},{14,18},{16,12}... | collective-permute-start | bytes 442376 | tf_op jit(solution)/shard_map/ppermute | solution.py:425
  19.3 14.5 %collective-permute-start.4 = (bf16[2,4,9216]{2,1,0:T(4,128)(2,1)S(1)}, bf16[2,4,9216]{2,1,0:T(4,128)(2,1)S(1)}, u32[]{:S(2)}, u32[]{:S(2)}) collective-permute-start(bf16[2,4,9216]{2,1,0:T(4,128)(2,1)S(1)} %get-tuple-element.22), channel_id=1, source_target_pairs={{0,8},{2,10},{4,12},{6,14},{8,0},{10,2},{12,4},{14,6},{16,24},{18,... | collective-permute-start | bytes 442376 | tf_op jit(solution)/shard_map/ppermute | solution.py:425
  26.3 7.5 %copy-start.2 = (f32[2,64,2]{1,2,0:T(2,128)S(1)}, f32[2,64,2]{1,2,0:T(2,128)}, u32[]{:S(2)}) copy-start(f32[2,64,2]{1,2,0:T(2,128)} %param.8) | copy-start | bytes 3076
  26.3 7.5 %copy-start.6 = (bf16[2,4,9216]{2,1,0:T(4,128)(2,1)S(1)}, bf16[2,4,9216]{2,1,0:T(4,128)(2,1)}, u32[]{:S(2)}) copy-start(bf16[2,4,9216]{2,1,0:T(4,128)(2,1)} %copy-done.5) | copy-start | bytes 442372
  26.3 34.5 %all-to-all-start = ((bf16[16,4,9216]{2,1,0:T(4,128)(2,1)}), bf16[16,4,9216]{2,1,0:T(4,128)(2,1)S(1)}, u32[]{:S(2)}, u32[]{:S(2)}) async-start(bf16[16,4,9216]{2,1,0:T(4,128)(2,1)} %kernel_grads.1.wire_ref), calls=%async_computation | async-start | bytes 2359296 | tf_op jit(solution)/shard_map/all_to_all | solution.py:487
  41.2 6.9 %collective-permute-start.9 = (bf16[144,1024]{1,0:T(8,128)(2,1)S(1)}, bf16[144,1024]{1,0:T(8,128)(2,1)S(1)}, u32[]{:S(2)}, u32[]{:S(2)}) collective-permute-start(bf16[144,1024]{1,0:T(8,128)(2,1)S(1)} %bitcast.23), channel_id=1, source_target_pairs={{0,1},{1,0},{2,3},{3,2},{4,5},{5,4},{6,7},{7,6},{8,9},{9,8},{10,11... | collective-permute-start | bytes 884744 | tf_op jit(solution)/shard_map/ppermute | solution.py:448
  49.1 13.8 %copy-start.7 = (bf16[1,256,1024]{2,1,0:T(8,128)(2,1)}, bf16[1,256,1024]{2,1,0:T(8,128)(2,1)S(1)}, u32[]{:S(2)}) copy-start(bf16[1,256,1024]{2,1,0:T(8,128)(2,1)S(1)} %fusion) | copy-start | bytes 1572868

commit v7 on v6

--- a/solution.py
+++ b/solution.py
@@ -375,13 +375,14 @@
 def sum_kernel(local_ref, gate_ref, got_ref, out_hbm, total_ref, sem):
     tiles, groups, width = got_ref.shape
     chunk = width // SUM_CHUNKS
+    unroll = min(tiles, 8)
     copies = []
     for part in range(SUM_CHUNKS):
         span = slice(part * chunk, (part + 1) * chunk)
         total_ref[:, :, span] = jnp.zeros(total_ref.shape[:2] + (chunk,), jnp.float32)
 
-        def add(quad, carry):
-            for tile in (quad * 4 + i for i in range(4)):
+        def add(group, carry):
+            for tile in (group * unroll + i for i in range(unroll)):
                 local = local_ref[tile]
                 gate = gate_ref[tile]
                 for at in range(part * chunk, (part + 1) * chunk, 128):
@@ -389,7 +390,7 @@
                     total_ref[local, :, lanes] += gate * got_ref[tile, :, lanes].astype(jnp.float32)
             return carry
 
-        lax.fori_loop(0, tiles // 4, add, 0)
+        lax.fori_loop(0, tiles // unroll, add, 0)
         copies.append(
             pltpu.make_async_copy(total_ref.at[:, :, span], out_hbm.at[:, :, span], sem.at[part])
         )

time: 63.1 us -> 63.1 us (level)
  no operation moved by 1% of the time
where the time goes in v7:
time: 63.1 us; the launch traced here: 62.8 us
  Pallas kernels  23.9 us (38%)
  starting transfers between devices  18.8 us (30%)
  waiting for transfers between devices  17.7 us (28%)
  local copies, waits for them, and re-layouts  1 us (2%)
  between operations  0.8 us (1%)
  other arithmetic  0.68 us (1%)
    all_to_all x1, waiting for transfers between devices, per_device(): lax.all_to_all(wire, 'grid', split_axis=0, concat_axis=0, tiled=True)  11.7 us
    ppermute x8, starting transfers between devices, swap(): return lax.ppermute(blocks, 'grid', [(i, i ^ step) for i in range(tiles)])  9.93 us
    pallas_call x1, Pallas kernels, per_device(): pl.pallas_call(functools.partial(adjoint_kernel, owned), out_shape=(jax.S...  7.42 us
    all_to_all x1, starting transfers between devices, per_device(): lax.all_to_all(wire, 'grid', split_axis=0, concat_axis=0, tiled=True)  6.7 us
    ppermute x2, waiting for transfers between devices, exchange(): lax.ppermute(blocks[step - 1], 'batch', [(i, (i + step) % batch) for i in...  5.22 us
    pallas_call x1, Pallas kernels, per_device(): pl.pallas_call(functools.partial(grads_kernel, owned, per_tile), out_shap...  4.77 us
    pallas_call x2, Pallas kernels, per_device(): pl.pallas_call(functools.partial(pack_kernel, owned, per_tile, some), out...  3.47 us
    pallas_call x1, Pallas kernels, per_device(): pl.pallas_call(functools.partial(tables_kernel, owned, per_tile), out_sha...  2.67 us
  transfers between devices with their start and end apart: 11, of which 4 were waited for; matrix products, arithmetic and copies ran while one was open for 2% of the time, Pallas kernels for 35%

profile of v7, /device:TPU:13, one launch (start us, length us, event | category | flops | bytes accessed | tf_op | source)
XLA Modules:
  0.0 62.8 jit_solution(8039599514139493836)
XLA Ops:
  0.6 0.0 copy-start
  0.6 0.0 copy-start.1
  0.7 0.7 %collective-permute-start.1 = (bf16[8,4,9216]{2,1,0:T(4,128)(2,1)}, bf16[8,4,9216]{2,1,0:T(4,128)(2,1)S(1)}, u32[]{:S(2)}, u32[]{:S(2)}) collective-permute-start(bf16[8,4,9216]{2,1,0:T(4,128)(2,1)} %own_ref.3), channel_id=1, source_target_pairs={{0,2},{2,0},{4,6},{6,4},{8,10},{10,8},{12,14},{14,12},{16,18},{18,... | collective-permute-start | bytes 1769480 | tf_op jit(solution)/shard_map/ppermute | solution.py:426
  1.4 1.8 %stage.1 = bf16[1,2,128,1024]{3,2,1,0:T(8,128)(2,1)} custom-call(bf16[1,256,1024]{2,1,0:T(8,128)(2,1)} %x_ref.1, bf16[1,256,1024]{2,1,0:T(8,128)(2,1)} %dy_ref.3), custom_call_target="tpu_custom_call" | custom-call | flops 20000000000 | bytes 1 | tf_op jit(solution)/shard_map/stage/pallas_call | solution.py:456
  3.2 1.3 %collective-permute-start = (bf16[2,128,1024]{2,1,0:T(8,128)(2,1)}, bf16[2,128,1024]{2,1,0:T(8,128)(2,1)S(1)}, u32[]{:S(2)}, u32[]{:S(2)}) collective-permute-start(bf16[2,128,1024]{2,1,0:T(8,128)(2,1)} %bitcast.24), channel_id=1, source_target_pairs={{0,1},{1,0},{2,3},{3,2},{4,5},{5,4},{6,7},{7,6},{8,9},{9,8},{10,11... | collective-permute-start | bytes 1572872 | tf_op jit(solution)/shard_map/ppermute | solution.py:449
  4.5 0.0 collective-permute-done.1.beside_ref
  4.5 0.0 copy-done
  4.5 0.0 copy-done.1
  4.5 0.0 copy-start.3
  4.5 0.0 copy-start.4
  4.5 1.7 %pack.2 = (bf16[2,4,9216]{2,1,0:T(4,128)(2,1)S(1)}, bf16[2,4,9216]{2,1,0:T(4,128)(2,1)S(1)}, bf16[2,4,9216]{2,1,0:T(4,128)(2,1)S(1)}) custom-call(s32[2,2,64]{2,1,0:T(2,128)S(1)} %bitcast.13, bf16[8,4,9216]{2,1,0:T(4,128)(2,1)S(1)} %copy-done, bf16[8,4,9216]{2,1,0:T(4,128)(2,1)S(1)} %collective-permute-done.1.beside_ref), custom_call_target="tpu_custom_call" | custom-call | tf_op jit(solution)/shard_map/pack/pallas_call | solution.py:433
  6.2 1.4 %collective-permute-start.2 = (bf16[2,4,9216]{2,1,0:T(4,128)(2,1)S(1)}, bf16[2,4,9216]{2,1,0:T(4,128)(2,1)S(1)}, u32[]{:S(2)}, u32[]{:S(2)}) collective-permute-start(bf16[2,4,9216]{2,1,0:T(4,128)(2,1)S(1)} %get-tuple-element.19), channel_id=1, source_target_pairs={{0,24},{2,26},{4,28},{6,30},{8,16},{10,18},{12,20},{14,22},{16,8},... | collective-permute-start | bytes 442376 | tf_op jit(solution)/shard_map/ppermute | solution.py:426
  7.6 0.2 collective-permute-start.3
  7.8 1.8 %pack.3 = (bf16[2,4,9216]{2,1,0:T(4,128)(2,1)}, bf16[2,4,9216]{2,1,0:T(4,128)(2,1)}, bf16[2,4,9216]{2,1,0:T(4,128)(2,1)}, bf16[2,4,9216]{2,1,0:T(4,128)(2,1)}, bf16[2,4,9216]{2,1,0:T(4,128)(2,1)S(1)}) custom-call(s32[2,2,64]{2,1,0:T(2,128)S(1)} %bitcast.14, bf16[8,4,9216]{2,1,0:T(4,128)(2,1)S(1)} %copy-done, ...), custom_call_target="tpu_custom_call" | custom-call | tf_op jit(solution)/shard_map/pack/pallas_call | solution.py:433
  9.6 0.0 copy-start.5
  9.6 0.7 %copy-done.5 = bf16[2,4,9216]{2,1,0:T(4,128)(2,1)} copy-done((bf16[2,4,9216]{2,1,0:T(4,128)(2,1)}, bf16[2,4,9216]{2,1,0:T(4,128)(2,1)S(1)}, u32[]{:S(2)}) %copy-start.5) | copy-done | bytes 147480
  10.2 3.2 %collective-permute-start.5 = (bf16[2,4,9216]{2,1,0:T(4,128)(2,1)}, bf16[2,4,9216]{2,1,0:T(4,128)(2,1)}, u32[]{:S(2)}, u32[]{:S(2)}) collective-permute-start(bf16[2,4,9216]{2,1,0:T(4,128)(2,1)} %get-tuple-element.23), channel_id=1, source_target_pairs={{0,12},{2,14},{4,8},{6,10},{8,4},{10,6},{12,0},{14,2},{16,28},{18,... | collective-permute-start | bytes 442376 | tf_op jit(solution)/shard_map/ppermute | solution.py:426
  13.4 0.0 collective-permute-start.6
  13.4 3.7 %collective-permute-done = bf16[2,128,1024]{2,1,0:T(8,128)(2,1)S(1)} collective-permute-done((bf16[2,128,1024]{2,1,0:T(8,128)(2,1)}, bf16[2,128,1024]{2,1,0:T(8,128)(2,1)S(1)}, u32[]{:S(2)}, u32[]{:S(2)}) %collective-permute-start) | collective-permute-done | bytes 524320 | tf_op jit(solution)/shard_map/ppermute | solution.py:449
  17.1 2.3 %collective-permute-start.7 = (bf16[2,4,9216]{2,1,0:T(4,128)(2,1)}, bf16[2,4,9216]{2,1,0:T(4,128)(2,1)}, u32[]{:S(2)}, u32[]{:S(2)}) collective-permute-start(bf16[2,4,9216]{2,1,0:T(4,128)(2,1)} %get-tuple-element.25), channel_id=1, source_target_pairs={{0,20},{2,22},{4,16},{6,18},{8,28},{10,30},{12,24},{14,26},{16,4},... | collective-permute-start | bytes 442376 | tf_op jit(solution)/shard_map/ppermute | solution.py:426
  19.3 0.0 collective-permute-done.2.rest_0_
  19.3 0.0 collective-permute-start.8
  19.3 0.0 collective-permute-done.3.rest_1_
  19.3 2.2 %collective-permute-start.4 = (bf16[2,4,9216]{2,1,0:T(4,128)(2,1)S(1)}, bf16[2,4,9216]{2,1,0:T(4,128)(2,1)S(1)}, u32[]{:S(2)}, u32[]{:S(2)}) collective-permute-start(bf16[2,4,9216]{2,1,0:T(4,128)(2,1)S(1)} %get-tuple-element.22), channel_id=1, source_target_pairs={{0,8},{2,10},{4,12},{6,14},{8,0},{10,2},{12,4},{14,6},{16,24},{18,... | collective-permute-start | bytes 442376 | tf_op jit(solution)/shard_map/ppermute | solution.py:426
  21.5 0.0 copy-done.3
  21.5 0.0 copy-done.4
  21.5 4.8 %kernel_grads.1.wire_ref = bf16[16,4,9216]{2,1,0:T(4,128)(2,1)} custom-call(s32[2,2,64]{2,1,0:T(2,128)S(1)} %bitcast.15, bf16[1,256,1024]{2,1,0:T(8,128)(2,1)S(1)} %copy-done.3, bf16[1,256,1024]{2,1,0:T(8,128)(2,1)S(1)} %copy-done.4, bf16[1,2,128,1024]{3,2,1,0:T(8,128)(2,1)S(1)} %bitcast.21), custom_call_target="tpu_custom_call" | custom-call | flops 20000000000 | bytes 1 | tf_op jit(solution)/shard_map/kernel_grads/pallas_call | solution.py:476
  26.3 6.7 %all-to-all-start = ((bf16[16,4,9216]{2,1,0:T(4,128)(2,1)}), bf16[16,4,9216]{2,1,0:T(4,128)(2,1)S(1)}, u32[]{:S(2)}, u32[]{:S(2)}) async-start(bf16[16,4,9216]{2,1,0:T(4,128)(2,1)} %kernel_grads.1.wire_ref), calls=%async_computation | async-start | bytes 2359296 | tf_op jit(solution)/shard_map/all_to_all | solution.py:488
  33.0 0.0 collective-permute-done.5.rest_3_
  33.0 0.0 collective-permute-done.6.rest_4_
  33.0 0.0 collective-permute-done.7.rest_5_
  33.0 0.8 %collective-permute-done.8.rest_6_ = bf16[2,4,9216]{2,1,0:T(4,128)(2,1)S(1)} collective-permute-done((bf16[2,4,9216]{2,1,0:T(4,128)(2,1)}, bf16[2,4,9216]{2,1,0:T(4,128)(2,1)S(1)}, u32[]{:S(2)}, u32[]{:S(2)}) %collective-permute-start.8) | collective-permute-done | bytes 147488 | tf_op jit(solution)/shard_map/ppermute | solution.py:426
  33.8 0.0 collective-permute-done.4.rest_2_
  33.8 0.0 copy-done.2
  33.8 0.0 copy-done.6
  33.8 7.4 %adjoint.1 = (bf16[1,144,1024]{2,1,0:T(8,128)(2,1)S(1)}, bf16[16,128]{1,0:T(8,128)(2,1)S(1)}, f32[2,3,256,128]{3,2,1,0:T(8,128)S(1)}) custom-call(s32[2,2,64]{2,1,0:T(2,128)S(1)} %bitcast.16, f32[2,2,64]{2,1,0:T(2,128)S(1)} %bitcast.18, bf16[16,4,9216]{2,1,0:T(4,128)(2,1)} %kernel_grads.1.wire_ref, bf16[1,2,128,1024]{3,2,1,0:T(8,128)(2,1)S(1)} %bitcast.22, ...), custom_call_target="tpu_custom_call" | custom-call | flops 20000000000 | bytes 1 | tf_op jit(solution)/shard_map/adjoint/pallas_call | solution.py:491
  41.2 0.8 %collective-permute-start.9 = (bf16[144,1024]{1,0:T(8,128)(2,1)S(1)}, bf16[144,1024]{1,0:T(8,128)(2,1)S(1)}, u32[]{:S(2)}, u32[]{:S(2)}) collective-permute-start(bf16[144,1024]{1,0:T(8,128)(2,1)S(1)} %bitcast.23), channel_id=1, source_target_pairs={{0,1},{1,0},{2,3},{3,2},{4,5},{5,4},{6,7},{7,6},{8,9},{9,8},{10,11... | collective-permute-start | bytes 884744 | tf_op jit(solution)/shard_map/ppermute | solution.py:449
  42.1 2.7 %tables.1 = (s32[16]{0:T(128)S(1)}, f32[16,4,128]{2,1,0:T(4,128)S(1)}) custom-call(s32[2,2,64]{2,1,0:T(2,128)S(1)} %bitcast.17, f32[2,2,64]{2,1,0:T(2,128)S(1)} %bitcast.19), custom_call_target="tpu_custom_call" | custom-call | tf_op jit(solution)/shard_map/tables/pallas_call | solution.py:528
  44.8 1.7 %own_adjoint.1 = bf16[128,1024]{1,0:T(8,128)(2,1)S(1)} custom-call(f32[2,3,256,128]{3,2,1,0:T(8,128)S(1)} %get-tuple-element.28.mixed_ref, bf16[1,256,1024]{2,1,0:T(8,128)(2,1)S(1)} %copy-done.4), custom_call_target="tpu_custom_call" | custom-call | flops 1000000000 | bytes 1 | tf_op jit(solution)/shard_map/own_adjoint/pallas_call | solution.py:516
  46.5 0.1 broadcast_in_dim.9
  46.6 1.6 %collective-permute-done.9 = bf16[144,1024]{1,0:T(8,128)(2,1)S(1)} collective-permute-done((bf16[144,1024]{1,0:T(8,128)(2,1)S(1)}, bf16[144,1024]{1,0:T(8,128)(2,1)S(1)}, u32[]{:S(2)}, u32[]{:S(2)}) %collective-permute-start.9) | collective-permute-done | bytes 294944 | tf_op jit(solution)/shard_map/ppermute | solution.py:449
  48.2 0.1 slice.20
  48.3 0.1 copy.9
  48.4 0.7 %fusion.2 = f32[2,4,2]{1,2,0:T(2,128)} fusion(f32[2,4,2]{1,2,0:T(2,128)S(1)} %copy.9, f32[2,2,64]{2,1,0:T(2,128)S(1)} %bitcast.20, s32[]{:T(128)S(6)} %select_n.11), kind=kLoop, calls=%fused_computation.5 | loop fusion | flops 112 | bytes 196 | tf_op jit(solution)/shard_map/div | solution.py:554
  49.1 0.0 copy-start.7
  49.1 11.7 %all-to-all-done.got_ref = bf16[16,4,9216]{2,1,0:T(4,128)(2,1)S(1)} async-done(((bf16[16,4,9216]{2,1,0:T(4,128)(2,1)}), bf16[16,4,9216]{2,1,0:T(4,128)(2,1)S(1)}, u32[]{:S(2)}, u32[]{:S(2)}) %all-to-all-start) | async-done | bytes 1179680 | tf_op jit(solution)/shard_map/all_to_all | solution.py:488
  60.7 2.1 %weight_sum.1 = f32[8,4,9216]{2,1,0:T(4,128)} custom-call(s32[16]{0:T(128)S(1)} %get-tuple-element.33.local_ref, f32[16,4,128]{2,1,0:T(4,128)S(1)} %get-tuple-element.34.gate_ref, bf16[16,4,9216]{2,1,0:T(4,128)(2,1)S(1)} %all-to-all-done.got_ref), custom_call_target="tpu_custom_call" | custom-call | tf_op jit(solution)/shard_map/weight_sum/pallas_call | solution.py:556
  62.8 0.0 copy-done.7
  (6 shorter events, 0.1 us)
Async XLA Ops:
  0.6 3.8 %copy-start = (bf16[8,4,9216]{2,1,0:T(4,128)(2,1)S(1)}, bf16[8,4,9216]{2,1,0:T(4,128)(2,1)}, u32[]{:S(2)}) copy-start(bf16[8,4,9216]{2,1,0:T(4,128)(2,1)} %own_ref.3) | copy-start | bytes 1769476
  0.6 3.8 %copy-start.1 = (s32[2,64,2]{1,2,0:T(2,128)S(1)}, s32[2,64,2]{1,2,0:T(2,128)}, u32[]{:S(2)}) copy-start(s32[2,64,2]{1,2,0:T(2,128)} %param.9) | copy-start | bytes 3076
  0.7 3.8 %collective-permute-start.1 = (bf16[8,4,9216]{2,1,0:T(4,128)(2,1)}, bf16[8,4,9216]{2,1,0:T(4,128)(2,1)S(1)}, u32[]{:S(2)}, u32[]{:S(2)}) collective-permute-start(bf16[8,4,9216]{2,1,0:T(4,128)(2,1)} %own_ref.3), channel_id=1, source_target_pairs={{0,2},{2,0},{4,6},{6,4},{8,10},{10,8},{12,14},{14,12},{16,18},{18,... | collective-permute-start | bytes 1769480 | tf_op jit(solution)/shard_map/ppermute | solution.py:426
  3.2 13.9 %collective-permute-start = (bf16[2,128,1024]{2,1,0:T(8,128)(2,1)}, bf16[2,128,1024]{2,1,0:T(8,128)(2,1)S(1)}, u32[]{:S(2)}, u32[]{:S(2)}) collective-permute-start(bf16[2,128,1024]{2,1,0:T(8,128)(2,1)} %bitcast.24), channel_id=1, source_target_pairs={{0,1},{1,0},{2,3},{3,2},{4,5},{5,4},{6,7},{7,6},{8,9},{9,8},{10,11... | collective-permute-start | bytes 1572872 | tf_op jit(solution)/shard_map/ppermute | solution.py:449
  4.5 17.0 %copy-start.3 = (bf16[1,256,1024]{2,1,0:T(8,128)(2,1)S(1)}, bf16[1,256,1024]{2,1,0:T(8,128)(2,1)}, u32[]{:S(2)}) copy-start(bf16[1,256,1024]{2,1,0:T(8,128)(2,1)} %x_ref.1) | copy-start | bytes 1572868
  4.5 17.0 %copy-start.4 = (bf16[1,256,1024]{2,1,0:T(8,128)(2,1)S(1)}, bf16[1,256,1024]{2,1,0:T(8,128)(2,1)}, u32[]{:S(2)}) copy-start(bf16[1,256,1024]{2,1,0:T(8,128)(2,1)} %dy_ref.3) | copy-start | bytes 1572868
  6.2 13.1 %collective-permute-start.2 = (bf16[2,4,9216]{2,1,0:T(4,128)(2,1)S(1)}, bf16[2,4,9216]{2,1,0:T(4,128)(2,1)S(1)}, u32[]{:S(2)}, u32[]{:S(2)}) collective-permute-start(bf16[2,4,9216]{2,1,0:T(4,128)(2,1)S(1)} %get-tuple-element.19), channel_id=1, source_target_pairs={{0,24},{2,26},{4,28},{6,30},{8,16},{10,18},{12,20},{14,22},{16,8},... | collective-permute-start | bytes 442376 | tf_op jit(solution)/shard_map/ppermute | solution.py:426
  7.6 11.8 %collective-permute-start.3 = (bf16[2,4,9216]{2,1,0:T(4,128)(2,1)S(1)}, bf16[2,4,9216]{2,1,0:T(4,128)(2,1)S(1)}, u32[]{:S(2)}, u32[]{:S(2)}) collective-permute-start(bf16[2,4,9216]{2,1,0:T(4,128)(2,1)S(1)} %get-tuple-element.20), channel_id=1, source_target_pairs={{0,4},{2,6},{4,0},{6,2},{8,12},{10,14},{12,8},{14,10},{16,20},{18,... | collective-permute-start | bytes 442376 | tf_op jit(solution)/shard_map/ppermute | solution.py:426
  9.6 0.7 %copy-start.5 = (bf16[2,4,9216]{2,1,0:T(4,128)(2,1)}, bf16[2,4,9216]{2,1,0:T(4,128)(2,1)S(1)}, u32[]{:S(2)}) copy-start(bf16[2,4,9216]{2,1,0:T(4,128)(2,1)S(1)} %get-tuple-element.27.rest_7_) | copy-start | bytes 442372
  10.2 22.8 %collective-permute-start.5 = (bf16[2,4,9216]{2,1,0:T(4,128)(2,1)}, bf16[2,4,9216]{2,1,0:T(4,128)(2,1)}, u32[]{:S(2)}, u32[]{:S(2)}) collective-permute-start(bf16[2,4,9216]{2,1,0:T(4,128)(2,1)} %get-tuple-element.23), channel_id=1, source_target_pairs={{0,12},{2,14},{4,8},{6,10},{8,4},{10,6},{12,0},{14,2},{16,28},{18,... | collective-permute-start | bytes 442376 | tf_op jit(solution)/shard_map/ppermute | solution.py:426
  13.4 19.6 %collective-permute-start.6 = (bf16[2,4,9216]{2,1,0:T(4,128)(2,1)}, bf16[2,4,9216]{2,1,0:T(4,128)(2,1)}, u32[]{:S(2)}, u32[]{:S(2)}) collective-permute-start(bf16[2,4,9216]{2,1,0:T(4,128)(2,1)} %get-tuple-element.24), channel_id=1, source_target_pairs={{0,16},{2,18},{4,20},{6,22},{8,24},{10,26},{12,28},{14,30},{16,0},... | collective-permute-start | bytes 442376 | tf_op jit(solution)/shard_map/ppermute | solution.py:426
  17.1 16.0 %collective-permute-start.7 = (bf16[2,4,9216]{2,1,0:T(4,128)(2,1)}, bf16[2,4,9216]{2,1,0:T(4,128)(2,1)}, u32[]{:S(2)}, u32[]{:S(2)}) collective-permute-start(bf16[2,4,9216]{2,1,0:T(4,128)(2,1)} %get-tuple-element.25), channel_id=1, source_target_pairs={{0,20},{2,22},{4,16},{6,18},{8,28},{10,30},{12,24},{14,26},{16,4},... | collective-permute-start | bytes 442376 | tf_op jit(solution)/shard_map/ppermute | solution.py:426
  19.3 14.5 %collective-permute-start.8 = (bf16[2,4,9216]{2,1,0:T(4,128)(2,1)}, bf16[2,4,9216]{2,1,0:T(4,128)(2,1)S(1)}, u32[]{:S(2)}, u32[]{:S(2)}) collective-permute-start(bf16[2,4,9216]{2,1,0:T(4,128)(2,1)} %get-tuple-element.26), channel_id=1, source_target_pairs={{0,28},{2,30},{4,24},{6,26},{8,20},{10,22},{12,16},{14,18},{16,12}... | collective-permute-start | bytes 442376 | tf_op jit(solution)/shard_map/ppermute | solution.py:426
  19.3 14.5 %collective-permute-start.4 = (bf16[2,4,9216]{2,1,0:T(4,128)(2,1)S(1)}, bf16[2,4,9216]{2,1,0:T(4,128)(2,1)S(1)}, u32[]{:S(2)}, u32[]{:S(2)}) collective-permute-start(bf16[2,4,9216]{2,1,0:T(4,128)(2,1)S(1)} %get-tuple-element.22), channel_id=1, source_target_pairs={{0,8},{2,10},{4,12},{6,14},{8,0},{10,2},{12,4},{14,6},{16,24},{18,... | collective-permute-start | bytes 442376 | tf_op jit(solution)/shard_map/ppermute | solution.py:426
  26.3 7.5 %copy-start.2 = (f32[2,64,2]{1,2,0:T(2,128)S(1)}, f32[2,64,2]{1,2,0:T(2,128)}, u32[]{:S(2)}) copy-start(f32[2,64,2]{1,2,0:T(2,128)} %param.8) | copy-start | bytes 3076
  26.3 7.5 %copy-start.6 = (bf16[2,4,9216]{2,1,0:T(4,128)(2,1)S(1)}, bf16[2,4,9216]{2,1,0:T(4,128)(2,1)}, u32[]{:S(2)}) copy-start(bf16[2,4,9216]{2,1,0:T(4,128)(2,1)} %copy-done.5) | copy-start | bytes 442372
  26.3 34.5 %all-to-all-start = ((bf16[16,4,9216]{2,1,0:T(4,128)(2,1)}), bf16[16,4,9216]{2,1,0:T(4,128)(2,1)S(1)}, u32[]{:S(2)}, u32[]{:S(2)}) async-start(bf16[16,4,9216]{2,1,0:T(4,128)(2,1)} %kernel_grads.1.wire_ref), calls=%async_computation | async-start | bytes 2359296 | tf_op jit(solution)/shard_map/all_to_all | solution.py:488
  41.2 6.9 %collective-permute-start.9 = (bf16[144,1024]{1,0:T(8,128)(2,1)S(1)}, bf16[144,1024]{1,0:T(8,128)(2,1)S(1)}, u32[]{:S(2)}, u32[]{:S(2)}) collective-permute-start(bf16[144,1024]{1,0:T(8,128)(2,1)S(1)} %bitcast.23), channel_id=1, source_target_pairs={{0,1},{1,0},{2,3},{3,2},{4,5},{5,4},{6,7},{7,6},{8,9},{9,8},{10,11... | collective-permute-start | bytes 884744 | tf_op jit(solution)/shard_map/ppermute | solution.py:449
  49.1 13.7 %copy-start.7 = (bf16[1,256,1024]{2,1,0:T(8,128)(2,1)}, bf16[1,256,1024]{2,1,0:T(8,128)(2,1)S(1)}, u32[]{:S(2)}) copy-start(bf16[1,256,1024]{2,1,0:T(8,128)(2,1)S(1)} %fusion) | copy-start | bytes 1572868
